TPU v7x, 32 devices: a whole 2x2x4 slice. The times are simulated.
32 devices in a mesh: pole: 4 (over x, core), row: 2 (over y), col: 4 (over z).
Axes of the slice: x: 2, y: 2, z: 4, core: 2. Of those that a mesh axis runs over, the one named last changes fastest.
Arguments:
- inverse: bfloat16 [12, 2, 6144, 6144], P('pole', None, 'col', 'row'), may hold values from -0.078125 to 0.078125
- lower: bfloat16 [12, 2, 6144, 512], P('pole', None, 'row', 'col'), may hold values from -6 to 6
- mask_tiles: int32 [16, 16], replicated, may hold values from 0 to 1, as said below
- pole_weight: float32 [12, 2], P('pole'), may hold values from -4 to 4
Outputs:
- panel: bfloat16 [12, 2, 6144, 512], P('pole', None, 'col', 'row')
- density: float32 [6144, 512], P(('col', 'pole'), 'row')
Inputs may be any that keep to these rules, and one draw needn't show every extreme that they name: `mask_tiles`: each tile row is either all ones or holds exactly one 1; of tile rows t and t + 8 exactly one is all ones.
All inputs are finite; a program needn't handle non-finite values.
Results may differ from a plain program's by a relative error of at most 0.017.
Values may be sent and summed in bfloat16 or wider, within the bound.
No kernel may reach another device: no remote copies, remote signals or barrier semaphores. Data moves between devices by JAX's collectives and lax.ppermute only.
A program may use at most 256 MiB of HBM per device.

v0:
```python
import functools

import jax
import jax.numpy as jnp
import numpy as np
from jax import lax
from jax.experimental import pallas as pl
from jax.experimental.pallas import tpu as pltpu
from jax.sharding import PartitionSpec as P

ANY = pl.BlockSpec(memory_space=pl.ANY)
SMEM = pl.BlockSpec(memory_space=pltpu.SMEM)
LANES = 128
FULL, SINGLE = 2, 1


def complex_product(block, factors):
    real_part = jnp.einsum(
        "prc,pcw->prw", block[:, 0], factors[:, 0], preferred_element_type=jnp.float32
    ) - jnp.einsum("prc,pcw->prw", block[:, 1], factors[:, 1], preferred_element_type=jnp.float32)
    imag_part = jnp.einsum(
        "prc,pcw->prw", block[:, 0], factors[:, 1], preferred_element_type=jnp.float32
    ) + jnp.einsum("prc,pcw->prw", block[:, 1], factors[:, 0], preferred_element_type=jnp.float32)
    return jnp.stack([real_part, imag_part], axis=1)


def general_body(tile, inverse, lower, mask_tiles, pole_weight):
    full_lower = lax.all_gather(lower, "col", axis=3, tiled=True)
    row_tiles = inverse.shape[2] // tile
    col_tiles = inverse.shape[3] // tile
    start = (lax.axis_index("col") * row_tiles, lax.axis_index("row") * col_tiles)
    own = lax.dynamic_slice(mask_tiles, start, (row_tiles, col_tiles))
    keep = jnp.repeat(jnp.repeat(own, tile, axis=0), tile, axis=1).astype(inverse.dtype)
    partial_value = complex_product(inverse * keep[None, None], full_lower)
    summed = lax.psum_scatter(
        partial_value.astype(jnp.bfloat16), "row", scatter_dimension=3, tiled=True
    ).astype(jnp.float32)
    panel = (-summed).astype(jnp.bfloat16)
    values = panel.astype(jnp.float32)
    weighted = jnp.sum(
        pole_weight[:, 0, None, None] * values[:, 1] + pole_weight[:, 1, None, None] * values[:, 0],
        axis=0,
    )
    density = lax.psum_scatter(
        weighted.astype(jnp.bfloat16), "pole", scatter_dimension=0, tiled=True
    ).astype(jnp.float32)
    return (panel, density)


def slice_kernel(cfg, *refs):
    pole, tile, row_tiles, n_pole = (cfg[k] for k in ("pole", "tile", "row_tiles", "n_pole"))
    parts = cfg["parts"]
    n_parts = len(parts)
    keep, last = cfg["kind"] == "keep", cfg["last"]
    refs = list(refs)

    def take(count):
        taken = refs[:count]
        del refs[:count]
        return taken

    meta, weight, inv = take(3)
    cands = dict(zip(cfg["arrays"], take(len(cfg["arrays"]))))
    if keep:
        recv = take(n_parts)
        take(1 if cfg["aliased"] else 0)
    outs = take(1 if keep else n_parts)
    dens = take(n_pole if last else 0)
    abuf, wbuf, prod, obuf, asem, wsem, osem = take(7)
    width = wbuf.shape[1] // (2 * n_parts)
    depth = wbuf.shape[0]
    n_buf = abuf.shape[0]

    def start(copy):
        copy.start()

    def wait(copy):
        copy.wait()

    def tile_rows(r):
        return pl.ds(pl.multiple_of(r * tile, tile), tile)

    def fetch(r, act):
        slot = lax.rem(r, n_buf)

        @pl.when(meta[r] == FULL)
        def _():
            for c in range(2):
                act(pltpu.make_async_copy(inv.at[pole, c, tile_rows(r), :], abuf.at[slot, c], asem.at[slot, c]))

        @pl.when(meta[r] == SINGLE)
        def _():
            cols = tile_rows(meta[row_tiles + r])
            for c in range(2):
                act(
                    pltpu.make_async_copy(
                        inv.at[pole, c, tile_rows(r), cols], abuf.at[slot, c, :, pl.ds(0, tile)], asem.at[slot, c]
                    )
                )

    def lower_copies(j, ref):
        return [
            pltpu.make_async_copy(ref.at[h], wbuf.at[:, pl.ds((2 * j + h) * width, width)], wsem.at[j, h])
            for h in range(2)
        ]

    def source(name):
        return cands[name].at[pole] if name == "own" else cands[name]

    for j, (names, base) in enumerate(parts):
        for i, name in enumerate(names):

            @pl.when(meta[base] == i)
            def _(j=j, name=name):
                for copy in lower_copies(j, source(name)):
                    copy.start()

    fetch(0, start)
    columns = [pl.ds(pl.multiple_of(meta[base + 1] * width, width), width) for _, base in parts]
    extras = []
    if keep:
        rbuf, rsem = take(2)
        extras += [pltpu.make_async_copy(recv[j], rbuf.at[j], rsem.at[j]) for j in range(n_parts)]
    if last:
        pbuf, d32, d16, psem, dsem = take(5)
        extras += [
            pltpu.make_async_copy(outs[0].at[q, :, :, columns[0]], pbuf.at[q], psem.at[q]) for q in range(pole)
        ]
    for copy in extras:
        copy.start()
    for r in range(1, min(n_buf, row_tiles)):
        fetch(r, start)
    for j, (names, _) in enumerate(parts):
        for copy in lower_copies(j, source(names[0])):
            copy.wait()

    def out_copy(r, j):
        rows = tile_rows(r)
        target = outs[0].at[pole, :, rows, columns[j]] if keep else outs[j].at[:, rows, :]
        return pltpu.make_async_copy(obuf.at[j, :, rows, :], target, osem.at[r, j])

    def step(r, carry):
        slot = lax.rem(r, n_buf)
        rows = tile_rows(r)
        fetch(r, wait)

        @pl.when(meta[r] == FULL)
        def _():
            both = abuf[slot].reshape(2 * tile, depth)
            prod[...] = jnp.dot(both, wbuf[...], preferred_element_type=jnp.float32)

        @pl.when(meta[r] == SINGLE)
        def _():
            both = abuf[slot, :, :, :tile].reshape(2 * tile, tile)
            prod[...] = jnp.dot(both, wbuf[tile_rows(meta[row_tiles + r]), :], preferred_element_type=jnp.float32)

        @pl.when(meta[r] == 0)
        def _():
            prod[...] = jnp.zeros_like(prod)

        if extras:

            @pl.when(r == 0)
            def _():
                for copy in extras:
                    copy.wait()

        if row_tiles > n_buf:

            @pl.when(r + n_buf < row_tiles)
            def _():
                fetch(r + n_buf, start)

        for j in range(n_parts):
            low, high = (pl.ds((2 * j + h) * width, width) for h in range(2))
            re = prod[:tile, low] - prod[tile:, high]
            im = prod[:tile, high] + prod[tile:, low]
            if keep:
                re = -(re + rbuf[j, 0, rows, :].astype(jnp.float32))
                im = -(im + rbuf[j, 1, rows, :].astype(jnp.float32))
            re = re.astype(jnp.bfloat16)
            im = im.astype(jnp.bfloat16)
            obuf[j, 0, rows, :] = re
            obuf[j, 1, rows, :] = im
            out_copy(r, j).start()
        if last:
            total = weight[pole, 0] * im.astype(jnp.float32) + weight[pole, 1] * re.astype(jnp.float32)
            for q in range(pole):
                total = total + (
                    weight[q, 0] * pbuf[q, 1, rows, :].astype(jnp.float32)
                    + weight[q, 1] * pbuf[q, 0, rows, :].astype(jnp.float32)
                )
            d32[rows, :] = total
            d16[rows, :] = total.astype(jnp.bfloat16)
        return carry

    lax.fori_loop(0, row_tiles, step, 0)

    if last:
        share = d32.shape[0] // n_pole
        mine = meta[2 * row_tiles]
        copies = []
        for d in range(n_pole):
            block = lax.rem(mine + d, n_pole)
            rows = pl.ds(pl.multiple_of(block * share, share), share)
            copies.append(pltpu.make_async_copy((d16 if d else d32).at[rows, :], dens[d], dsem.at[d]))
        for copy in copies:
            copy.start()
        for copy in copies:
            copy.wait()

    def drain(r, carry):
        for j in range(n_parts):
            out_copy(r, j).wait()
        return carry

    lax.fori_loop(0, row_tiles, drain, 0)


def slice_product(cfg, meta, weight, inverse, arrays, width, recv=None, panel=None):
    poles, _, rows, depth = inverse.shape
    tile, row_tiles, n_pole, parts = cfg["tile"], cfg["row_tiles"], cfg["n_pole"], cfg["parts"]
    keep, last = cfg["kind"] == "keep", cfg["last"]
    n_buf = min(row_tiles, 4)
    n_parts = len(parts)
    names = sorted({name for part, _ in parts for name in part})
    part_shape = (2, rows, width)
    operands = [meta, weight, inverse, *(arrays[name] for name in names)]
    specs = [SMEM, SMEM] + [ANY] * (1 + len(names))
    aliases = {}
    outs = []
    if keep:
        operands += recv
        specs += [ANY] * n_parts
        outs.append(jax.ShapeDtypeStruct((poles, 2, rows, cfg["panel_width"]), jnp.bfloat16))
        if panel is not None:
            aliases = {len(operands): 0}
            operands.append(panel)
            specs.append(ANY)
    else:
        outs += [jax.ShapeDtypeStruct(part_shape, jnp.bfloat16)] * n_parts
    if last:
        share = rows // n_pole
        for d in range(n_pole):
            outs.append(jax.ShapeDtypeStruct((share, width), jnp.bfloat16 if d else jnp.float32))
    scratch = [
        pltpu.VMEM((n_buf, 2, tile, depth), jnp.bfloat16),
        pltpu.VMEM((depth, 2 * width * n_parts), jnp.bfloat16),
        pltpu.VMEM((2 * tile, 2 * width * n_parts), jnp.float32),
        pltpu.VMEM((n_parts, *part_shape), jnp.bfloat16),
        pltpu.SemaphoreType.DMA((n_buf, 2)),
        pltpu.SemaphoreType.DMA((n_parts, 2)),
        pltpu.SemaphoreType.DMA((row_tiles, n_parts)),
    ]
    if keep:
        scratch += [pltpu.VMEM((n_parts, *part_shape), jnp.bfloat16), pltpu.SemaphoreType.DMA((n_parts,))]
    if last:
        scratch += [
            pltpu.VMEM((max(poles - 1, 1), *part_shape), jnp.bfloat16),
            pltpu.VMEM((rows, width), jnp.float32),
            pltpu.VMEM((rows, width), jnp.bfloat16),
            pltpu.SemaphoreType.DMA((max(poles - 1, 1),)),
            pltpu.SemaphoreType.DMA((n_pole,)),
        ]
    cfg = dict(cfg, aliased=panel is not None, arrays=names)
    return pl.pallas_call(
        functools.partial(slice_kernel, cfg),
        out_shape=outs,
        in_specs=specs,
        out_specs=[ANY] * len(outs),
        scratch_shapes=scratch,
        input_output_aliases=aliases,
        compiler_params=pltpu.CompilerParams(vmem_limit_bytes=48 * 2**20),
        cost_estimate=pl.CostEstimate(flops=30 * rows * depth * n_parts, bytes_accessed=rows * width, transcendentals=0),
        name=cfg["name"],
    )(*operands)


def half_order(n_col, half, z):
    group = n_col // 2
    return sorted(range(half * group, (half + 1) * group), key=lambda s: abs(s - z))


def plan_transfers(n_col, poles):
    end, half = poles - 1, n_col // 2
    where = {(z, y, p, z): ("own", p) for z in range(n_col) for y in range(2) for p in range(poles)}
    lists = {"out": [], "across": [], "in": []}
    at = {}

    def add(kind, name, moves):
        moves = [m for m in moves if m[3] < n_col and m[4] < n_col]
        if not moves:
            return
        both = moves + [
            (n_col - 1 - z, n_col - 1 - to, p, n_col - 1 - s1, n_col - 1 - s0) for z, to, p, s0, s1 in moves
        ]
        for z, to, p, s0, s1 in both:
            where[(to, 0, p, s0)] = where[(to, 1, p, s1)] = name
        at[name] = len(lists[kind])
        lists[kind].append((name, both))

    def hop(z, p, step):
        return (z, z - 1, p, z + step - 1, z + step - 1)

    steps = range(1, n_col)
    pairs = [(p, step) for p in range(end) for step in steps]
    for p, step in sorted(pairs, key=lambda item: (item[0] * (n_col - 1) + item[1] - 3 * (item[1] == 1), item)):
        add("out", f"o{p}s{step}", [hop(z, p, step) for z in range(1, half)])
    natural = list(steps)
    turned = sorted(natural, key=lambda s: (s < half, s))
    for i, (a, b) in enumerate(zip(natural, turned)):
        far = [hop(z, end, i + 1) for z in range(2, half)]
        add("out", f"o{end}s{i + 1}", [(1, 0, end, b, a)] + [m for m in far if m[3] < n_col])
    for p in range(poles):
        for step in steps:
            add("across", f"a{p}s{step}", [hop(half, p, step)])
    for p in range(poles):
        for step in steps:
            add("in", f"i{p}s{step}", [hop(z, p, step) for z in range(half + 1, n_col)])
    return lists, where, at


def make_fast_body(n_col, n_pole, tile):
    group = n_col // 2
    places = [(zz, yy) for zz in range(n_col) for yy in range(2)]

    def body(inverse, lower, mask_tiles, pole_weight):
        poles, _, rows, depth = inverse.shape
        width = lower.shape[3]
        row_tiles, col_tiles = rows // tile, depth // tile
        end = poles - 1
        z, y, mine = lax.axis_index("col"), lax.axis_index("row"), lax.axis_index("pole")
        lists, where, ready = plan_transfers(n_col, poles)
        final = len(lists["out"]) - 1

        head_size = 2 * row_tiles + 1
        tables = []
        calls = []
        for p in range(poles):
            whole, single = [list(range(group))], [[i] for i in range(group)]
            for kind in ("send", "keep"):
                for bunch in single if p >= end - 1 else whole:
                    parts = []
                    for i in bunch:
                        names, picks, columns = [], np.zeros((n_col, 2), np.int32), np.zeros((n_col, 2), np.int32)
                        for zz, yy in places:
                            half = yy if kind == "keep" else 1 - yy
                            s = half_order(n_col, half, zz)[i]
                            name = where[(zz, yy, p, s)]
                            name = "own" if isinstance(name, tuple) else name
                            if name not in names:
                                names.append(name)
                            picks[zz, yy] = names.index(name)
                            columns[zz, yy] = s - half * group
                        parts.append((names, head_size + len(tables)))
                        tables += [picks, columns]
                    calls.append((p, kind, tuple(bunch), parts))
        chosen = lax.dynamic_slice(jnp.asarray(np.stack(tables)), (0, z, y), (len(tables), 1, 1)).reshape(-1)

        own = lax.dynamic_slice(mask_tiles, (z * row_tiles, y * col_tiles), (row_tiles, col_tiles))
        count = jnp.sum(own, axis=1)
        modes = jnp.where(count == col_tiles, FULL, jnp.where(count == 0, 0, SINGLE))
        single = jnp.argmax(own, axis=1)
        meta = jnp.concatenate([modes, single, jnp.reshape(mine, (1,)), chosen]).astype(jnp.int32)

        arrays = {"own": lower}
        rest = lower
        for p in range(poles):
            arrays[("own", p)] = rest[p]
            rest, arrays[("own", p)] = lax.optimization_barrier((rest, arrays[("own", p)]))

        queue = [[] for _ in range(final + 1)]
        sent_at = {}
        for call in calls:
            p, kind, bunch, parts = call
            t = max([ready.get(name, 0) for names, _ in parts for name in names])
            if kind == "send":
                sent_at.update({(p, i): t for i in bunch})
            else:
                t = min(max([t] + [sent_at[(p, i)] + 1 for i in bunch]), final)
            queue[t].append(call)

        late = {"meta": meta}
        state = {"panel": None, "part": {}, "sent": {}, "dens": {}}

        def run(call):
            p, kind, bunch, parts = call
            cfg = dict(
                name=f"{kind}_{p}_{bunch[0]}",
                kind=kind,
                last=kind == "keep" and p == end,
                parts=parts,
                pole=p,
                tile=tile,
                row_tiles=row_tiles,
                n_pole=n_pole,
                panel_width=group * width,
            )
            if kind == "send":
                made = slice_product(cfg, late["meta"], pole_weight, inverse, arrays, width)
                for i, part in zip(bunch, made):
                    state["part"][(p, i)] = part
                    state["sent"][(p, i)] = lax.ppermute(part, "row", [(0, 1), (1, 0)])
                return
            recv = [state["sent"][(p, i)] for i in bunch]
            panel, *shares = slice_product(
                cfg, late["meta"], pole_weight, inverse, arrays, width, recv, state["panel"]
            )
            state["panel"] = panel
            if shares:
                total = shares[0]
                for d in range(1, n_pole):
                    ways = [(q, (q + d) % n_pole) for q in range(n_pole)]
                    total = total + lax.ppermute(shares[d], "pole", ways).astype(jnp.float32)
                state["dens"][bunch[0]] = (total, meta[parts[0][1] + 1])

        def launch(kind, t, deps):
            if t >= len(lists[kind]):
                return
            name, moves = lists[kind][t]
            held = {}
            for zz, _, p, s0, s1 in moves:
                for yy, s in ((0, s0), (1, s1)):
                    held.setdefault(where[(zz, yy, p, s)], []).append((zz, yy))
            held = sorted(held.items(), key=lambda item: -len(item[1]))
            values = [arrays[source] for source, _ in held]
            values, state["panel"], _ = lax.optimization_barrier((values, state["panel"], deps))
            value = values[0]
            for other, (_, spots) in zip(values[1:], held[1:]):
                here = functools.reduce(jnp.logical_or, [(z == a) & (y == b) for a, b in spots])
                value = jnp.where(here, other, value)
            arrays[name] = lax.ppermute(value, "col", [(zz, to) for zz, to, *_ in moves])

        def landed(kind, t):
            return [arrays[lists[kind][t][0]]] if 0 <= t < len(lists[kind]) else []

        launch("out", 0, [])
        launch("across", 0, [])
        launch("in", 0, [])
        launch("out", 1, [])
        launch("across", 1, [])
        for t in range(final + 1):
            deps = landed("out", t)
            deps += [state["part"][key] for key, at in sent_at.items() if at == t - 1]
            deps += [state["sent"][key] for key, at in sent_at.items() if at == t - 2]
            launch("out", t + 2, deps)
            launch("across", t + 2, landed("out", t) + landed("across", t))
            launch("in", t + 1, landed("out", t - 1) + landed("in", t))
            for kind in ("send", "keep"):
                for call in queue[t]:
                    if call[1] == kind:
                        run(call)
                if t >= final - 2:
                    made = [state["part"][key] for key, at in sent_at.items() if at == t]
                    late["meta"], state["panel"], _ = lax.optimization_barrier((late["meta"], state["panel"], made))

        dens = state["dens"]
        columns = []
        for c in range(group):
            value = dens[0][0]
            for i in range(1, group):
                value = jnp.where(dens[i][1] == c, dens[i][0], value)
            columns.append(value)
        return (state["panel"], jnp.concatenate(columns, axis=1))

    return body


def solution(mesh):
    n_pole, n_row, n_col = (mesh.shape[name] for name in ("pole", "row", "col"))

    def whole(inverse, lower, mask_tiles, pole_weight):
        tile = inverse.shape[2] // mask_tiles.shape[0]
        width = lower.shape[3] // n_col
        rows = inverse.shape[2] // n_col
        fits = n_row == 2 and n_col % 2 == 0 and n_col > 2 and width % LANES == 0
        fits = fits and tile % LANES == 0 and rows % (16 * n_pole) == 0 and inverse.shape[0] > n_pole
        if fits:
            body = make_fast_body(n_col, n_pole, tile)
        else:
            body = functools.partial(general_body, tile)
        return jax.shard_map(
            body,
            mesh=mesh,
            in_specs=(
                P("pole", None, "col", "row"),
                P("pole", None, "row", "col"),
                P(),
                P("pole", None),
            ),
            out_specs=(P("pole", None, "col", "row"), P(("col", "pole"), "row")),
            check_vma=False,
        )(inverse, lower, mask_tiles, pole_weight)

    return whole
```

profile of v0, /device:TPU:1, one launch (start us, length us, event | category | flops | bytes accessed | tf_op | source)
XLA Modules:
  0.0 329.7 jit_solution(6333471631484582850)
XLA Ops:
  2.2 4.1 %collective-permute-start.1 = (bf16[2,3072,128]{2,1,0:T(8,128)(2,1)S(1)}, bf16[2,3072,128]{2,1,0:T(8,128)(2,1)S(1)}, u32[]{:S(2)}, u32[]{:S(2)}) collective-permute-start(bf16[2,3072,128]{2,1,0:T(8,128)(2,1)S(1)} %slice_bitcast_fusion.2), channel_id=1, source_target_pairs={{3,2},{0,1},{7,6},{4,5},{11,10},{8,9},{15,14},{12,13},{19,18},{16,... | collective-permute-start | bytes 4718600 | tf_op jit(solution)/shard_map/ppermute | solution.py:432
  11.2 28.0 %collective-permute-done.1.refs_5_ = bf16[2,3072,128]{2,1,0:T(8,128)(2,1)S(1)} collective-permute-done((bf16[2,3072,128]{2,1,0:T(8,128)(2,1)S(1)}, bf16[2,3072,128]{2,1,0:T(8,128)(2,1)S(1)}, u32[]{:S(2)}, u32[]{:S(2)}) %collective-permute-start.1) | collective-permute-done | bytes 1572896 | tf_op jit(solution)/shard_map/ppermute | solution.py:432
  39.2 5.3 %collective-permute-start.2 = (bf16[2,3072,128]{2,1,0:T(8,128)(2,1)S(1)}, bf16[2,3072,128]{2,1,0:T(8,128)(2,1)}, u32[]{:S(2)}, u32[]{:S(2)}) collective-permute-start(bf16[2,3072,128]{2,1,0:T(8,128)(2,1)S(1)} %slice_bitcast_fusion.1), channel_id=1, source_target_pairs={{3,2},{0,1},{7,6},{4,5},{11,10},{8,9},{15,14},{12,13},{19,18},{16,... | collective-permute-start | bytes 4718600 | tf_op jit(solution)/shard_map/ppermute | solution.py:432
  52.2 24.7 %collective-permute-done.5.refs_5_ = bf16[2,3072,128]{2,1,0:T(8,128)(2,1)S(1)} collective-permute-done((bf16[2,3072,128]{2,1,0:T(8,128)(2,1)S(1)}, bf16[2,3072,128]{2,1,0:T(8,128)(2,1)S(1)}, u32[]{:S(2)}, u32[]{:S(2)}) %collective-permute-start.5) | collective-permute-done | bytes 1572896 | tf_op jit(solution)/shard_map/ppermute | solution.py:432
  81.2 7.0 %collective-permute-start.3 = (bf16[2,3072,128]{2,1,0:T(8,128)(2,1)}, bf16[2,3072,128]{2,1,0:T(8,128)(2,1)S(1)}, u32[]{:S(2)}, u32[]{:S(2)}) collective-permute-start(bf16[2,3072,128]{2,1,0:T(8,128)(2,1)} %slice_bitcast_fusion), channel_id=1, source_target_pairs={{3,2},{0,1},{7,6},{4,5},{11,10},{8,9},{15,14},{12,13},{19,18},{16,... | collective-permute-start | bytes 4718600 | tf_op jit(solution)/shard_map/ppermute | solution.py:432
  88.2 22.3 %collective-permute-done.11.refs_7_ = bf16[2,3072,128]{2,1,0:T(8,128)(2,1)S(1)} collective-permute-done((bf16[2,3072,128]{2,1,0:T(8,128)(2,1)S(1)}, bf16[2,3072,128]{2,1,0:T(8,128)(2,1)S(1)}, u32[]{:S(2)}, u32[]{:S(2)}) %collective-permute-start.11) | collective-permute-done | bytes 1572896 | tf_op jit(solution)/shard_map/ppermute | solution.py:432
  115.7 28.7 %collective-permute-done.6.refs_8_ = bf16[2,3072,128]{2,1,0:T(8,128)(2,1)} collective-permute-done((bf16[2,3072,128]{2,1,0:T(8,128)(2,1)}, bf16[2,3072,128]{2,1,0:T(8,128)(2,1)}, u32[]{:S(2)}, u32[]{:S(2)}) %collective-permute-start.6) | collective-permute-done | bytes 1572896 | tf_op jit(solution)/shard_map/ppermute | solution.py:432
  147.8 7.7 %send_0_0.1 = (bf16[2,1536,128]{2,1,0:T(8,128)(2,1)S(1)}, bf16[2,1536,128]{2,1,0:T(8,128)(2,1)S(1)}) custom-call(s32[33]{0:T(128)S(1)} %pad_add_fusion.refs_0_, f32[3,2]{1,0:T(4,128)S(1)} %copy.14.refs_1_, bf16[3,2,1536,3072]{3,2,1,0:T(8,128)(2,1)} %refs_2_.19, bf16[2,3072,128]{2,1,0:T(8,128)(2,1)S(1)} %copy-done.5, ...), custom_call_target="tpu_custom_call" | custom-call | flops 283115520 | bytes 196608 | tf_op jit(solution)/shard_map/send_0_0/pallas_call | solution.py:266
  157.4 20.6 %collective-permute-done.12.refs_4_ = bf16[2,3072,128]{2,1,0:T(8,128)(2,1)} collective-permute-done((bf16[2,3072,128]{2,1,0:T(8,128)(2,1)}, bf16[2,3072,128]{2,1,0:T(8,128)(2,1)}, u32[]{:S(2)}, u32[]{:S(2)}) %collective-permute-start.12) | collective-permute-done | bytes 1572896 | tf_op jit(solution)/shard_map/ppermute | solution.py:432
  180.8 5.4 %send_1_0.1 = bf16[2,1536,128]{2,1,0:T(8,128)(2,1)S(1)} custom-call(s32[33]{0:T(128)S(1)} %pad_add_fusion.refs_0_, f32[3,2]{1,0:T(4,128)S(1)} %copy.14.refs_1_, bf16[3,2,1536,3072]{3,2,1,0:T(8,128)(2,1)} %refs_2_.19, bf16[2,3072,128]{2,1,0:T(8,128)(2,1)} %collective-permute-done.10.refs_3_, bf16[2,3072,128]{2,1,0:T(8,128)(2,1)} %collective-permute-done.12.refs_4_, ...), custom_call_target="tpu_custom_call" | custom-call | flops 141557760 | bytes 196608 | tf_op jit(solution)/shard_map/send_1_0/pallas_call | solution.py:266
  188.8 7.9 %keep_0_0.1.refs_7_ = bf16[3,2,1536,256]{3,2,1,0:T(8,128)(2,1)} custom-call(s32[33]{0:T(128)S(1)} %pad_add_fusion.refs_0_, f32[3,2]{1,0:T(4,128)S(1)} %copy.14.refs_1_, bf16[3,2,1536,3072]{3,2,1,0:T(8,128)(2,1)} %refs_2_.19, bf16[2,3072,128]{2,1,0:T(8,128)(2,1)S(1)} %copy-done.6, bf16[2,3072,128]{2,1,0:T(8,128)(2,1)} %collective-permute-done.4.refs_4_, ...), custom_call_target="tpu_custom_call" | custom-call | flops 283115520 | bytes 196608 | tf_op jit(solution)/shard_map/keep_0_0/pallas_call | solution.py:266
  196.7 15.1 %collective-permute-done.17.refs_6_ = bf16[2,3072,128]{2,1,0:T(8,128)(2,1)} collective-permute-done((bf16[2,3072,128]{2,1,0:T(8,128)(2,1)}, bf16[2,3072,128]{2,1,0:T(8,128)(2,1)}, u32[]{:S(2)}, u32[]{:S(2)}) %collective-permute-start.17) | collective-permute-done | bytes 1572896 | tf_op jit(solution)/shard_map/ppermute | solution.py:432
  214.4 5.4 %send_1_1.1 = bf16[2,1536,128]{2,1,0:T(8,128)(2,1)S(1)} custom-call(s32[33]{0:T(128)S(1)} %pad_add_fusion.refs_0_, f32[3,2]{1,0:T(4,128)S(1)} %copy.14.refs_1_, bf16[3,2,1536,3072]{3,2,1,0:T(8,128)(2,1)} %refs_2_.19, bf16[2,3072,128]{2,1,0:T(8,128)(2,1)} %collective-permute-done.7.refs_3_, bf16[2,3072,128]{2,1,0:T(8,128)(2,1)} %collective-permute-done.2.refs_4_, ...), custom_call_target="tpu_custom_call" | custom-call | flops 141557760 | bytes 196608 | tf_op jit(solution)/shard_map/send_1_1/pallas_call | solution.py:266
  221.2 6.1 %keep_1_0.1.refs_8_ = bf16[3,2,1536,256]{3,2,1,0:T(8,128)(2,1)} custom-call(s32[33]{0:T(128)S(1)} %pad_add_fusion.refs_0_, f32[3,2]{1,0:T(4,128)S(1)} %copy.14.refs_1_, bf16[3,2,1536,3072]{3,2,1,0:T(8,128)(2,1)} %refs_2_.19, bf16[2,3072,128]{2,1,0:T(8,128)(2,1)} %collective-permute-done.10.refs_3_, ...), custom_call_target="tpu_custom_call", output_to_operand_aliasing={{}: (7, {})} | custom-call | flops 141557760 | bytes 196608 | tf_op jit(solution)/shard_map/keep_1_0/pallas_call | solution.py:266
  227.4 18.0 %collective-permute-done.18.refs_4_.refs_5_ = bf16[2,3072,128]{2,1,0:T(8,128)(2,1)S(1)} collective-permute-done((bf16[2,3072,128]{2,1,0:T(8,128)(2,1)}, bf16[2,3072,128]{2,1,0:T(8,128)(2,1)S(1)}, u32[]{:S(2)}, u32[]{:S(2)}) %collective-permute-start.18) | collective-permute-done | bytes 1572896 | tf_op jit(solution)/shard_map/ppermute | solution.py:432
  249.4 5.9 %send_2_0.1 = bf16[2,1536,128]{2,1,0:T(8,128)(2,1)} custom-call(s32[33]{0:T(128)S(1)} %pad_add_fusion.refs_0_, f32[3,2]{1,0:T(4,128)S(1)} %copy.14.refs_1_, bf16[3,2,1536,3072]{3,2,1,0:T(8,128)(2,1)} %refs_2_.19, bf16[2,3072,128]{2,1,0:T(8,128)(2,1)S(1)} %collective-permute-done.14.refs_3_, ...), custom_call_target="tpu_custom_call" | custom-call | flops 141557760 | bytes 196608 | tf_op jit(solution)/shard_map/send_2_0/pallas_call | solution.py:266
  257.0 6.0 %keep_1_1.1.refs_7_ = bf16[3,2,1536,256]{3,2,1,0:T(8,128)(2,1)} custom-call(s32[33]{0:T(128)S(1)} %pad_add_fusion.refs_0_, f32[3,2]{1,0:T(4,128)S(1)} %copy.14.refs_1_, bf16[3,2,1536,3072]{3,2,1,0:T(8,128)(2,1)} %refs_2_.19, bf16[2,3072,128]{2,1,0:T(8,128)(2,1)} %collective-permute-done.7.refs_3_, ...), custom_call_target="tpu_custom_call", output_to_operand_aliasing={{}: (8, {})} | custom-call | flops 141557760 | bytes 196608 | tf_op jit(solution)/shard_map/keep_1_1/pallas_call | solution.py:266
  262.9 16.1 %collective-permute-done.20.refs_6_.refs_4_ = bf16[2,3072,128]{2,1,0:T(8,128)(2,1)S(1)} collective-permute-done((bf16[2,3072,128]{2,1,0:T(8,128)(2,1)}, bf16[2,3072,128]{2,1,0:T(8,128)(2,1)S(1)}, u32[]{:S(2)}, u32[]{:S(2)}) %collective-permute-start.20) | collective-permute-done | bytes 1572896 | tf_op jit(solution)/shard_map/ppermute | solution.py:432
  280.3 5.3 %send_2_1.1 = bf16[2,1536,128]{2,1,0:T(8,128)(2,1)S(1)} custom-call(s32[33]{0:T(128)S(1)} %pad_add_fusion.refs_0_, f32[3,2]{1,0:T(4,128)S(1)} %copy.14.refs_1_, bf16[3,2,1536,3072]{3,2,1,0:T(8,128)(2,1)} %refs_2_.19, bf16[2,3072,128]{2,1,0:T(8,128)(2,1)S(1)} %collective-permute-done.8.refs_3_, bf16[2,3072,128]{2,1,0:T(8,128)(2,1)S(1)} %collective-permute-done.3.refs_4_, ...), custom_call_target="tpu_custom_call" | custom-call | flops 141557760 | bytes 196608 | tf_op jit(solution)/shard_map/send_2_1/pallas_call | solution.py:266
  288.4 7.4 %keep_2_0.1 = (bf16[3,2,1536,256]{3,2,1,0:T(8,128)(2,1)}, f32[384,128]{1,0:T(8,128)S(1)}, bf16[384,128]{1,0:T(8,128)(2,1)S(1)}, bf16[384,128]{1,0:T(8,128)(2,1)S(1)}, bf16[384,128]{1,0:T(8,128)(2,1)S(1)}) custom-call(s32[33]{0:T(128)S(1)} %pad_add_fusion.refs_0_, f32[3,2]{1,0:T(4,128)S(1)} %copy.14.refs_1_, ...), custom_call_target="tpu_custom_call", output_to_operand_aliasing={{0}: (7, {})} | custom-call | flops 141557760 | bytes 196608 | tf_op jit(solution)/shard_map/keep_2_0/pallas_call | solution.py:266
  295.8 4.8 %collective-permute-start.27 = (bf16[384,128]{1,0:T(8,128)(2,1)S(1)}, bf16[384,128]{1,0:T(8,128)(2,1)S(1)}, u32[]{:S(2)}, u32[]{:S(2)}) collective-permute-start(bf16[384,128]{1,0:T(8,128)(2,1)S(1)} %get-tuple-element.93), channel_id=1, source_target_pairs={{0,8},{8,16},{16,24},{24,0},{1,9},{9,17},{17,25},{25,1},{2,10},{10... | collective-permute-start | bytes 294920 | tf_op jit(solution)/shard_map/ppermute | solution.py:414
  301.1 11.8 %collective-permute-done.22.refs_5_ = bf16[2,3072,128]{2,1,0:T(8,128)(2,1)} collective-permute-done((bf16[2,3072,128]{2,1,0:T(8,128)(2,1)}, bf16[2,3072,128]{2,1,0:T(8,128)(2,1)}, u32[]{:S(2)}, u32[]{:S(2)}) %collective-permute-start.22) | collective-permute-done | bytes 1572896 | tf_op jit(solution)/shard_map/ppermute | solution.py:432
  312.9 7.5 %keep_2_1.1 = (bf16[3,2,1536,256]{3,2,1,0:T(8,128)(2,1)}, f32[384,128]{1,0:T(8,128)S(1)}, bf16[384,128]{1,0:T(8,128)(2,1)S(1)}, bf16[384,128]{1,0:T(8,128)(2,1)S(1)}, bf16[384,128]{1,0:T(8,128)(2,1)S(1)}) custom-call(s32[33]{0:T(128)S(1)} %pad_add_fusion.refs_0_, f32[3,2]{1,0:T(4,128)S(1)} %copy.14.refs_1_, ...), custom_call_target="tpu_custom_call", output_to_operand_aliasing={{0}: (7, {})} | custom-call | flops 141557760 | bytes 196608 | tf_op jit(solution)/shard_map/keep_2_1/pallas_call | solution.py:266
  320.4 3.0 collective-permute-start.24
  (88 shorter events, 53.1 us)
Async XLA Ops:
  2.2 37.1 %collective-permute-start.1 = (bf16[2,3072,128]{2,1,0:T(8,128)(2,1)S(1)}, bf16[2,3072,128]{2,1,0:T(8,128)(2,1)S(1)}, u32[]{:S(2)}, u32[]{:S(2)}) collective-permute-start(bf16[2,3072,128]{2,1,0:T(8,128)(2,1)S(1)} %slice_bitcast_fusion.2), channel_id=1, source_target_pairs={{3,2},{0,1},{7,6},{4,5},{11,10},{8,9},{15,14},{12,13},{19,18},{16,... | collective-permute-start | bytes 4718600 | tf_op jit(solution)/shard_map/ppermute | solution.py:432
  6.3 40.1 %collective-permute-start = (bf16[2,3072,128]{2,1,0:T(8,128)(2,1)S(1)}, bf16[2,3072,128]{2,1,0:T(8,128)(2,1)S(1)}, u32[]{:S(2)}, u32[]{:S(2)}) collective-permute-start(bf16[2,3072,128]{2,1,0:T(8,128)(2,1)S(1)} %slice_bitcast_fusion.2), channel_id=1, source_target_pairs={{1,0},{2,3},{5,4},{6,7},{9,8},{10,11},{13,12},{14,15},{17,16},{18,... | collective-permute-start | bytes 4718600 | tf_op jit(solution)/shard_map/ppermute | solution.py:432
  7.6 38.8 %collective-permute-start.9 = (bf16[2,3072,128]{2,1,0:T(8,128)(2,1)S(1)}, bf16[2,3072,128]{2,1,0:T(8,128)(2,1)S(1)}, u32[]{:S(2)}, u32[]{:S(2)}) collective-permute-start(bf16[2,3072,128]{2,1,0:T(8,128)(2,1)S(1)} %slice_bitcast_fusion.2), channel_id=1, source_target_pairs={{2,1},{1,2},{6,5},{5,6},{10,9},{9,10},{14,13},{13,14},{18,17},{17,... | collective-permute-start | bytes 4718600 | tf_op jit(solution)/shard_map/ppermute | solution.py:432
  9.9 66.9 %collective-permute-start.5 = (bf16[2,3072,128]{2,1,0:T(8,128)(2,1)S(1)}, bf16[2,3072,128]{2,1,0:T(8,128)(2,1)S(1)}, u32[]{:S(2)}, u32[]{:S(2)}) collective-permute-start(bf16[2,3072,128]{2,1,0:T(8,128)(2,1)S(1)} %slice_bitcast_fusion.1), channel_id=1, source_target_pairs={{1,0},{2,3},{5,4},{6,7},{9,8},{10,11},{13,12},{14,15},{17,16},{18,... | collective-permute-start | bytes 4718600 | tf_op jit(solution)/shard_map/ppermute | solution.py:432
  39.2 38.8 %collective-permute-start.2 = (bf16[2,3072,128]{2,1,0:T(8,128)(2,1)S(1)}, bf16[2,3072,128]{2,1,0:T(8,128)(2,1)}, u32[]{:S(2)}, u32[]{:S(2)}) collective-permute-start(bf16[2,3072,128]{2,1,0:T(8,128)(2,1)S(1)} %slice_bitcast_fusion.1), channel_id=1, source_target_pairs={{3,2},{0,1},{7,6},{4,5},{11,10},{8,9},{15,14},{12,13},{19,18},{16,... | collective-permute-start | bytes 4718600 | tf_op jit(solution)/shard_map/ppermute | solution.py:432
  44.5 33.5 %collective-permute-start.4 = (bf16[2,3072,128]{2,1,0:T(8,128)(2,1)S(1)}, bf16[2,3072,128]{2,1,0:T(8,128)(2,1)}, u32[]{:S(2)}, u32[]{:S(2)}) collective-permute-start(bf16[2,3072,128]{2,1,0:T(8,128)(2,1)S(1)} %collective-permute-done.1.refs_5_), channel_id=1, source_target_pairs={{2,1},{1,2},{6,5},{5,6},{10,9},{9,10},{14,13},{13,14},{18,17},{17,... | collective-permute-start | bytes 4718600 | tf_op jit(solution)/shard_map/ppermute | solution.py:432
  46.4 64.2 %collective-permute-start.11 = (bf16[2,3072,128]{2,1,0:T(8,128)(2,1)S(1)}, bf16[2,3072,128]{2,1,0:T(8,128)(2,1)S(1)}, u32[]{:S(2)}, u32[]{:S(2)}) collective-permute-start(bf16[2,3072,128]{2,1,0:T(8,128)(2,1)S(1)} %collective-permute-done.9.refs_3_), channel_id=1, source_target_pairs={{1,0},{2,3},{5,4},{6,7},{9,8},{10,11},{13,12},{14,15},{17,16},{18,... | collective-permute-start | bytes 4718600 | tf_op jit(solution)/shard_map/ppermute | solution.py:432
  47.7 62.9 %collective-permute-start.10 = (bf16[2,3072,128]{2,1,0:T(8,128)(2,1)S(1)}, bf16[2,3072,128]{2,1,0:T(8,128)(2,1)}, u32[]{:S(2)}, u32[]{:S(2)}) collective-permute-start(bf16[2,3072,128]{2,1,0:T(8,128)(2,1)S(1)} %slice_bitcast_fusion.1), channel_id=1, source_target_pairs={{2,1},{1,2},{6,5},{5,6},{10,9},{9,10},{14,13},{13,14},{18,17},{17,... | collective-permute-start | bytes 4718600 | tf_op jit(solution)/shard_map/ppermute | solution.py:432
  78.1 37.6 %collective-permute-start.7 = (bf16[2,3072,128]{2,1,0:T(8,128)(2,1)}, bf16[2,3072,128]{2,1,0:T(8,128)(2,1)}, u32[]{:S(2)}, u32[]{:S(2)}) collective-permute-start(bf16[2,3072,128]{2,1,0:T(8,128)(2,1)} %collective-permute-done.2.refs_4_), channel_id=1, source_target_pairs={{2,1},{1,2},{6,5},{5,6},{10,9},{9,10},{14,13},{13,14},{18,17},{17,... | collective-permute-start | bytes 4718600 | tf_op jit(solution)/shard_map/ppermute | solution.py:432
  79.9 64.5 %collective-permute-start.6 = (bf16[2,3072,128]{2,1,0:T(8,128)(2,1)}, bf16[2,3072,128]{2,1,0:T(8,128)(2,1)}, u32[]{:S(2)}, u32[]{:S(2)}) collective-permute-start(bf16[2,3072,128]{2,1,0:T(8,128)(2,1)} %collective-permute-done.4.refs_4_), channel_id=1, source_target_pairs={{1,0},{2,3},{5,4},{6,7},{9,8},{10,11},{13,12},{14,15},{17,16},{18,... | collective-permute-start | bytes 4718600 | tf_op jit(solution)/shard_map/ppermute | solution.py:432
  81.2 64.5 %collective-permute-start.3 = (bf16[2,3072,128]{2,1,0:T(8,128)(2,1)}, bf16[2,3072,128]{2,1,0:T(8,128)(2,1)S(1)}, u32[]{:S(2)}, u32[]{:S(2)}) collective-permute-start(bf16[2,3072,128]{2,1,0:T(8,128)(2,1)} %slice_bitcast_fusion), channel_id=1, source_target_pairs={{3,2},{0,1},{7,6},{4,5},{11,10},{8,9},{15,14},{12,13},{19,18},{16,... | collective-permute-start | bytes 4718600 | tf_op jit(solution)/shard_map/ppermute | solution.py:432
  111.7 45.6 %collective-permute-start.14 = (bf16[2,3072,128]{2,1,0:T(8,128)(2,1)}, bf16[2,3072,128]{2,1,0:T(8,128)(2,1)S(1)}, u32[]{:S(2)}, u32[]{:S(2)}) collective-permute-start(bf16[2,3072,128]{2,1,0:T(8,128)(2,1)} %slice_bitcast_fusion), channel_id=1, source_target_pairs={{2,1},{1,2},{6,5},{5,6},{10,9},{9,10},{14,13},{13,14},{18,17},{17,... | collective-permute-start | bytes 4718600 | tf_op jit(solution)/shard_map/ppermute | solution.py:432
  112.5 65.6 %collective-permute-start.12 = (bf16[2,3072,128]{2,1,0:T(8,128)(2,1)}, bf16[2,3072,128]{2,1,0:T(8,128)(2,1)}, u32[]{:S(2)}, u32[]{:S(2)}) collective-permute-start(bf16[2,3072,128]{2,1,0:T(8,128)(2,1)} %collective-permute-done.10.refs_3_), channel_id=1, source_target_pairs={{1,0},{2,3},{5,4},{6,7},{9,8},{10,11},{13,12},{14,15},{17,16},{18,... | collective-permute-start | bytes 4718600 | tf_op jit(solution)/shard_map/ppermute | solution.py:432
  144.4 67.4 %collective-permute-start.17 = (bf16[2,3072,128]{2,1,0:T(8,128)(2,1)}, bf16[2,3072,128]{2,1,0:T(8,128)(2,1)}, u32[]{:S(2)}, u32[]{:S(2)}) collective-permute-start(bf16[2,3072,128]{2,1,0:T(8,128)(2,1)} %collective-permute-done.7.refs_3_), channel_id=1, source_target_pairs={{1,0},{2,3},{5,4},{6,7},{9,8},{10,11},{13,12},{14,15},{17,16},{18,... | collective-permute-start | bytes 4718600 | tf_op jit(solution)/shard_map/ppermute | solution.py:432
  145.7 66.1 %collective-permute-start.8 = (bf16[2,3072,128]{2,1,0:T(8,128)(2,1)S(1)}, bf16[2,3072,128]{2,1,0:T(8,128)(2,1)S(1)}, u32[]{:S(2)}, u32[]{:S(2)}) collective-permute-start(bf16[2,3072,128]{2,1,0:T(8,128)(2,1)S(1)} %collective-permute-done.3.refs_4_), channel_id=1, source_target_pairs={{2,1},{1,2},{6,5},{5,6},{10,9},{9,10},{14,13},{13,14},{18,17},{17,... | collective-permute-start | bytes 4718600 | tf_op jit(solution)/shard_map/ppermute | solution.py:432
  155.6 30.7 %collective-permute-start.15 = (bf16[2,1536,128]{2,1,0:T(8,128)(2,1)S(1)}, bf16[2,1536,128]{2,1,0:T(8,128)(2,1)S(1)}, u32[]{:S(2)}, u32[]{:S(2)}) collective-permute-start(bf16[2,1536,128]{2,1,0:T(8,128)(2,1)S(1)} %get-tuple-element.64), channel_id=1, source_target_pairs={{0,4},{4,0},{1,5},{5,1},{2,6},{6,2},{3,7},{7,3},{8,12},{12,8},{9,1... | collective-permute-start | bytes 2359304 | tf_op jit(solution)/shard_map/ppermute | solution.py:403
  157.3 31.5 %collective-permute-start.16 = (bf16[2,1536,128]{2,1,0:T(8,128)(2,1)S(1)}, bf16[2,1536,128]{2,1,0:T(8,128)(2,1)S(1)}, u32[]{:S(2)}, u32[]{:S(2)}) collective-permute-start(bf16[2,1536,128]{2,1,0:T(8,128)(2,1)S(1)} %get-tuple-element.65), channel_id=1, source_target_pairs={{0,4},{4,0},{1,5},{5,1},{2,6},{6,2},{3,7},{7,3},{8,12},{12,8},{9,1... | collective-permute-start | bytes 2359304 | tf_op jit(solution)/shard_map/ppermute | solution.py:403
  179.4 66.0 %collective-permute-start.18 = (bf16[2,3072,128]{2,1,0:T(8,128)(2,1)}, bf16[2,3072,128]{2,1,0:T(8,128)(2,1)S(1)}, u32[]{:S(2)}, u32[]{:S(2)}) collective-permute-start(bf16[2,3072,128]{2,1,0:T(8,128)(2,1)} %broadcast_select_fusion.2), channel_id=1, source_target_pairs={{1,0},{2,3},{5,4},{6,7},{9,8},{10,11},{13,12},{14,15},{17,16},{18,... | collective-permute-start | bytes 4718600 | tf_op jit(solution)/shard_map/ppermute | solution.py:432
  186.2 35.0 %collective-permute-start.13 = (bf16[2,1536,128]{2,1,0:T(8,128)(2,1)S(1)}, bf16[2,1536,128]{2,1,0:T(8,128)(2,1)S(1)}, u32[]{:S(2)}, u32[]{:S(2)}) collective-permute-start(bf16[2,1536,128]{2,1,0:T(8,128)(2,1)S(1)} %send_1_0.1), channel_id=1, source_target_pairs={{0,4},{4,0},{1,5},{5,1},{2,6},{6,2},{3,7},{7,3},{8,12},{12,8},{9,1... | collective-permute-start | bytes 2359304 | tf_op jit(solution)/shard_map/ppermute | solution.py:403
  213.1 66.0 %collective-permute-start.20 = (bf16[2,3072,128]{2,1,0:T(8,128)(2,1)}, bf16[2,3072,128]{2,1,0:T(8,128)(2,1)S(1)}, u32[]{:S(2)}, u32[]{:S(2)}) collective-permute-start(bf16[2,3072,128]{2,1,0:T(8,128)(2,1)} %broadcast_select_fusion.1), channel_id=1, source_target_pairs={{1,0},{2,3},{5,4},{6,7},{9,8},{10,11},{13,12},{14,15},{17,16},{18,... | collective-permute-start | bytes 4718600 | tf_op jit(solution)/shard_map/ppermute | solution.py:432
  219.8 37.2 %collective-permute-start.19 = (bf16[2,1536,128]{2,1,0:T(8,128)(2,1)S(1)}, bf16[2,1536,128]{2,1,0:T(8,128)(2,1)S(1)}, u32[]{:S(2)}, u32[]{:S(2)}) collective-permute-start(bf16[2,1536,128]{2,1,0:T(8,128)(2,1)S(1)} %send_1_1.1), channel_id=1, source_target_pairs={{0,4},{4,0},{1,5},{5,1},{2,6},{6,2},{3,7},{7,3},{8,12},{12,8},{9,1... | collective-permute-start | bytes 2359304 | tf_op jit(solution)/shard_map/ppermute | solution.py:403
  248.2 64.7 %collective-permute-start.22 = (bf16[2,3072,128]{2,1,0:T(8,128)(2,1)}, bf16[2,3072,128]{2,1,0:T(8,128)(2,1)}, u32[]{:S(2)}, u32[]{:S(2)}) collective-permute-start(bf16[2,3072,128]{2,1,0:T(8,128)(2,1)} %broadcast_select_fusion), channel_id=1, source_target_pairs={{1,0},{2,3},{5,4},{6,7},{9,8},{10,11},{13,12},{14,15},{17,16},{18,... | collective-permute-start | bytes 4718600 | tf_op jit(solution)/shard_map/ppermute | solution.py:432
  255.3 31.6 %collective-permute-start.21 = (bf16[2,1536,128]{2,1,0:T(8,128)(2,1)}, bf16[2,1536,128]{2,1,0:T(8,128)(2,1)S(1)}, u32[]{:S(2)}, u32[]{:S(2)}) collective-permute-start(bf16[2,1536,128]{2,1,0:T(8,128)(2,1)} %send_2_0.1), channel_id=1, source_target_pairs={{0,4},{4,0},{1,5},{5,1},{2,6},{6,2},{3,7},{7,3},{8,12},{12,8},{9,1... | collective-permute-start | bytes 2359304 | tf_op jit(solution)/shard_map/ppermute | solution.py:403
  295.8 27.8 %collective-permute-start.27 = (bf16[384,128]{1,0:T(8,128)(2,1)S(1)}, bf16[384,128]{1,0:T(8,128)(2,1)S(1)}, u32[]{:S(2)}, u32[]{:S(2)}) collective-permute-start(bf16[384,128]{1,0:T(8,128)(2,1)S(1)} %get-tuple-element.93), channel_id=1, source_target_pairs={{0,8},{8,16},{16,24},{24,0},{1,9},{9,17},{17,25},{25,1},{2,10},{10... | collective-permute-start | bytes 294920 | tf_op jit(solution)/shard_map/ppermute | solution.py:414
  (19 other events, 445.2 us)
where the time goes:
time: 332 us; the launch traced here: 330 us
  waiting for transfers between devices  189 us (57%)
  Pallas kernels  64.5 us (19%)
  starting transfers between devices  52.3 us (16%)
  local copies, waits for them, and re-layouts  14.2 us (4%)
  other arithmetic  7.36 us (2%)
    ppermute x18, waiting for transfers between devices, launch(): lax.ppermute(value, 'col', [(zz, to) for zz, to, *_ in moves])  186 us
    pallas_call x10, Pallas kernels, slice_product(): pl.pallas_call(functools.partial(slice_kernel, cfg), out_shape=outs, in_s...  64.5 us
    ppermute x18, starting transfers between devices, launch(): lax.ppermute(value, 'col', [(zz, to) for zz, to, *_ in moves])  35.9 us
    ppermute x6, starting transfers between devices, run(): total = total + lax.ppermute(shares[d], 'pole', ways).astype(jnp.float32)  8.71 us
    ppermute x6, starting transfers between devices, run(): state['sent'][p, i] = lax.ppermute(part, 'row', [(0, 1), (1, 0)])  7.69 us
  transfers between devices with their start and end apart: 30, of which 12 were waited for; matrix products, arithmetic and copies ran while one was open for 4% of the time, Pallas kernels for 20%

commit v1 on v0

--- a/solution.py
+++ b/solution.py
@@ -51,7 +51,10 @@
     pole, tile, row_tiles, n_pole = (cfg[k] for k in ("pole", "tile", "row_tiles", "n_pole"))
     parts = cfg["parts"]
     n_parts = len(parts)
-    keep, last = cfg["kind"] == "keep", cfg["last"]
+    keep, fold, last = cfg["kind"] == "keep", cfg["kind"] == "fold", cfg["last"]
+    low_tile, n_tiles = cfg["span"]
+    folded = low_tile > 0
+    span = pl.ds(low_tile * tile, n_tiles * tile)
     refs = list(refs)
 
     def take(count):
@@ -63,8 +66,13 @@
     cands = dict(zip(cfg["arrays"], take(len(cfg["arrays"]))))
     if keep:
         recv = take(n_parts)
+        earlier = take(2 if folded else 0)
         take(1 if cfg["aliased"] else 0)
-    outs = take(1 if keep else n_parts)
+    if fold:
+        (panel,) = take(1)
+    outs = take(2 if fold else 1 if keep else n_parts)
+    if keep:
+        (panel,) = outs
     dens = take(n_pole if last else 0)
     abuf, wbuf, prod, obuf, asem, wsem, osem = take(7)
     width = wbuf.shape[1] // (2 * n_parts)
@@ -80,15 +88,19 @@
     def tile_rows(r):
         return pl.ds(pl.multiple_of(r * tile, tile), tile)
 
+    def single(r):
+        at = meta[row_tiles + r]
+        return (meta[r] == SINGLE) & (at >= low_tile) & (at < low_tile + n_tiles)
+
     def fetch(r, act):
         slot = lax.rem(r, n_buf)
 
         @pl.when(meta[r] == FULL)
         def _():
             for c in range(2):
-                act(pltpu.make_async_copy(inv.at[pole, c, tile_rows(r), :], abuf.at[slot, c], asem.at[slot, c]))
-
-        @pl.when(meta[r] == SINGLE)
+                act(pltpu.make_async_copy(inv.at[pole, c, tile_rows(r), span], abuf.at[slot, c], asem.at[slot, c]))
+
+        @pl.when(single(r))
         def _():
             cols = tile_rows(meta[row_tiles + r])
             for c in range(2):
@@ -100,12 +112,13 @@
 
     def lower_copies(j, ref):
         return [
-            pltpu.make_async_copy(ref.at[h], wbuf.at[:, pl.ds((2 * j + h) * width, width)], wsem.at[j, h])
+            pltpu.make_async_copy(ref[h], wbuf.at[:, pl.ds((2 * j + h) * width, width)], wsem.at[j, h])
             for h in range(2)
         ]
 
     def source(name):
-        return cands[name].at[pole] if name == "own" else cands[name]
+        whole = cands[name].at[pole] if name == "own" else cands[name]
+        return [whole.at[h] if name in cfg["cut"] else whole.at[h, span, :] for h in range(2)]
 
     for j, (names, base) in enumerate(parts):
         for i, name in enumerate(names):
@@ -121,11 +134,17 @@
     if keep:
         rbuf, rsem = take(2)
         extras += [pltpu.make_async_copy(recv[j], rbuf.at[j], rsem.at[j]) for j in range(n_parts)]
+    if fold or (last and not folded):
+        pbuf, psem = take(2)
+        extras += [
+            pltpu.make_async_copy(panel.at[q, :, :, columns[0]], pbuf.at[q], psem.at[q]) for q in range(pole)
+        ]
+    if last and folded:
+        held, hsem = take(2)
+        base, bsem = take(2)
+        extras += [pltpu.make_async_copy(earlier[0], held, hsem), pltpu.make_async_copy(earlier[1], base, bsem)]
     if last:
-        pbuf, d32, d16, psem, dsem = take(5)
-        extras += [
-            pltpu.make_async_copy(outs[0].at[q, :, :, columns[0]], pbuf.at[q], psem.at[q]) for q in range(pole)
-        ]
+        d32, d16, dsem = take(3)
     for copy in extras:
         copy.start()
     for r in range(1, min(n_buf, row_tiles)):
@@ -136,8 +155,21 @@
 
     def out_copy(r, j):
         rows = tile_rows(r)
-        target = outs[0].at[pole, :, rows, columns[j]] if keep else outs[j].at[:, rows, :]
+        target = panel.at[pole, :, rows, columns[j]] if keep else outs[j].at[:, rows, :]
         return pltpu.make_async_copy(obuf.at[j, :, rows, :], target, osem.at[r, j])
+
+    def sum_copy(r):
+        return pltpu.make_async_copy(sbuf.at[tile_rows(r), :], outs[1].at[tile_rows(r), :], ssem.at[r])
+
+    def other_poles(rows):
+        return sum(
+            weight[q, 0] * pbuf[q, 1, rows, :].astype(jnp.float32)
+            + weight[q, 1] * pbuf[q, 0, rows, :].astype(jnp.float32)
+            for q in range(pole)
+        )
+
+    if fold:
+        sbuf, ssem = take(2)
 
     def step(r, carry):
         slot = lax.rem(r, n_buf)
@@ -146,15 +178,15 @@
 
         @pl.when(meta[r] == FULL)
         def _():
-            both = abuf[slot].reshape(2 * tile, depth)
+            both = abuf[slot].reshape(2 * tile, n_tiles * tile)
             prod[...] = jnp.dot(both, wbuf[...], preferred_element_type=jnp.float32)
 
-        @pl.when(meta[r] == SINGLE)
+        @pl.when(single(r))
         def _():
             both = abuf[slot, :, :, :tile].reshape(2 * tile, tile)
-            prod[...] = jnp.dot(both, wbuf[tile_rows(meta[row_tiles + r]), :], preferred_element_type=jnp.float32)
-
-        @pl.when(meta[r] == 0)
+            prod[...] = jnp.dot(both, wbuf[tile_rows(meta[row_tiles + r] - low_tile), :], preferred_element_type=jnp.float32)
+
+        @pl.when((meta[r] != FULL) & jnp.logical_not(single(r)))
         def _():
             prod[...] = jnp.zeros_like(prod)
 
@@ -176,22 +208,25 @@
             re = prod[:tile, low] - prod[tile:, high]
             im = prod[:tile, high] + prod[tile:, low]
             if keep:
-                re = -(re + rbuf[j, 0, rows, :].astype(jnp.float32))
-                im = -(im + rbuf[j, 1, rows, :].astype(jnp.float32))
-            re = re.astype(jnp.bfloat16)
-            im = im.astype(jnp.bfloat16)
+                re = re + rbuf[j, 0, rows, :].astype(jnp.float32)
+                im = im + rbuf[j, 1, rows, :].astype(jnp.float32)
+                if folded:
+                    re = re + held[0, rows, :]
+                    im = im + held[1, rows, :]
+                re, im = -re, -im
+            re = re.astype(obuf.dtype)
+            im = im.astype(obuf.dtype)
             obuf[j, 0, rows, :] = re
             obuf[j, 1, rows, :] = im
             out_copy(r, j).start()
         if last:
             total = weight[pole, 0] * im.astype(jnp.float32) + weight[pole, 1] * re.astype(jnp.float32)
-            for q in range(pole):
-                total = total + (
-                    weight[q, 0] * pbuf[q, 1, rows, :].astype(jnp.float32)
-                    + weight[q, 1] * pbuf[q, 0, rows, :].astype(jnp.float32)
-                )
+            total = total + (base[rows, :] if folded else other_poles(rows))
             d32[rows, :] = total
             d16[rows, :] = total.astype(jnp.bfloat16)
+        if fold:
+            sbuf[rows, :] = other_poles(rows)
+            sum_copy(r).start()
         return carry
 
     lax.fori_loop(0, row_tiles, step, 0)
@@ -212,16 +247,19 @@
     def drain(r, carry):
         for j in range(n_parts):
             out_copy(r, j).wait()
+        if fold:
+            sum_copy(r).wait()
         return carry
 
     lax.fori_loop(0, row_tiles, drain, 0)
 
 
-def slice_product(cfg, meta, weight, inverse, arrays, width, recv=None, panel=None):
-    poles, _, rows, depth = inverse.shape
+def slice_product(cfg, meta, weight, inverse, arrays, width, recv=None, panel=None, earlier=()):
+    poles, _, rows, _ = inverse.shape
     tile, row_tiles, n_pole, parts = cfg["tile"], cfg["row_tiles"], cfg["n_pole"], cfg["parts"]
-    keep, last = cfg["kind"] == "keep", cfg["last"]
+    keep, fold, last = cfg["kind"] == "keep", cfg["kind"] == "fold", cfg["last"]
     n_buf = min(row_tiles, 4)
+    depth = cfg["span"][1] * tile
     n_parts = len(parts)
     names = sorted({name for part, _ in parts for name in part})
     part_shape = (2, rows, width)
@@ -230,13 +268,17 @@
     aliases = {}
     outs = []
     if keep:
-        operands += recv
-        specs += [ANY] * n_parts
+        operands += [*recv, *earlier]
+        specs += [ANY] * (n_parts + len(earlier))
         outs.append(jax.ShapeDtypeStruct((poles, 2, rows, cfg["panel_width"]), jnp.bfloat16))
         if panel is not None:
             aliases = {len(operands): 0}
             operands.append(panel)
             specs.append(ANY)
+    elif fold:
+        operands.append(panel)
+        specs.append(ANY)
+        outs += [jax.ShapeDtypeStruct(part_shape, jnp.float32), jax.ShapeDtypeStruct((rows, width), jnp.float32)]
     else:
         outs += [jax.ShapeDtypeStruct(part_shape, jnp.bfloat16)] * n_parts
     if last:
@@ -247,21 +289,29 @@
         pltpu.VMEM((n_buf, 2, tile, depth), jnp.bfloat16),
         pltpu.VMEM((depth, 2 * width * n_parts), jnp.bfloat16),
         pltpu.VMEM((2 * tile, 2 * width * n_parts), jnp.float32),
-        pltpu.VMEM((n_parts, *part_shape), jnp.bfloat16),
+        pltpu.VMEM((n_parts, *part_shape), jnp.float32 if fold else jnp.bfloat16),
         pltpu.SemaphoreType.DMA((n_buf, 2)),
         pltpu.SemaphoreType.DMA((n_parts, 2)),
         pltpu.SemaphoreType.DMA((row_tiles, n_parts)),
     ]
     if keep:
         scratch += [pltpu.VMEM((n_parts, *part_shape), jnp.bfloat16), pltpu.SemaphoreType.DMA((n_parts,))]
+    if fold or (last and not earlier):
+        scratch += [
+            pltpu.VMEM((max(poles - 1, 1), *part_shape), jnp.bfloat16),
+            pltpu.SemaphoreType.DMA((max(poles - 1, 1),)),
+        ]
+    if last and earlier:
+        scratch += [pltpu.VMEM(part_shape, jnp.float32), pltpu.SemaphoreType.DMA]
+        scratch += [pltpu.VMEM((rows, width), jnp.float32), pltpu.SemaphoreType.DMA]
     if last:
         scratch += [
-            pltpu.VMEM((max(poles - 1, 1), *part_shape), jnp.bfloat16),
             pltpu.VMEM((rows, width), jnp.float32),
             pltpu.VMEM((rows, width), jnp.bfloat16),
-            pltpu.SemaphoreType.DMA((max(poles - 1, 1),)),
             pltpu.SemaphoreType.DMA((n_pole,)),
         ]
+    if fold:
+        scratch += [pltpu.VMEM((rows, width), jnp.float32), pltpu.SemaphoreType.DMA((row_tiles,))]
     cfg = dict(cfg, aliased=panel is not None, arrays=names)
     return pl.pallas_call(
         functools.partial(slice_kernel, cfg),
@@ -332,6 +382,8 @@
         z, y, mine = lax.axis_index("col"), lax.axis_index("row"), lax.axis_index("pole")
         lists, where, ready = plan_transfers(n_col, poles)
         final = len(lists["out"]) - 1
+        final_name = lists["out"][final][0]
+        cuts = col_tiles - max(1, 3 * col_tiles // 8) if col_tiles > 1 and poles > 1 else 0
 
         head_size = 2 * row_tiles + 1
         tables = []
@@ -395,6 +447,8 @@
                 row_tiles=row_tiles,
                 n_pole=n_pole,
                 panel_width=group * width,
+                span=(0, col_tiles),
+                cut=[],
             )
             if kind == "send":
                 made = slice_product(cfg, late["meta"], pole_weight, inverse, arrays, width)
@@ -403,8 +457,17 @@
                     state["sent"][(p, i)] = lax.ppermute(part, "row", [(0, 1), (1, 0)])
                 return
             recv = [state["sent"][(p, i)] for i in bunch]
+            sources, earlier = arrays, ()
+            if cuts and final_name in parts[0][0]:
+                sources = dict(arrays, **{final_name: arrays[final_name][0]})
+                first = dict(cfg, name=f"fold_{p}_{bunch[0]}", kind="fold", last=False, span=(0, cuts), cut=[final_name])
+                earlier = slice_product(
+                    first, late["meta"], pole_weight, inverse, sources, width, panel=state["panel"]
+                )
+                sources = dict(arrays, **{final_name: arrays[final_name][1]})
+                cfg.update(span=(cuts, col_tiles - cuts), cut=[final_name])
             panel, *shares = slice_product(
-                cfg, late["meta"], pole_weight, inverse, arrays, width, recv, state["panel"]
+                cfg, late["meta"], pole_weight, inverse, sources, width, recv, state["panel"], earlier
             )
             state["panel"] = panel
             if shares:
@@ -412,7 +475,10 @@
                 for d in range(1, n_pole):
                     ways = [(q, (q + d) % n_pole) for q in range(n_pole)]
                     total = total + lax.ppermute(shares[d], "pole", ways).astype(jnp.float32)
-                state["dens"][bunch[0]] = (total, meta[parts[0][1] + 1])
+                state["dens"][bunch[0]] = total
+
+        def is_one_of(spots):
+            return functools.reduce(jnp.logical_or, [(z == a) & (y == b) for a, b in spots])
 
         def launch(kind, t, deps):
             if t >= len(lists[kind]):
@@ -427,9 +493,13 @@
             values, state["panel"], _ = lax.optimization_barrier((values, state["panel"], deps))
             value = values[0]
             for other, (_, spots) in zip(values[1:], held[1:]):
-                here = functools.reduce(jnp.logical_or, [(z == a) & (y == b) for a, b in spots])
-                value = jnp.where(here, other, value)
-            arrays[name] = lax.ppermute(value, "col", [(zz, to) for zz, to, *_ in moves])
+                value = jnp.where(is_one_of(spots), other, value)
+            ways = [(zz, to) for zz, to, *_ in moves]
+            if name == final_name and cuts:
+                pieces = [value[:, : cuts * tile], value[:, cuts * tile :]]
+                arrays[name] = [lax.ppermute(piece, "col", ways) for piece in pieces]
+            else:
+                arrays[name] = lax.ppermute(value, "col", ways)
 
         def landed(kind, t):
             return [arrays[lists[kind][t][0]]] if 0 <= t < len(lists[kind]) else []
@@ -445,7 +515,7 @@
             deps += [state["sent"][key] for key, at in sent_at.items() if at == t - 2]
             launch("out", t + 2, deps)
             launch("across", t + 2, landed("out", t) + landed("across", t))
-            launch("in", t + 1, landed("out", t - 1) + landed("in", t))
+            launch("in", t + 1, landed("out", t) + landed("in", t))
             for kind in ("send", "keep"):
                 for call in queue[t]:
                     if call[1] == kind:
@@ -457,9 +527,10 @@
         dens = state["dens"]
         columns = []
         for c in range(group):
-            value = dens[0][0]
+            value = dens[0]
             for i in range(1, group):
-                value = jnp.where(dens[i][1] == c, dens[i][0], value)
+                spots = [(a, b) for a, b in places if half_order(n_col, b, a)[i] - b * group == c]
+                value = jnp.where(is_one_of(spots), dens[i], value)
             columns.append(value)
         return (state["panel"], jnp.concatenate(columns, axis=1))
 

time: 332 us -> 332 us (level)
  Pallas kernels: 64.5 us -> 111 us
  waiting for transfers between devices: 189 us -> 143 us
    ppermute x18 -> x19, waiting for transfers between devices: 186 us -> 132 us  [the longest x17 132 us: launch(): arrays[name] = lax.ppermute(value, 'col', ways)]
    pallas_call x10 -> x11, Pallas kernels: 64.5 us -> 111 us  [slice_product(): pl.pallas_call(functools.partial(slice_kernel, cfg), out_shape=outs, in_s...]
    ppermute x6, waiting for transfers between devices: 1.12 us -> 5.62 us  [run(): state['sent'][p, i] = lax.ppermute(part, 'row', [(0, 1), (1, 0)])]
    ppermute x18 -> x19, starting transfers between devices: 35.9 us -> 39.9 us  [the longest x17 37.3 us: launch(): arrays[name] = lax.ppermute(value, 'col', ways)]
    unnamed x27 -> x35, local copies, waits for them, and re-layouts: 6.57 us -> 8.76 us
  transfers between devices with their start and end apart: 30 -> 31, of which waited for: 12 -> 13; matrix products, arithmetic and copies ran while one was open for 4% -> 4% of each run, Pallas kernels for 20% -> 33%
where the time goes in v1:
time: 332 us
  waiting for transfers between devices  143 us (43%)
  Pallas kernels  111 us (33%)
  starting transfers between devices  54.3 us (16%)
  local copies, waits for them, and re-layouts  17.3 us (5%)
  other arithmetic  6.24 us (2%)
    ppermute x17, waiting for transfers between devices, launch(): arrays[name] = lax.ppermute(value, 'col', ways)  132 us
    pallas_call x11, Pallas kernels, slice_product(): pl.pallas_call(functools.partial(slice_kernel, cfg), out_shape=outs, in_s...  111 us
    ppermute x17, starting transfers between devices, launch(): arrays[name] = lax.ppermute(value, 'col', ways)  37.3 us
    unnamed x35, local copies, waits for them, and re-layouts  8.76 us
    ppermute x6, starting transfers between devices, run(): total = total + lax.ppermute(shares[d], 'pole', ways).astype(jnp.float32)  7.4 us
    ppermute x6, starting transfers between devices, run(): state['sent'][p, i] = lax.ppermute(part, 'row', [(0, 1), (1, 0)])  7.05 us
  transfers between devices with their start and end apart: 31, of which 13 were waited for; matrix products, arithmetic and copies ran while one was open for 4% of the time, Pallas kernels for 33%

profile of v1, /device:TPU:1, one launch (start us, length us, event | category | flops | bytes accessed | tf_op | source)
XLA Modules:
  0.0 332.2 jit_solution(3057004328965908659)
XLA Ops:
  3.5 4.2 %collective-permute-start.2 = (bf16[2,3072,128]{2,1,0:T(8,128)(2,1)S(1)}, bf16[2,3072,128]{2,1,0:T(8,128)(2,1)S(1)}, u32[]{:S(2)}, u32[]{:S(2)}) collective-permute-start(bf16[2,3072,128]{2,1,0:T(8,128)(2,1)S(1)} %slice_bitcast_fusion.2), channel_id=1, source_target_pairs={{3,2},{0,1},{7,6},{4,5},{11,10},{8,9},{15,14},{12,13},{19,18},{16,... | collective-permute-start | bytes 4718600 | tf_op jit(solution)/shard_map/ppermute | solution.py:502
  11.3 28.4 %collective-permute-done.1.refs_6_ = bf16[2,3072,128]{2,1,0:T(8,128)(2,1)S(1)} collective-permute-done((bf16[2,3072,128]{2,1,0:T(8,128)(2,1)S(1)}, bf16[2,3072,128]{2,1,0:T(8,128)(2,1)S(1)}, u32[]{:S(2)}, u32[]{:S(2)}) %collective-permute-start.1) | collective-permute-done | bytes 1572896 | tf_op jit(solution)/shard_map/ppermute | solution.py:502
  40.6 4.2 %collective-permute-start.3 = (bf16[2,3072,128]{2,1,0:T(8,128)(2,1)S(1)}, bf16[2,3072,128]{2,1,0:T(8,128)(2,1)S(1)}, u32[]{:S(2)}, u32[]{:S(2)}) collective-permute-start(bf16[2,3072,128]{2,1,0:T(8,128)(2,1)S(1)} %slice_bitcast_fusion.1), channel_id=1, source_target_pairs={{3,2},{0,1},{7,6},{4,5},{11,10},{8,9},{15,14},{12,13},{19,18},{16,... | collective-permute-start | bytes 4718600 | tf_op jit(solution)/shard_map/ppermute | solution.py:502
  52.6 20.8 %collective-permute-done.refs_5_ = bf16[2,3072,128]{2,1,0:T(8,128)(2,1)S(1)} collective-permute-done((bf16[2,3072,128]{2,1,0:T(8,128)(2,1)S(1)}, bf16[2,3072,128]{2,1,0:T(8,128)(2,1)S(1)}, u32[]{:S(2)}, u32[]{:S(2)}) %collective-permute-start) | collective-permute-done | bytes 1572896 | tf_op jit(solution)/shard_map/ppermute | solution.py:502
  81.1 10.5 %collective-permute-start.4 = (bf16[2,3072,128]{2,1,0:T(8,128)(2,1)}, bf16[2,3072,128]{2,1,0:T(8,128)(2,1)}, u32[]{:S(2)}, u32[]{:S(2)}) collective-permute-start(bf16[2,3072,128]{2,1,0:T(8,128)(2,1)} %slice_bitcast_fusion), channel_id=1, source_target_pairs={{3,2},{0,1},{7,6},{4,5},{11,10},{8,9},{15,14},{12,13},{19,18},{16,... | collective-permute-start | bytes 4718600 | tf_op jit(solution)/shard_map/ppermute | solution.py:502
  91.6 15.5 %collective-permute-done.11.refs_7_ = bf16[2,3072,128]{2,1,0:T(8,128)(2,1)S(1)} collective-permute-done((bf16[2,3072,128]{2,1,0:T(8,128)(2,1)S(1)}, bf16[2,3072,128]{2,1,0:T(8,128)(2,1)S(1)}, u32[]{:S(2)}, u32[]{:S(2)}) %collective-permute-start.11) | collective-permute-done | bytes 1572896 | tf_op jit(solution)/shard_map/ppermute | solution.py:502
  110.3 30.6 %collective-permute-done.6.refs_8_ = bf16[2,3072,128]{2,1,0:T(8,128)(2,1)} collective-permute-done((bf16[2,3072,128]{2,1,0:T(8,128)(2,1)}, bf16[2,3072,128]{2,1,0:T(8,128)(2,1)}, u32[]{:S(2)}, u32[]{:S(2)}) %collective-permute-start.6) | collective-permute-done | bytes 1572896 | tf_op jit(solution)/shard_map/ppermute | solution.py:502
  146.2 15.3 %send_0_0.1 = (bf16[2,1536,128]{2,1,0:T(8,128)(2,1)S(1)}, bf16[2,1536,128]{2,1,0:T(8,128)(2,1)S(1)}) custom-call(s32[33]{0:T(128)S(1)} %pad_add_fusion.refs_0_, f32[3,2]{1,0:T(4,128)S(1)} %copy.14.refs_1_, bf16[3,2,1536,3072]{3,2,1,0:T(8,128)(2,1)} %refs_2_.21, bf16[2,3072,128]{2,1,0:T(8,128)(2,1)S(1)} %copy-done.7, ...), custom_call_target="tpu_custom_call" | custom-call | flops 283115520 | bytes 196608 | tf_op jit(solution)/shard_map/send_0_0/pallas_call | solution.py:316
  163.0 11.6 %collective-permute-done.12.refs_4_ = bf16[2,3072,128]{2,1,0:T(8,128)(2,1)} collective-permute-done((bf16[2,3072,128]{2,1,0:T(8,128)(2,1)}, bf16[2,3072,128]{2,1,0:T(8,128)(2,1)}, u32[]{:S(2)}, u32[]{:S(2)}) %collective-permute-start.12) | collective-permute-done | bytes 1572896 | tf_op jit(solution)/shard_map/ppermute | solution.py:502
  177.4 10.1 %send_1_0.1 = bf16[2,1536,128]{2,1,0:T(8,128)(2,1)S(1)} custom-call(s32[33]{0:T(128)S(1)} %pad_add_fusion.refs_0_, f32[3,2]{1,0:T(4,128)S(1)} %copy.14.refs_1_, bf16[3,2,1536,3072]{3,2,1,0:T(8,128)(2,1)} %refs_2_.21, bf16[2,3072,128]{2,1,0:T(8,128)(2,1)} %collective-permute-done.10.refs_3_, bf16[2,3072,128]{2,1,0:T(8,128)(2,1)} %collective-permute-done.12.refs_4_, ...), custom_call_target="tpu_custom_call" | custom-call | flops 141557760 | bytes 196608 | tf_op jit(solution)/shard_map/send_1_0/pallas_call | solution.py:316
  189.7 5.6 %collective-permute-done.16.refs_11_ = bf16[2,1536,128]{2,1,0:T(8,128)(2,1)S(1)} collective-permute-done((bf16[2,1536,128]{2,1,0:T(8,128)(2,1)S(1)}, bf16[2,1536,128]{2,1,0:T(8,128)(2,1)S(1)}, u32[]{:S(2)}, u32[]{:S(2)}) %collective-permute-start.16) | collective-permute-done | bytes 786464 | tf_op jit(solution)/shard_map/ppermute | solution.py:457
  195.3 13.7 %keep_0_0.1.refs_7_ = bf16[3,2,1536,256]{3,2,1,0:T(8,128)(2,1)} custom-call(s32[33]{0:T(128)S(1)} %pad_add_fusion.refs_0_, f32[3,2]{1,0:T(4,128)S(1)} %copy.14.refs_1_, bf16[3,2,1536,3072]{3,2,1,0:T(8,128)(2,1)} %refs_2_.21, bf16[2,3072,128]{2,1,0:T(8,128)(2,1)S(1)} %copy-done.8, bf16[2,3072,128]{2,1,0:T(8,128)(2,1)} %collective-permute-done.5.refs_4_, ...), custom_call_target="tpu_custom_call" | custom-call | flops 283115520 | bytes 196608 | tf_op jit(solution)/shard_map/keep_0_0/pallas_call | solution.py:316
  211.9 8.9 %send_1_1.1 = bf16[2,1536,128]{2,1,0:T(8,128)(2,1)S(1)} custom-call(s32[33]{0:T(128)S(1)} %pad_add_fusion.refs_0_, f32[3,2]{1,0:T(4,128)S(1)} %copy.14.refs_1_, bf16[3,2,1536,3072]{3,2,1,0:T(8,128)(2,1)} %refs_2_.21, bf16[2,3072,128]{2,1,0:T(8,128)(2,1)} %collective-permute-done.7.refs_3_, bf16[2,3072,128]{2,1,0:T(8,128)(2,1)S(1)} %copy-done.5, ...), custom_call_target="tpu_custom_call" | custom-call | flops 141557760 | bytes 196608 | tf_op jit(solution)/shard_map/send_1_1/pallas_call | solution.py:316
  221.3 9.1 %keep_1_0.1.refs_8_ = bf16[3,2,1536,256]{3,2,1,0:T(8,128)(2,1)} custom-call(s32[33]{0:T(128)S(1)} %pad_add_fusion.refs_0_, f32[3,2]{1,0:T(4,128)S(1)} %copy.14.refs_1_, bf16[3,2,1536,3072]{3,2,1,0:T(8,128)(2,1)} %refs_2_.21, bf16[2,3072,128]{2,1,0:T(8,128)(2,1)} %collective-permute-done.10.refs_3_, ...), custom_call_target="tpu_custom_call", output_to_operand_aliasing={{}: (7, {})} | custom-call | flops 141557760 | bytes 196608 | tf_op jit(solution)/shard_map/keep_1_0/pallas_call | solution.py:316
  230.5 11.5 %collective-permute-done.18.refs_4_.refs_5_ = bf16[2,3072,128]{2,1,0:T(8,128)(2,1)S(1)} collective-permute-done((bf16[2,3072,128]{2,1,0:T(8,128)(2,1)}, bf16[2,3072,128]{2,1,0:T(8,128)(2,1)S(1)}, u32[]{:S(2)}, u32[]{:S(2)}) %collective-permute-start.18) | collective-permute-done | bytes 1572896 | tf_op jit(solution)/shard_map/ppermute | solution.py:502
  245.9 8.8 %send_2_0.1 = bf16[2,1536,128]{2,1,0:T(8,128)(2,1)} custom-call(s32[33]{0:T(128)S(1)} %pad_add_fusion.refs_0_, f32[3,2]{1,0:T(4,128)S(1)} %copy.14.refs_1_, bf16[3,2,1536,3072]{3,2,1,0:T(8,128)(2,1)} %refs_2_.21, bf16[2,3072,128]{2,1,0:T(8,128)(2,1)S(1)} %collective-permute-done.14.refs_3_, ...), custom_call_target="tpu_custom_call" | custom-call | flops 141557760 | bytes 196608 | tf_op jit(solution)/shard_map/send_2_0/pallas_call | solution.py:316
  256.4 8.9 %keep_1_1.1.refs_7_ = bf16[3,2,1536,256]{3,2,1,0:T(8,128)(2,1)} custom-call(s32[33]{0:T(128)S(1)} %pad_add_fusion.refs_0_, f32[3,2]{1,0:T(4,128)S(1)} %copy.14.refs_1_, bf16[3,2,1536,3072]{3,2,1,0:T(8,128)(2,1)} %refs_2_.21, bf16[2,3072,128]{2,1,0:T(8,128)(2,1)} %collective-permute-done.7.refs_3_, ...), custom_call_target="tpu_custom_call", output_to_operand_aliasing={{}: (8, {})} | custom-call | flops 141557760 | bytes 196608 | tf_op jit(solution)/shard_map/keep_1_1/pallas_call | solution.py:316
  265.4 10.2 %collective-permute-done.20.refs_6_.refs_4_ = bf16[2,3072,128]{2,1,0:T(8,128)(2,1)S(1)} collective-permute-done((bf16[2,3072,128]{2,1,0:T(8,128)(2,1)}, bf16[2,3072,128]{2,1,0:T(8,128)(2,1)S(1)}, u32[]{:S(2)}, u32[]{:S(2)}) %collective-permute-start.20) | collective-permute-done | bytes 1572896 | tf_op jit(solution)/shard_map/ppermute | solution.py:502
  276.8 8.9 %send_2_1.1 = bf16[2,1536,128]{2,1,0:T(8,128)(2,1)S(1)} custom-call(s32[33]{0:T(128)S(1)} %pad_add_fusion.refs_0_, f32[3,2]{1,0:T(4,128)S(1)} %copy.14.refs_1_, bf16[3,2,1536,3072]{3,2,1,0:T(8,128)(2,1)} %refs_2_.21, bf16[2,3072,128]{2,1,0:T(8,128)(2,1)S(1)} %collective-permute-done.8.refs_3_, bf16[2,3072,128]{2,1,0:T(8,128)(2,1)} %collective-permute-done.4.refs_4_, ...), custom_call_target="tpu_custom_call" | custom-call | flops 141557760 | bytes 196608 | tf_op jit(solution)/shard_map/send_2_1/pallas_call | solution.py:316
  290.7 11.5 %keep_2_0.1 = (bf16[3,2,1536,256]{3,2,1,0:T(8,128)(2,1)}, f32[384,128]{1,0:T(8,128)S(1)}, bf16[384,128]{1,0:T(8,128)(2,1)S(1)}, bf16[384,128]{1,0:T(8,128)(2,1)S(1)}, bf16[384,128]{1,0:T(8,128)(2,1)S(1)}) custom-call(s32[33]{0:T(128)S(1)} %pad_add_fusion.refs_0_, f32[3,2]{1,0:T(4,128)S(1)} %copy.14.refs_1_, ...), custom_call_target="tpu_custom_call", output_to_operand_aliasing={{0}: (7, {})} | custom-call | flops 141557760 | bytes 196608 | tf_op jit(solution)/shard_map/keep_2_0/pallas_call | solution.py:316
  302.2 4.1 %collective-permute-start.28 = (bf16[384,128]{1,0:T(8,128)(2,1)S(1)}, bf16[384,128]{1,0:T(8,128)(2,1)S(1)}, u32[]{:S(2)}, u32[]{:S(2)}) collective-permute-start(bf16[384,128]{1,0:T(8,128)(2,1)S(1)} %get-tuple-element.97), channel_id=1, source_target_pairs={{0,8},{8,16},{16,24},{24,0},{1,9},{9,17},{17,25},{25,1},{2,10},{10... | collective-permute-start | bytes 294920 | tf_op jit(solution)/shard_map/ppermute | solution.py:477
  306.8 9.2 %fold_2_1.1 = (f32[2,1536,128]{2,1,0:T(8,128)S(1)}, f32[1536,128]{1,0:T(8,128)S(1)}) custom-call(s32[33]{0:T(128)S(1)} %pad_add_fusion.refs_0_, f32[3,2]{1,0:T(4,128)S(1)} %copy.14.refs_1_, bf16[3,2,1536,3072]{3,2,1,0:T(8,128)(2,1)} %refs_2_.21, bf16[2,3072,128]{2,1,0:T(8,128)(2,1)S(1)} %collective-permute-done.8.refs_3_, ...), custom_call_target="tpu_custom_call" | custom-call | flops 88473600 | bytes 196608 | tf_op jit(solution)/shard_map/fold_2_1/pallas_call | solution.py:316
  317.2 6.2 %keep_2_1.1 = (bf16[3,2,1536,256]{3,2,1,0:T(8,128)(2,1)}, f32[384,128]{1,0:T(8,128)S(1)}, bf16[384,128]{1,0:T(8,128)(2,1)S(1)}, bf16[384,128]{1,0:T(8,128)(2,1)S(1)}, bf16[384,128]{1,0:T(8,128)(2,1)S(1)}) custom-call(s32[33]{0:T(128)S(1)} %pad_add_fusion.refs_0_, f32[3,2]{1,0:T(4,128)S(1)} %copy.14.refs_1_, ...), custom_call_target="tpu_custom_call", output_to_operand_aliasing={{0}: (9, {})} | custom-call | flops 53084160 | bytes 196608 | tf_op jit(solution)/shard_map/keep_2_1/pallas_call | solution.py:316
  326.9 3.8 %collective-permute-done.26 = bf16[384,128]{1,0:T(8,128)(2,1)S(1)} collective-permute-done((bf16[384,128]{1,0:T(8,128)(2,1)S(1)}, bf16[384,128]{1,0:T(8,128)(2,1)S(1)}, u32[]{:S(2)}, u32[]{:S(2)}) %collective-permute-start.26) | collective-permute-done | bytes 98336 | tf_op jit(solution)/shard_map/ppermute | solution.py:477
  (99 shorter events, 59.5 us)
Async XLA Ops:
  2.2 37.5 %collective-permute-start.1 = (bf16[2,3072,128]{2,1,0:T(8,128)(2,1)S(1)}, bf16[2,3072,128]{2,1,0:T(8,128)(2,1)S(1)}, u32[]{:S(2)}, u32[]{:S(2)}) collective-permute-start(bf16[2,3072,128]{2,1,0:T(8,128)(2,1)S(1)} %slice_bitcast_fusion.2), channel_id=1, source_target_pairs={{1,0},{2,3},{5,4},{6,7},{9,8},{10,11},{13,12},{14,15},{17,16},{18,... | collective-permute-start | bytes 4718600 | tf_op jit(solution)/shard_map/ppermute | solution.py:502
  3.5 37.2 %collective-permute-start.2 = (bf16[2,3072,128]{2,1,0:T(8,128)(2,1)S(1)}, bf16[2,3072,128]{2,1,0:T(8,128)(2,1)S(1)}, u32[]{:S(2)}, u32[]{:S(2)}) collective-permute-start(bf16[2,3072,128]{2,1,0:T(8,128)(2,1)S(1)} %slice_bitcast_fusion.2), channel_id=1, source_target_pairs={{3,2},{0,1},{7,6},{4,5},{11,10},{8,9},{15,14},{12,13},{19,18},{16,... | collective-permute-start | bytes 4718600 | tf_op jit(solution)/shard_map/ppermute | solution.py:502
  7.7 39.0 %collective-permute-start.9 = (bf16[2,3072,128]{2,1,0:T(8,128)(2,1)S(1)}, bf16[2,3072,128]{2,1,0:T(8,128)(2,1)S(1)}, u32[]{:S(2)}, u32[]{:S(2)}) collective-permute-start(bf16[2,3072,128]{2,1,0:T(8,128)(2,1)S(1)} %slice_bitcast_fusion.2), channel_id=1, source_target_pairs={{2,1},{1,2},{6,5},{5,6},{10,9},{9,10},{14,13},{13,14},{18,17},{17,... | collective-permute-start | bytes 4718600 | tf_op jit(solution)/shard_map/ppermute | solution.py:502
  10.0 63.4 %collective-permute-start = (bf16[2,3072,128]{2,1,0:T(8,128)(2,1)S(1)}, bf16[2,3072,128]{2,1,0:T(8,128)(2,1)S(1)}, u32[]{:S(2)}, u32[]{:S(2)}) collective-permute-start(bf16[2,3072,128]{2,1,0:T(8,128)(2,1)S(1)} %slice_bitcast_fusion.1), channel_id=1, source_target_pairs={{1,0},{2,3},{5,4},{6,7},{9,8},{10,11},{13,12},{14,15},{17,16},{18,... | collective-permute-start | bytes 4718600 | tf_op jit(solution)/shard_map/ppermute | solution.py:502
  40.6 36.2 %collective-permute-start.3 = (bf16[2,3072,128]{2,1,0:T(8,128)(2,1)S(1)}, bf16[2,3072,128]{2,1,0:T(8,128)(2,1)S(1)}, u32[]{:S(2)}, u32[]{:S(2)}) collective-permute-start(bf16[2,3072,128]{2,1,0:T(8,128)(2,1)S(1)} %slice_bitcast_fusion.1), channel_id=1, source_target_pairs={{3,2},{0,1},{7,6},{4,5},{11,10},{8,9},{15,14},{12,13},{19,18},{16,... | collective-permute-start | bytes 4718600 | tf_op jit(solution)/shard_map/ppermute | solution.py:502
  44.8 32.0 %collective-permute-start.5 = (bf16[2,3072,128]{2,1,0:T(8,128)(2,1)S(1)}, bf16[2,3072,128]{2,1,0:T(8,128)(2,1)}, u32[]{:S(2)}, u32[]{:S(2)}) collective-permute-start(bf16[2,3072,128]{2,1,0:T(8,128)(2,1)S(1)} %collective-permute-done.2.refs_5_), channel_id=1, source_target_pairs={{2,1},{1,2},{6,5},{5,6},{10,9},{9,10},{14,13},{13,14},{18,17},{17,... | collective-permute-start | bytes 4718600 | tf_op jit(solution)/shard_map/ppermute | solution.py:502
  46.7 60.4 %collective-permute-start.11 = (bf16[2,3072,128]{2,1,0:T(8,128)(2,1)S(1)}, bf16[2,3072,128]{2,1,0:T(8,128)(2,1)S(1)}, u32[]{:S(2)}, u32[]{:S(2)}) collective-permute-start(bf16[2,3072,128]{2,1,0:T(8,128)(2,1)S(1)} %collective-permute-done.9.refs_3_), channel_id=1, source_target_pairs={{1,0},{2,3},{5,4},{6,7},{9,8},{10,11},{13,12},{14,15},{17,16},{18,... | collective-permute-start | bytes 4718600 | tf_op jit(solution)/shard_map/ppermute | solution.py:502
  48.0 59.1 %collective-permute-start.10 = (bf16[2,3072,128]{2,1,0:T(8,128)(2,1)S(1)}, bf16[2,3072,128]{2,1,0:T(8,128)(2,1)}, u32[]{:S(2)}, u32[]{:S(2)}) collective-permute-start(bf16[2,3072,128]{2,1,0:T(8,128)(2,1)S(1)} %slice_bitcast_fusion.1), channel_id=1, source_target_pairs={{2,1},{1,2},{6,5},{5,6},{10,9},{9,10},{14,13},{13,14},{18,17},{17,... | collective-permute-start | bytes 4718600 | tf_op jit(solution)/shard_map/ppermute | solution.py:502
  76.9 33.5 %collective-permute-start.7 = (bf16[2,3072,128]{2,1,0:T(8,128)(2,1)S(1)}, bf16[2,3072,128]{2,1,0:T(8,128)(2,1)}, u32[]{:S(2)}, u32[]{:S(2)}) collective-permute-start(bf16[2,3072,128]{2,1,0:T(8,128)(2,1)S(1)} %collective-permute-done.3.refs_4_), channel_id=1, source_target_pairs={{2,1},{1,2},{6,5},{5,6},{10,9},{9,10},{14,13},{13,14},{18,17},{17,... | collective-permute-start | bytes 4718600 | tf_op jit(solution)/shard_map/ppermute | solution.py:502
  79.8 61.1 %collective-permute-start.6 = (bf16[2,3072,128]{2,1,0:T(8,128)(2,1)}, bf16[2,3072,128]{2,1,0:T(8,128)(2,1)}, u32[]{:S(2)}, u32[]{:S(2)}) collective-permute-start(bf16[2,3072,128]{2,1,0:T(8,128)(2,1)} %collective-permute-done.5.refs_4_), channel_id=1, source_target_pairs={{1,0},{2,3},{5,4},{6,7},{9,8},{10,11},{13,12},{14,15},{17,16},{18,... | collective-permute-start | bytes 4718600 | tf_op jit(solution)/shard_map/ppermute | solution.py:502
  81.1 61.1 %collective-permute-start.4 = (bf16[2,3072,128]{2,1,0:T(8,128)(2,1)}, bf16[2,3072,128]{2,1,0:T(8,128)(2,1)}, u32[]{:S(2)}, u32[]{:S(2)}) collective-permute-start(bf16[2,3072,128]{2,1,0:T(8,128)(2,1)} %slice_bitcast_fusion), channel_id=1, source_target_pairs={{3,2},{0,1},{7,6},{4,5},{11,10},{8,9},{15,14},{12,13},{19,18},{16,... | collective-permute-start | bytes 4718600 | tf_op jit(solution)/shard_map/ppermute | solution.py:502
  108.3 54.5 %collective-permute-start.14 = (bf16[2,3072,128]{2,1,0:T(8,128)(2,1)}, bf16[2,3072,128]{2,1,0:T(8,128)(2,1)S(1)}, u32[]{:S(2)}, u32[]{:S(2)}) collective-permute-start(bf16[2,3072,128]{2,1,0:T(8,128)(2,1)} %slice_bitcast_fusion), channel_id=1, source_target_pairs={{2,1},{1,2},{6,5},{5,6},{10,9},{9,10},{14,13},{13,14},{18,17},{17,... | collective-permute-start | bytes 4718600 | tf_op jit(solution)/shard_map/ppermute | solution.py:502
  109.0 65.6 %collective-permute-start.12 = (bf16[2,3072,128]{2,1,0:T(8,128)(2,1)}, bf16[2,3072,128]{2,1,0:T(8,128)(2,1)}, u32[]{:S(2)}, u32[]{:S(2)}) collective-permute-start(bf16[2,3072,128]{2,1,0:T(8,128)(2,1)} %collective-permute-done.10.refs_3_), channel_id=1, source_target_pairs={{1,0},{2,3},{5,4},{6,7},{9,8},{10,11},{13,12},{14,15},{17,16},{18,... | collective-permute-start | bytes 4718600 | tf_op jit(solution)/shard_map/ppermute | solution.py:502
  140.9 68.2 %collective-permute-start.17 = (bf16[2,3072,128]{2,1,0:T(8,128)(2,1)}, bf16[2,3072,128]{2,1,0:T(8,128)(2,1)}, u32[]{:S(2)}, u32[]{:S(2)}) collective-permute-start(bf16[2,3072,128]{2,1,0:T(8,128)(2,1)} %collective-permute-done.7.refs_3_), channel_id=1, source_target_pairs={{1,0},{2,3},{5,4},{6,7},{9,8},{10,11},{13,12},{14,15},{17,16},{18,... | collective-permute-start | bytes 4718600 | tf_op jit(solution)/shard_map/ppermute | solution.py:502
  142.2 66.9 %collective-permute-start.8 = (bf16[2,3072,128]{2,1,0:T(8,128)(2,1)}, bf16[2,3072,128]{2,1,0:T(8,128)(2,1)S(1)}, u32[]{:S(2)}, u32[]{:S(2)}) collective-permute-start(bf16[2,3072,128]{2,1,0:T(8,128)(2,1)} %collective-permute-done.4.refs_4_), channel_id=1, source_target_pairs={{2,1},{1,2},{6,5},{5,6},{10,9},{9,10},{14,13},{13,14},{18,17},{17,... | collective-permute-start | bytes 4718600 | tf_op jit(solution)/shard_map/ppermute | solution.py:502
  162.8 32.6 %collective-permute-start.16 = (bf16[2,1536,128]{2,1,0:T(8,128)(2,1)S(1)}, bf16[2,1536,128]{2,1,0:T(8,128)(2,1)S(1)}, u32[]{:S(2)}, u32[]{:S(2)}) collective-permute-start(bf16[2,1536,128]{2,1,0:T(8,128)(2,1)S(1)} %get-tuple-element.67), channel_id=1, source_target_pairs={{0,4},{4,0},{1,5},{5,1},{2,6},{6,2},{3,7},{7,3},{8,12},{12,8},{9,1... | collective-permute-start | bytes 2359304 | tf_op jit(solution)/shard_map/ppermute | solution.py:457
  176.0 65.9 %collective-permute-start.18 = (bf16[2,3072,128]{2,1,0:T(8,128)(2,1)}, bf16[2,3072,128]{2,1,0:T(8,128)(2,1)S(1)}, u32[]{:S(2)}, u32[]{:S(2)}) collective-permute-start(bf16[2,3072,128]{2,1,0:T(8,128)(2,1)} %broadcast_select_fusion.2), channel_id=1, source_target_pairs={{1,0},{2,3},{5,4},{6,7},{9,8},{10,11},{13,12},{14,15},{17,16},{18,... | collective-permute-start | bytes 4718600 | tf_op jit(solution)/shard_map/ppermute | solution.py:502
  187.6 33.7 %collective-permute-start.13 = (bf16[2,1536,128]{2,1,0:T(8,128)(2,1)S(1)}, bf16[2,1536,128]{2,1,0:T(8,128)(2,1)S(1)}, u32[]{:S(2)}, u32[]{:S(2)}) collective-permute-start(bf16[2,1536,128]{2,1,0:T(8,128)(2,1)S(1)} %send_1_0.1), channel_id=1, source_target_pairs={{0,4},{4,0},{1,5},{5,1},{2,6},{6,2},{3,7},{7,3},{8,12},{12,8},{9,1... | collective-permute-start | bytes 2359304 | tf_op jit(solution)/shard_map/ppermute | solution.py:457
  210.5 65.1 %collective-permute-start.20 = (bf16[2,3072,128]{2,1,0:T(8,128)(2,1)}, bf16[2,3072,128]{2,1,0:T(8,128)(2,1)S(1)}, u32[]{:S(2)}, u32[]{:S(2)}) collective-permute-start(bf16[2,3072,128]{2,1,0:T(8,128)(2,1)} %broadcast_select_fusion.1), channel_id=1, source_target_pairs={{1,0},{2,3},{5,4},{6,7},{9,8},{10,11},{13,12},{14,15},{17,16},{18,... | collective-permute-start | bytes 4718600 | tf_op jit(solution)/shard_map/ppermute | solution.py:502
  220.9 35.6 %collective-permute-start.19 = (bf16[2,1536,128]{2,1,0:T(8,128)(2,1)S(1)}, bf16[2,1536,128]{2,1,0:T(8,128)(2,1)S(1)}, u32[]{:S(2)}, u32[]{:S(2)}) collective-permute-start(bf16[2,1536,128]{2,1,0:T(8,128)(2,1)S(1)} %send_1_1.1), channel_id=1, source_target_pairs={{0,4},{4,0},{1,5},{5,1},{2,6},{6,2},{3,7},{7,3},{8,12},{12,8},{9,1... | collective-permute-start | bytes 2359304 | tf_op jit(solution)/shard_map/ppermute | solution.py:457
  244.7 62.0 %collective-permute-start.24 = (bf16[2,1920,128]{2,1,0:T(8,128)(2,1)}, bf16[2,1920,128]{2,1,0:T(8,128)(2,1)S(1)}, u32[]{:S(2)}, u32[]{:S(2)}) collective-permute-start(bf16[2,1920,128]{2,1,0:T(8,128)(2,1)} %slice.21), channel_id=1, source_target_pairs={{1,0},{2,3},{5,4},{6,7},{9,8},{10,11},{13,12},{14,15},{17,16},{18,... | collective-permute-start | bytes 2949128 | tf_op jit(solution)/shard_map/ppermute | solution.py:500
  254.8 34.6 %collective-permute-start.21 = (bf16[2,1536,128]{2,1,0:T(8,128)(2,1)}, bf16[2,1536,128]{2,1,0:T(8,128)(2,1)S(1)}, u32[]{:S(2)}, u32[]{:S(2)}) collective-permute-start(bf16[2,1536,128]{2,1,0:T(8,128)(2,1)} %send_2_0.1), channel_id=1, source_target_pairs={{0,4},{4,0},{1,5},{5,1},{2,6},{6,2},{3,7},{7,3},{8,12},{12,8},{9,1... | collective-permute-start | bytes 2359304 | tf_op jit(solution)/shard_map/ppermute | solution.py:457
  285.7 31.5 %collective-permute-start.23 = (bf16[2,1536,128]{2,1,0:T(8,128)(2,1)S(1)}, bf16[2,1536,128]{2,1,0:T(8,128)(2,1)S(1)}, u32[]{:S(2)}, u32[]{:S(2)}) collective-permute-start(bf16[2,1536,128]{2,1,0:T(8,128)(2,1)S(1)} %send_2_1.1), channel_id=1, source_target_pairs={{0,4},{4,0},{1,5},{5,1},{2,6},{6,2},{3,7},{7,3},{8,12},{12,8},{9,1... | collective-permute-start | bytes 2359304 | tf_op jit(solution)/shard_map/ppermute | solution.py:457
  288.0 29.1 %collective-permute-start.22 = (bf16[2,1152,128]{2,1,0:T(8,128)(2,1)S(1)}, bf16[2,1152,128]{2,1,0:T(8,128)(2,1)S(1)}, u32[]{:S(2)}, u32[]{:S(2)}) collective-permute-start(bf16[2,1152,128]{2,1,0:T(8,128)(2,1)S(1)} %slice.20), channel_id=1, source_target_pairs={{1,0},{2,3},{5,4},{6,7},{9,8},{10,11},{13,12},{14,15},{17,16},{18,... | collective-permute-start | bytes 1769480 | tf_op jit(solution)/shard_map/ppermute | solution.py:500
  (24 other events, 524.5 us)

commit v2 on v1

--- a/solution.py
+++ b/solution.py
@@ -67,7 +67,7 @@
     if keep:
         recv = take(n_parts)
         earlier = take(2 if folded else 0)
-        take(1 if cfg["aliased"] else 0)
+        take(cfg["aliased"])
     if fold:
         (panel,) = take(1)
     outs = take(2 if fold else 1 if keep else n_parts)
@@ -238,7 +238,9 @@
         for d in range(n_pole):
             block = lax.rem(mine + d, n_pole)
             rows = pl.ds(pl.multiple_of(block * share, share), share)
-            copies.append(pltpu.make_async_copy((d16 if d else d32).at[rows, :], dens[d], dsem.at[d]))
+            copies.append(
+                pltpu.make_async_copy((d16 if d else d32).at[rows, :], dens[d], dsem.at[d])
+            )
         for copy in copies:
             copy.start()
         for copy in copies:
@@ -312,7 +314,7 @@
         ]
     if fold:
         scratch += [pltpu.VMEM((rows, width), jnp.float32), pltpu.SemaphoreType.DMA((row_tiles,))]
-    cfg = dict(cfg, aliased=panel is not None, arrays=names)
+    cfg = dict(cfg, aliased=len(aliases), arrays=names)
     return pl.pallas_call(
         functools.partial(slice_kernel, cfg),
         out_shape=outs,
@@ -320,8 +322,8 @@
         out_specs=[ANY] * len(outs),
         scratch_shapes=scratch,
         input_output_aliases=aliases,
-        compiler_params=pltpu.CompilerParams(vmem_limit_bytes=48 * 2**20),
-        cost_estimate=pl.CostEstimate(flops=30 * rows * depth * n_parts, bytes_accessed=rows * width, transcendentals=0),
+        compiler_params=pltpu.CompilerParams(vmem_limit_bytes=30 * 2**20),
+        cost_estimate=pl.CostEstimate(flops=300 * rows * depth * n_parts, bytes_accessed=rows * width, transcendentals=0),
         name=cfg["name"],
     )(*operands)
 
@@ -354,16 +356,25 @@
 
     steps = range(1, n_col)
     pairs = [(p, step) for p in range(end) for step in steps]
-    for p, step in sorted(pairs, key=lambda item: (item[0] * (n_col - 1) + item[1] - 3 * (item[1] == 1), item)):
+    pairs = sorted(pairs, key=lambda item: (item[0] * (n_col - 1) + item[1] - 3 * (item[1] == 1), item))
+
+    def add_end(i):
+        far = [hop(z, end, i + 1) for z in range(2, half)]
+        add("out", f"o{end}s{i + 1}", [(1, 0, end, first_row[i], second_row[i])] + [m for m in far if m[3] < n_col])
+
+    first_row = sorted(steps, key=lambda s: (s < half, s))
+    second_row = sorted(steps, key=lambda s: (s != half, s))
+    for p, step in pairs[:-1]:
         add("out", f"o{p}s{step}", [hop(z, p, step) for z in range(1, half)])
-    natural = list(steps)
-    turned = sorted(natural, key=lambda s: (s < half, s))
-    for i, (a, b) in enumerate(zip(natural, turned)):
-        far = [hop(z, end, i + 1) for z in range(2, half)]
-        add("out", f"o{end}s{i + 1}", [(1, 0, end, b, a)] + [m for m in far if m[3] < n_col])
-    for p in range(poles):
-        for step in steps:
-            add("across", f"a{p}s{step}", [hop(half, p, step)])
+    add_end(0)
+    for p, step in pairs[-1:]:
+        add("out", f"o{p}s{step}", [hop(z, p, step) for z in range(1, half)])
+    for i in range(1, len(first_row)):
+        add_end(i)
+    pairs = [(p, step) for p in range(poles) for step in range(1, half + 1)]
+    pairs = sorted(pairs, key=lambda item: (item[0] - (item == (end, 1)), item == (end - 1, half), item))
+    for p, step in pairs:
+        add("across", f"a{p}s{step}", [hop(half, p, step)])
     for p in range(poles):
         for step in steps:
             add("in", f"i{p}s{step}", [hop(z, p, step) for z in range(half + 1, n_col)])
@@ -389,9 +400,8 @@
         tables = []
         calls = []
         for p in range(poles):
-            whole, single = [list(range(group))], [[i] for i in range(group)]
             for kind in ("send", "keep"):
-                for bunch in single if p >= end - 1 else whole:
+                for bunch in [[i] for i in range(group)]:
                     parts = []
                     for i in bunch:
                         names, picks, columns = [], np.zeros((n_col, 2), np.int32), np.zeros((n_col, 2), np.int32)
@@ -491,15 +501,17 @@
             held = sorted(held.items(), key=lambda item: -len(item[1]))
             values = [arrays[source] for source, _ in held]
             values, state["panel"], _ = lax.optimization_barrier((values, state["panel"], deps))
-            value = values[0]
-            for other, (_, spots) in zip(values[1:], held[1:]):
-                value = jnp.where(is_one_of(spots), other, value)
             ways = [(zz, to) for zz, to, *_ in moves]
+            pieces = [slice(None)]
             if name == final_name and cuts:
-                pieces = [value[:, : cuts * tile], value[:, cuts * tile :]]
-                arrays[name] = [lax.ppermute(piece, "col", ways) for piece in pieces]
-            else:
-                arrays[name] = lax.ppermute(value, "col", ways)
+                pieces = [slice(0, cuts * tile), slice(cuts * tile, None)]
+            moved = []
+            for piece in pieces:
+                value = values[0][:, piece]
+                for other, (_, spots) in zip(values[1:], held[1:]):
+                    value = jnp.where(is_one_of(spots), other[:, piece], value)
+                moved.append(lax.ppermute(value, "col", ways))
+            arrays[name] = moved if len(moved) > 1 else moved[0]
 
         def landed(kind, t):
             return [arrays[lists[kind][t][0]]] if 0 <= t < len(lists[kind]) else []
@@ -524,13 +536,12 @@
                     made = [state["part"][key] for key, at in sent_at.items() if at == t]
                     late["meta"], state["panel"], _ = lax.optimization_barrier((late["meta"], state["panel"], made))
 
-        dens = state["dens"]
         columns = []
         for c in range(group):
-            value = dens[0]
+            value = state["dens"][0]
             for i in range(1, group):
                 spots = [(a, b) for a, b in places if half_order(n_col, b, a)[i] - b * group == c]
-                value = jnp.where(is_one_of(spots), dens[i], value)
+                value = jnp.where(is_one_of(spots), state["dens"][i], value)
             columns.append(value)
         return (state["panel"], jnp.concatenate(columns, axis=1))
 

time: 332 us -> 334 us (level)
  waiting for transfers between devices: 143 us -> 137 us
    ppermute x6, waiting for transfers between devices: 5.62 us -> 0.02 us  [run(): state['sent'][p, i] = lax.ppermute(part, 'row', [(0, 1), (1, 0)])]
    unnamed x35 -> x45, local copies, waits for them, and re-layouts: 8.76 us -> 12.4 us
    pallas_call x11 -> x13, Pallas kernels: 111 us -> 114 us  [slice_product(): pl.pallas_call(functools.partial(slice_kernel, cfg), out_shape=outs, in_s...]
  transfers between devices with their start and end apart: 31 -> 31, of which waited for: 13 -> 12; matrix products, arithmetic and copies ran while one was open for 4% -> 3% of each run, Pallas kernels for 33% -> 34%
where the time goes in v2:
time: 334 us; the launch traced here: 332 us
  waiting for transfers between devices  137 us (41%)
  Pallas kernels  114 us (34%)
  starting transfers between devices  54.3 us (16%)
  local copies, waits for them, and re-layouts  19.9 us (6%)
  other arithmetic  5.49 us (2%)
    ppermute x19, waiting for transfers between devices, launch(): moved.append(lax.ppermute(value, 'col', ways))  133 us
    pallas_call x13, Pallas kernels, slice_product(): pl.pallas_call(functools.partial(slice_kernel, cfg), out_shape=outs, in_s...  114 us
    ppermute x19, starting transfers between devices, launch(): moved.append(lax.ppermute(value, 'col', ways))  37.5 us
    unnamed x45, local copies, waits for them, and re-layouts  12.4 us
    ppermute x6, starting transfers between devices, run(): state['sent'][p, i] = lax.ppermute(part, 'row', [(0, 1), (1, 0)])  8.75 us
    ppermute x6, starting transfers between devices, run(): total = total + lax.ppermute(shares[d], 'pole', ways).astype(jnp.float32)  8.06 us
    squeeze x3, local copies, waits for them, and re-layouts, body(): arrays['own', p] = rest[p]  6.85 us
  transfers between devices with their start and end apart: 31, of which 12 were waited for; matrix products, arithmetic and copies ran while one was open for 3% of the time, Pallas kernels for 34%

profile of v2, /device:TPU:1, one launch (start us, length us, event | category | flops | bytes accessed | tf_op | source)
XLA Modules:
  0.0 332.2 jit_solution(10949312006875397529)
XLA Ops:
  13.5 25.7 %collective-permute-done.2.refs_4_ = bf16[2,3072,128]{2,1,0:T(8,128)(2,1)S(1)} collective-permute-done((bf16[2,3072,128]{2,1,0:T(8,128)(2,1)S(1)}, bf16[2,3072,128]{2,1,0:T(8,128)(2,1)S(1)}, u32[]{:S(2)}, u32[]{:S(2)}) %collective-permute-start.2) | collective-permute-done | bytes 1572896 | tf_op jit(solution)/shard_map/ppermute | solution.py:513
  43.1 4.7 %collective-permute-start.3 = (bf16[2,3072,128]{2,1,0:T(8,128)(2,1)}, bf16[2,3072,128]{2,1,0:T(8,128)(2,1)}, u32[]{:S(2)}, u32[]{:S(2)}) collective-permute-start(bf16[2,3072,128]{2,1,0:T(8,128)(2,1)} %slice_bitcast_fusion.1), channel_id=1, source_target_pairs={{3,2},{0,1},{7,6},{4,5},{11,10},{8,9},{15,14},{12,13},{19,18},{16,... | collective-permute-start | bytes 4718600 | tf_op jit(solution)/shard_map/ppermute | solution.py:513
  53.7 23.1 %collective-permute-done.refs_5_ = bf16[2,3072,128]{2,1,0:T(8,128)(2,1)S(1)} collective-permute-done((bf16[2,3072,128]{2,1,0:T(8,128)(2,1)}, bf16[2,3072,128]{2,1,0:T(8,128)(2,1)S(1)}, u32[]{:S(2)}, u32[]{:S(2)}) %collective-permute-start) | collective-permute-done | bytes 1572896 | tf_op jit(solution)/shard_map/ppermute | solution.py:513
  81.2 6.6 %collective-permute-start.4 = (bf16[2,3072,128]{2,1,0:T(8,128)(2,1)}, bf16[2,3072,128]{2,1,0:T(8,128)(2,1)S(1)}, u32[]{:S(2)}, u32[]{:S(2)}) collective-permute-start(bf16[2,3072,128]{2,1,0:T(8,128)(2,1)} %slice_bitcast_fusion), channel_id=1, source_target_pairs={{3,2},{0,1},{7,6},{4,5},{11,10},{8,9},{15,14},{12,13},{19,18},{16,... | collective-permute-start | bytes 4718600 | tf_op jit(solution)/shard_map/ppermute | solution.py:513
  89.5 21.1 %collective-permute-done.11.refs_4_ = bf16[2,3072,128]{2,1,0:T(8,128)(2,1)} collective-permute-done((bf16[2,3072,128]{2,1,0:T(8,128)(2,1)}, bf16[2,3072,128]{2,1,0:T(8,128)(2,1)}, u32[]{:S(2)}, u32[]{:S(2)}) %collective-permute-start.11) | collective-permute-done | bytes 1572896 | tf_op jit(solution)/shard_map/ppermute | solution.py:513
  116.2 8.9 %send_0_0.1 = bf16[2,1536,128]{2,1,0:T(8,128)(2,1)S(1)} custom-call(s32[33]{0:T(128)S(1)} %pad_add_fusion.refs_0_, f32[3,2]{1,0:T(4,128)S(1)} %copy.17.refs_1_, bf16[3,2,1536,3072]{3,2,1,0:T(8,128)(2,1)} %refs_2_.25, bf16[2,3072,128]{2,1,0:T(8,128)(2,1)} %collective-permute-done.9.refs_3_, bf16[2,3072,128]{2,1,0:T(8,128)(2,1)} %collective-permute-done.11.refs_4_, ...), custom_call_target="tpu_custom_call" | custom-call | flops 1415577600 | bytes 196608 | tf_op jit(solution)/shard_map/send_0_0/pallas_call | solution.py:318
  126.4 18.0 %collective-permute-done.6.refs_6_ = bf16[2,3072,128]{2,1,0:T(8,128)(2,1)} collective-permute-done((bf16[2,3072,128]{2,1,0:T(8,128)(2,1)S(1)}, bf16[2,3072,128]{2,1,0:T(8,128)(2,1)}, u32[]{:S(2)}, u32[]{:S(2)}) %collective-permute-start.6) | collective-permute-done | bytes 1572896 | tf_op jit(solution)/shard_map/ppermute | solution.py:513
  147.9 8.8 %send_0_1.1 = bf16[2,1536,128]{2,1,0:T(8,128)(2,1)} custom-call(s32[33]{0:T(128)S(1)} %pad_add_fusion.refs_0_, f32[3,2]{1,0:T(4,128)S(1)} %copy.17.refs_1_, bf16[3,2,1536,3072]{3,2,1,0:T(8,128)(2,1)} %refs_2_.25, bf16[2,3072,128]{2,1,0:T(8,128)(2,1)S(1)} %copy-done.14, bf16[2,3072,128]{2,1,0:T(8,128)(2,1)S(1)} %copy-done.8, ...), custom_call_target="tpu_custom_call" | custom-call | flops 1415577600 | bytes 196608 | tf_op jit(solution)/shard_map/send_0_1/pallas_call | solution.py:318
  162.3 8.7 %keep_0_0.1.refs_8_ = bf16[3,2,1536,256]{3,2,1,0:T(8,128)(2,1)} custom-call(s32[33]{0:T(128)S(1)} %pad_add_fusion.refs_0_, f32[3,2]{1,0:T(4,128)S(1)} %copy.17.refs_1_, bf16[3,2,1536,3072]{3,2,1,0:T(8,128)(2,1)} %refs_2_.25, bf16[2,3072,128]{2,1,0:T(8,128)(2,1)} %collective-permute-done.9.refs_3_, bf16[2,3072,128]{2,1,0:T(8,128)(2,1)} %collective-permute-done.11.refs_4_, ...), custom_call_target="tpu_custom_call" | custom-call | flops 1415577600 | bytes 196608 | tf_op jit(solution)/shard_map/keep_0_0/pallas_call | solution.py:318
  171.1 7.0 %collective-permute-done.12.refs_4_ = bf16[2,3072,128]{2,1,0:T(8,128)(2,1)} collective-permute-done((bf16[2,3072,128]{2,1,0:T(8,128)(2,1)}, bf16[2,3072,128]{2,1,0:T(8,128)(2,1)}, u32[]{:S(2)}, u32[]{:S(2)}) %collective-permute-start.12) | collective-permute-done | bytes 1572896 | tf_op jit(solution)/shard_map/ppermute | solution.py:513
  178.1 8.9 %send_1_0.1 = bf16[2,1536,128]{2,1,0:T(8,128)(2,1)S(1)} custom-call(s32[33]{0:T(128)S(1)} %pad_add_fusion.refs_0_, f32[3,2]{1,0:T(4,128)S(1)} %copy.17.refs_1_, bf16[3,2,1536,3072]{3,2,1,0:T(8,128)(2,1)} %refs_2_.25, bf16[2,3072,128]{2,1,0:T(8,128)(2,1)} %collective-permute-done.10.refs_3_, bf16[2,3072,128]{2,1,0:T(8,128)(2,1)} %collective-permute-done.12.refs_4_, ...), custom_call_target="tpu_custom_call" | custom-call | flops 1415577600 | bytes 196608 | tf_op jit(solution)/shard_map/send_1_0/pallas_call | solution.py:318
  189.9 10.4 %keep_0_1.1.refs_7_ = bf16[3,2,1536,256]{3,2,1,0:T(8,128)(2,1)} custom-call(s32[33]{0:T(128)S(1)} %pad_add_fusion.refs_0_, f32[3,2]{1,0:T(4,128)S(1)} %copy.17.refs_1_, bf16[3,2,1536,3072]{3,2,1,0:T(8,128)(2,1)} %refs_2_.25, bf16[2,3072,128]{2,1,0:T(8,128)(2,1)S(1)} %copy-done.15, ...), custom_call_target="tpu_custom_call", output_to_operand_aliasing={{}: (8, {})} | custom-call | flops 1415577600 | bytes 196608 | tf_op jit(solution)/shard_map/keep_0_1/pallas_call | solution.py:318
  200.3 11.5 %collective-permute-done.17.refs_4_ = bf16[2,3072,128]{2,1,0:T(8,128)(2,1)} collective-permute-done((bf16[2,3072,128]{2,1,0:T(8,128)(2,1)}, bf16[2,3072,128]{2,1,0:T(8,128)(2,1)}, u32[]{:S(2)}, u32[]{:S(2)}) %collective-permute-start.17) | collective-permute-done | bytes 1572896 | tf_op jit(solution)/shard_map/ppermute | solution.py:513
  213.3 8.6 %send_2_0.1 = bf16[2,1536,128]{2,1,0:T(8,128)(2,1)S(1)} custom-call(s32[33]{0:T(128)S(1)} %pad_add_fusion.refs_0_, f32[3,2]{1,0:T(4,128)S(1)} %copy.17.refs_1_, bf16[3,2,1536,3072]{3,2,1,0:T(8,128)(2,1)} %refs_2_.25, bf16[2,3072,128]{2,1,0:T(8,128)(2,1)} %collective-permute-done.7.refs_3_, bf16[2,3072,128]{2,1,0:T(8,128)(2,1)} %collective-permute-done.17.refs_4_, ...), custom_call_target="tpu_custom_call" | custom-call | flops 1415577600 | bytes 196608 | tf_op jit(solution)/shard_map/send_2_0/pallas_call | solution.py:318
  223.3 8.7 %keep_1_0.1.refs_7_ = bf16[3,2,1536,256]{3,2,1,0:T(8,128)(2,1)} custom-call(s32[33]{0:T(128)S(1)} %pad_add_fusion.refs_0_, f32[3,2]{1,0:T(4,128)S(1)} %copy.17.refs_1_, bf16[3,2,1536,3072]{3,2,1,0:T(8,128)(2,1)} %refs_2_.25, bf16[2,3072,128]{2,1,0:T(8,128)(2,1)} %collective-permute-done.10.refs_3_, ...), custom_call_target="tpu_custom_call", output_to_operand_aliasing={{}: (7, {})} | custom-call | flops 1415577600 | bytes 196608 | tf_op jit(solution)/shard_map/keep_1_0/pallas_call | solution.py:318
  232.0 13.4 %collective-permute-done.18.refs_6_ = bf16[2,3072,128]{2,1,0:T(8,128)(2,1)S(1)} collective-permute-done((bf16[2,3072,128]{2,1,0:T(8,128)(2,1)}, bf16[2,3072,128]{2,1,0:T(8,128)(2,1)S(1)}, u32[]{:S(2)}, u32[]{:S(2)}) %collective-permute-start.18) | collective-permute-done | bytes 1572896 | tf_op jit(solution)/shard_map/ppermute | solution.py:513
  248.0 8.4 %send_1_1.1 = bf16[2,1536,128]{2,1,0:T(8,128)(2,1)S(1)} custom-call(s32[33]{0:T(128)S(1)} %pad_add_fusion.refs_0_, f32[3,2]{1,0:T(4,128)S(1)} %copy.17.refs_1_, bf16[3,2,1536,3072]{3,2,1,0:T(8,128)(2,1)} %refs_2_.25, bf16[2,3072,128]{2,1,0:T(8,128)(2,1)} %collective-permute-done.15.refs_3_, bf16[2,3072,128]{2,1,0:T(8,128)(2,1)} %collective-permute-done.3.refs_4_, ...), custom_call_target="tpu_custom_call" | custom-call | flops 1415577600 | bytes 196608 | tf_op jit(solution)/shard_map/send_1_1/pallas_call | solution.py:318
  258.0 11.3 %keep_2_0.1 = (bf16[3,2,1536,256]{3,2,1,0:T(8,128)(2,1)}, f32[384,128]{1,0:T(8,128)S(1)}, bf16[384,128]{1,0:T(8,128)(2,1)S(1)}, bf16[384,128]{1,0:T(8,128)(2,1)}, bf16[384,128]{1,0:T(8,128)(2,1)}) custom-call(s32[33]{0:T(128)S(1)} %pad_add_fusion.refs_0_, f32[3,2]{1,0:T(4,128)S(1)} %copy.17.refs_1_, ...), custom_call_target="tpu_custom_call", output_to_operand_aliasing={{0}: (7, {})} | custom-call | flops 1415577600 | bytes 196608 | tf_op jit(solution)/shard_map/keep_2_0/pallas_call | solution.py:318
  269.3 9.8 %collective-permute-done.20.refs_5_ = bf16[2,3072,128]{2,1,0:T(8,128)(2,1)S(1)} collective-permute-done((bf16[2,3072,128]{2,1,0:T(8,128)(2,1)S(1)}, bf16[2,3072,128]{2,1,0:T(8,128)(2,1)S(1)}, u32[]{:S(2)}, u32[]{:S(2)}) %collective-permute-start.20) | collective-permute-done | bytes 1572896 | tf_op jit(solution)/shard_map/ppermute | solution.py:513
  279.1 8.4 %send_2_1.1 = bf16[2,1536,128]{2,1,0:T(8,128)(2,1)S(1)} custom-call(s32[33]{0:T(128)S(1)} %pad_add_fusion.refs_0_, f32[3,2]{1,0:T(4,128)S(1)} %copy.17.refs_1_, bf16[3,2,1536,3072]{3,2,1,0:T(8,128)(2,1)} %refs_2_.25, bf16[2,3072,128]{2,1,0:T(8,128)(2,1)S(1)} %collective-permute-done.8.refs_3_, bf16[2,3072,128]{2,1,0:T(8,128)(2,1)S(1)} %collective-permute-done.4.refs_4_, ...), custom_call_target="tpu_custom_call" | custom-call | flops 1415577600 | bytes 196608 | tf_op jit(solution)/shard_map/send_2_1/pallas_call | solution.py:318
  291.8 4.8 %collective-permute-start.28 = (bf16[384,128]{1,0:T(8,128)(2,1)S(1)}, bf16[384,128]{1,0:T(8,128)(2,1)S(1)}, u32[]{:S(2)}, u32[]{:S(2)}) collective-permute-start(bf16[384,128]{1,0:T(8,128)(2,1)S(1)} %get-tuple-element.93), channel_id=1, source_target_pairs={{0,8},{8,16},{16,24},{24,0},{1,9},{9,17},{17,25},{25,1},{2,10},{10... | collective-permute-start | bytes 294920 | tf_op jit(solution)/shard_map/ppermute | solution.py:487
  296.8 8.7 %keep_1_1.1.refs_6_.refs_9_ = bf16[3,2,1536,256]{3,2,1,0:T(8,128)(2,1)} custom-call(s32[33]{0:T(128)S(1)} %pad_add_fusion.refs_0_, f32[3,2]{1,0:T(4,128)S(1)} %copy.17.refs_1_, bf16[3,2,1536,3072]{3,2,1,0:T(8,128)(2,1)} %refs_2_.25, bf16[2,3072,128]{2,1,0:T(8,128)(2,1)} %collective-permute-done.15.refs_3_, ...), custom_call_target="tpu_custom_call", output_to_operand_aliasing={{}: (8, {})} | custom-call | flops 1415577600 | bytes 196608 | tf_op jit(solution)/shard_map/keep_1_1/pallas_call | solution.py:318
  308.1 7.9 %fold_2_1.1 = (f32[2,1536,128]{2,1,0:T(8,128)S(1)}, f32[1536,128]{1,0:T(8,128)S(1)}) custom-call(s32[33]{0:T(128)S(1)} %pad_add_fusion.refs_0_, f32[3,2]{1,0:T(4,128)S(1)} %copy.17.refs_1_, bf16[3,2,1536,3072]{3,2,1,0:T(8,128)(2,1)} %refs_2_.25, bf16[2,3072,128]{2,1,0:T(8,128)(2,1)S(1)} %collective-permute-done.8.refs_3_, ...), custom_call_target="tpu_custom_call" | custom-call | flops 884736000 | bytes 196608 | tf_op jit(solution)/shard_map/fold_2_1/pallas_call | solution.py:318
  316.0 6.1 %keep_2_1.1 = (bf16[3,2,1536,256]{3,2,1,0:T(8,128)(2,1)}, f32[384,128]{1,0:T(8,128)S(1)}, bf16[384,128]{1,0:T(8,128)(2,1)}, bf16[384,128]{1,0:T(8,128)(2,1)}, bf16[384,128]{1,0:T(8,128)(2,1)}) custom-call(s32[33]{0:T(128)S(1)} %pad_add_fusion.refs_0_, f32[3,2]{1,0:T(4,128)S(1)} %copy.17.refs_1_, ...), custom_call_target="tpu_custom_call", output_to_operand_aliasing={{0}: (9, {})} | custom-call | flops 530841600 | bytes 196608 | tf_op jit(solution)/shard_map/keep_2_1/pallas_call | solution.py:318
  (110 shorter events, 71.6 us)
Async XLA Ops:
  2.2 37.1 %collective-permute-start.2 = (bf16[2,3072,128]{2,1,0:T(8,128)(2,1)S(1)}, bf16[2,3072,128]{2,1,0:T(8,128)(2,1)S(1)}, u32[]{:S(2)}, u32[]{:S(2)}) collective-permute-start(bf16[2,3072,128]{2,1,0:T(8,128)(2,1)S(1)} %slice_bitcast_fusion.2), channel_id=1, source_target_pairs={{3,2},{0,1},{7,6},{4,5},{11,10},{8,9},{15,14},{12,13},{19,18},{16,... | collective-permute-start | bytes 4718600 | tf_op jit(solution)/shard_map/ppermute | solution.py:513
  6.3 36.8 %collective-permute-start.1 = (bf16[2,3072,128]{2,1,0:T(8,128)(2,1)S(1)}, bf16[2,3072,128]{2,1,0:T(8,128)(2,1)S(1)}, u32[]{:S(2)}, u32[]{:S(2)}) collective-permute-start(bf16[2,3072,128]{2,1,0:T(8,128)(2,1)S(1)} %slice_bitcast_fusion.2), channel_id=1, source_target_pairs={{1,0},{2,3},{5,4},{6,7},{9,8},{10,11},{13,12},{14,15},{17,16},{18,... | collective-permute-start | bytes 4718600 | tf_op jit(solution)/shard_map/ppermute | solution.py:513
  7.6 40.3 %collective-permute-start.9 = (bf16[2,3072,128]{2,1,0:T(8,128)(2,1)S(1)}, bf16[2,3072,128]{2,1,0:T(8,128)(2,1)}, u32[]{:S(2)}, u32[]{:S(2)}) collective-permute-start(bf16[2,3072,128]{2,1,0:T(8,128)(2,1)S(1)} %slice_bitcast_fusion.2), channel_id=1, source_target_pairs={{2,1},{1,2},{6,5},{5,6},{10,9},{9,10},{14,13},{13,14},{18,17},{17,... | collective-permute-start | bytes 4718600 | tf_op jit(solution)/shard_map/ppermute | solution.py:513
  12.1 64.8 %collective-permute-start = (bf16[2,3072,128]{2,1,0:T(8,128)(2,1)}, bf16[2,3072,128]{2,1,0:T(8,128)(2,1)S(1)}, u32[]{:S(2)}, u32[]{:S(2)}) collective-permute-start(bf16[2,3072,128]{2,1,0:T(8,128)(2,1)} %slice_bitcast_fusion.1), channel_id=1, source_target_pairs={{1,0},{2,3},{5,4},{6,7},{9,8},{10,11},{13,12},{14,15},{17,16},{18,... | collective-permute-start | bytes 4718600 | tf_op jit(solution)/shard_map/ppermute | solution.py:513
  39.2 38.8 %collective-permute-start.5 = (bf16[2,3072,128]{2,1,0:T(8,128)(2,1)S(1)}, bf16[2,3072,128]{2,1,0:T(8,128)(2,1)S(1)}, u32[]{:S(2)}, u32[]{:S(2)}) collective-permute-start(bf16[2,3072,128]{2,1,0:T(8,128)(2,1)S(1)} %collective-permute-done.2.refs_4_), channel_id=1, source_target_pairs={{2,1},{1,2},{6,5},{5,6},{10,9},{9,10},{14,13},{13,14},{18,17},{17,... | collective-permute-start | bytes 4718600 | tf_op jit(solution)/shard_map/ppermute | solution.py:513
  43.1 38.0 %collective-permute-start.3 = (bf16[2,3072,128]{2,1,0:T(8,128)(2,1)}, bf16[2,3072,128]{2,1,0:T(8,128)(2,1)}, u32[]{:S(2)}, u32[]{:S(2)}) collective-permute-start(bf16[2,3072,128]{2,1,0:T(8,128)(2,1)} %slice_bitcast_fusion.1), channel_id=1, source_target_pairs={{3,2},{0,1},{7,6},{4,5},{11,10},{8,9},{15,14},{12,13},{19,18},{16,... | collective-permute-start | bytes 4718600 | tf_op jit(solution)/shard_map/ppermute | solution.py:513
  47.9 62.8 %collective-permute-start.11 = (bf16[2,3072,128]{2,1,0:T(8,128)(2,1)}, bf16[2,3072,128]{2,1,0:T(8,128)(2,1)}, u32[]{:S(2)}, u32[]{:S(2)}) collective-permute-start(bf16[2,3072,128]{2,1,0:T(8,128)(2,1)} %collective-permute-done.9.refs_3_), channel_id=1, source_target_pairs={{1,0},{2,3},{5,4},{6,7},{9,8},{10,11},{13,12},{14,15},{17,16},{18,... | collective-permute-start | bytes 4718600 | tf_op jit(solution)/shard_map/ppermute | solution.py:513
  49.2 61.5 %collective-permute-start.10 = (bf16[2,3072,128]{2,1,0:T(8,128)(2,1)}, bf16[2,3072,128]{2,1,0:T(8,128)(2,1)}, u32[]{:S(2)}, u32[]{:S(2)}) collective-permute-start(bf16[2,3072,128]{2,1,0:T(8,128)(2,1)} %slice_bitcast_fusion.1), channel_id=1, source_target_pairs={{2,1},{1,2},{6,5},{5,6},{10,9},{9,10},{14,13},{13,14},{18,17},{17,... | collective-permute-start | bytes 4718600 | tf_op jit(solution)/shard_map/ppermute | solution.py:513
  78.1 47.1 %collective-permute-start.7 = (bf16[2,3072,128]{2,1,0:T(8,128)(2,1)}, bf16[2,3072,128]{2,1,0:T(8,128)(2,1)}, u32[]{:S(2)}, u32[]{:S(2)}) collective-permute-start(bf16[2,3072,128]{2,1,0:T(8,128)(2,1)} %slice_bitcast_fusion), channel_id=1, source_target_pairs={{2,1},{1,2},{6,5},{5,6},{10,9},{9,10},{14,13},{13,14},{18,17},{17,... | collective-permute-start | bytes 4718600 | tf_op jit(solution)/shard_map/ppermute | solution.py:513
  79.9 64.5 %collective-permute-start.6 = (bf16[2,3072,128]{2,1,0:T(8,128)(2,1)S(1)}, bf16[2,3072,128]{2,1,0:T(8,128)(2,1)}, u32[]{:S(2)}, u32[]{:S(2)}) collective-permute-start(bf16[2,3072,128]{2,1,0:T(8,128)(2,1)S(1)} %collective-permute-done.5.refs_3_), channel_id=1, source_target_pairs={{1,0},{2,3},{5,4},{6,7},{9,8},{10,11},{13,12},{14,15},{17,16},{18,... | collective-permute-start | bytes 4718600 | tf_op jit(solution)/shard_map/ppermute | solution.py:513
  81.2 64.5 %collective-permute-start.4 = (bf16[2,3072,128]{2,1,0:T(8,128)(2,1)}, bf16[2,3072,128]{2,1,0:T(8,128)(2,1)S(1)}, u32[]{:S(2)}, u32[]{:S(2)}) collective-permute-start(bf16[2,3072,128]{2,1,0:T(8,128)(2,1)} %slice_bitcast_fusion), channel_id=1, source_target_pairs={{3,2},{0,1},{7,6},{4,5},{11,10},{8,9},{15,14},{12,13},{19,18},{16,... | collective-permute-start | bytes 4718600 | tf_op jit(solution)/shard_map/ppermute | solution.py:513
  110.7 60.4 %collective-permute-start.15 = (bf16[2,3072,128]{2,1,0:T(8,128)(2,1)}, bf16[2,3072,128]{2,1,0:T(8,128)(2,1)}, u32[]{:S(2)}, u32[]{:S(2)}) collective-permute-start(bf16[2,3072,128]{2,1,0:T(8,128)(2,1)} %collective-permute-done.3.refs_4_), channel_id=1, source_target_pairs={{2,1},{1,2},{6,5},{5,6},{10,9},{9,10},{14,13},{13,14},{18,17},{17,... | collective-permute-start | bytes 4718600 | tf_op jit(solution)/shard_map/ppermute | solution.py:513
  112.5 65.6 %collective-permute-start.12 = (bf16[2,3072,128]{2,1,0:T(8,128)(2,1)}, bf16[2,3072,128]{2,1,0:T(8,128)(2,1)}, u32[]{:S(2)}, u32[]{:S(2)}) collective-permute-start(bf16[2,3072,128]{2,1,0:T(8,128)(2,1)} %collective-permute-done.10.refs_3_), channel_id=1, source_target_pairs={{1,0},{2,3},{5,4},{6,7},{9,8},{10,11},{13,12},{14,15},{17,16},{18,... | collective-permute-start | bytes 4718600 | tf_op jit(solution)/shard_map/ppermute | solution.py:513
  125.1 31.5 %collective-permute-start.16 = (bf16[2,1536,128]{2,1,0:T(8,128)(2,1)S(1)}, bf16[2,1536,128]{2,1,0:T(8,128)(2,1)S(1)}, u32[]{:S(2)}, u32[]{:S(2)}) collective-permute-start(bf16[2,1536,128]{2,1,0:T(8,128)(2,1)S(1)} %send_0_0.1), channel_id=1, source_target_pairs={{0,4},{4,0},{1,5},{5,1},{2,6},{6,2},{3,7},{7,3},{8,12},{12,8},{9,1... | collective-permute-start | bytes 2359304 | tf_op jit(solution)/shard_map/ppermute | solution.py:467
  144.4 67.4 %collective-permute-start.17 = (bf16[2,3072,128]{2,1,0:T(8,128)(2,1)}, bf16[2,3072,128]{2,1,0:T(8,128)(2,1)}, u32[]{:S(2)}, u32[]{:S(2)}) collective-permute-start(bf16[2,3072,128]{2,1,0:T(8,128)(2,1)} %collective-permute-done.7.refs_3_), channel_id=1, source_target_pairs={{1,0},{2,3},{5,4},{6,7},{9,8},{10,11},{13,12},{14,15},{17,16},{18,... | collective-permute-start | bytes 4718600 | tf_op jit(solution)/shard_map/ppermute | solution.py:513
  145.7 66.1 %collective-permute-start.8 = (bf16[2,3072,128]{2,1,0:T(8,128)(2,1)S(1)}, bf16[2,3072,128]{2,1,0:T(8,128)(2,1)S(1)}, u32[]{:S(2)}, u32[]{:S(2)}) collective-permute-start(bf16[2,3072,128]{2,1,0:T(8,128)(2,1)S(1)} %collective-permute-done.4.refs_4_), channel_id=1, source_target_pairs={{2,1},{1,2},{6,5},{5,6},{10,9},{9,10},{14,13},{13,14},{18,17},{17,... | collective-permute-start | bytes 4718600 | tf_op jit(solution)/shard_map/ppermute | solution.py:513
  157.5 32.3 %collective-permute-start.14 = (bf16[2,1536,128]{2,1,0:T(8,128)(2,1)}, bf16[2,1536,128]{2,1,0:T(8,128)(2,1)}, u32[]{:S(2)}, u32[]{:S(2)}) collective-permute-start(bf16[2,1536,128]{2,1,0:T(8,128)(2,1)} %send_0_1.1), channel_id=1, source_target_pairs={{0,4},{4,0},{1,5},{5,1},{2,6},{6,2},{3,7},{7,3},{8,12},{12,8},{9,1... | collective-permute-start | bytes 2359304 | tf_op jit(solution)/shard_map/ppermute | solution.py:467
  187.0 36.3 %collective-permute-start.13 = (bf16[2,1536,128]{2,1,0:T(8,128)(2,1)S(1)}, bf16[2,1536,128]{2,1,0:T(8,128)(2,1)S(1)}, u32[]{:S(2)}, u32[]{:S(2)}) collective-permute-start(bf16[2,1536,128]{2,1,0:T(8,128)(2,1)S(1)} %send_1_0.1), channel_id=1, source_target_pairs={{0,4},{4,0},{1,5},{5,1},{2,6},{6,2},{3,7},{7,3},{8,12},{12,8},{9,1... | collective-permute-start | bytes 2359304 | tf_op jit(solution)/shard_map/ppermute | solution.py:467
  188.5 56.8 %collective-permute-start.18 = (bf16[2,3072,128]{2,1,0:T(8,128)(2,1)}, bf16[2,3072,128]{2,1,0:T(8,128)(2,1)S(1)}, u32[]{:S(2)}, u32[]{:S(2)}) collective-permute-start(bf16[2,3072,128]{2,1,0:T(8,128)(2,1)} %collective-permute-done.15.refs_3_), channel_id=1, source_target_pairs={{1,0},{2,3},{5,4},{6,7},{9,8},{10,11},{13,12},{14,15},{17,16},{18,... | collective-permute-start | bytes 4718600 | tf_op jit(solution)/shard_map/ppermute | solution.py:513
  211.9 67.1 %collective-permute-start.20 = (bf16[2,3072,128]{2,1,0:T(8,128)(2,1)S(1)}, bf16[2,3072,128]{2,1,0:T(8,128)(2,1)S(1)}, u32[]{:S(2)}, u32[]{:S(2)}) collective-permute-start(bf16[2,3072,128]{2,1,0:T(8,128)(2,1)S(1)} %broadcast_select_fusion), channel_id=1, source_target_pairs={{1,0},{2,3},{5,4},{6,7},{9,8},{10,11},{13,12},{14,15},{17,16},{18,... | collective-permute-start | bytes 4718600 | tf_op jit(solution)/shard_map/ppermute | solution.py:513
  221.9 36.1 %collective-permute-start.19 = (bf16[2,1536,128]{2,1,0:T(8,128)(2,1)S(1)}, bf16[2,1536,128]{2,1,0:T(8,128)(2,1)S(1)}, u32[]{:S(2)}, u32[]{:S(2)}) collective-permute-start(bf16[2,1536,128]{2,1,0:T(8,128)(2,1)S(1)} %send_2_0.1), channel_id=1, source_target_pairs={{0,4},{4,0},{1,5},{5,1},{2,6},{6,2},{3,7},{7,3},{8,12},{12,8},{9,1... | collective-permute-start | bytes 2359304 | tf_op jit(solution)/shard_map/ppermute | solution.py:467
  246.7 58.8 %collective-permute-start.24 = (bf16[2,1920,128]{2,1,0:T(8,128)(2,1)S(1)}, bf16[2,1920,128]{2,1,0:T(8,128)(2,1)S(1)}, u32[]{:S(2)}, u32[]{:S(2)}) collective-permute-start(bf16[2,1920,128]{2,1,0:T(8,128)(2,1)S(1)} %slice_select_fusion), channel_id=1, source_target_pairs={{1,0},{2,3},{5,4},{6,7},{9,8},{10,11},{13,12},{14,15},{17,16},{18,... | collective-permute-start | bytes 2949128 | tf_op jit(solution)/shard_map/ppermute | solution.py:513
  256.4 40.1 %collective-permute-start.21 = (bf16[2,1536,128]{2,1,0:T(8,128)(2,1)S(1)}, bf16[2,1536,128]{2,1,0:T(8,128)(2,1)S(1)}, u32[]{:S(2)}, u32[]{:S(2)}) collective-permute-start(bf16[2,1536,128]{2,1,0:T(8,128)(2,1)S(1)} %send_1_1.1), channel_id=1, source_target_pairs={{0,4},{4,0},{1,5},{5,1},{2,6},{6,2},{3,7},{7,3},{8,12},{12,8},{9,1... | collective-permute-start | bytes 2359304 | tf_op jit(solution)/shard_map/ppermute | solution.py:467
  291.8 33.1 %collective-permute-start.28 = (bf16[384,128]{1,0:T(8,128)(2,1)S(1)}, bf16[384,128]{1,0:T(8,128)(2,1)S(1)}, u32[]{:S(2)}, u32[]{:S(2)}) collective-permute-start(bf16[384,128]{1,0:T(8,128)(2,1)S(1)} %get-tuple-element.93), channel_id=1, source_target_pairs={{0,8},{8,16},{16,24},{24,0},{1,9},{9,17},{17,25},{25,1},{2,10},{10... | collective-permute-start | bytes 294920 | tf_op jit(solution)/shard_map/ppermute | solution.py:487
  (29 other events, 601.5 us)

commit v3 on v2

--- a/solution.py
+++ b/solution.py
@@ -322,8 +322,8 @@
         out_specs=[ANY] * len(outs),
         scratch_shapes=scratch,
         input_output_aliases=aliases,
-        compiler_params=pltpu.CompilerParams(vmem_limit_bytes=30 * 2**20),
-        cost_estimate=pl.CostEstimate(flops=300 * rows * depth * n_parts, bytes_accessed=rows * width, transcendentals=0),
+        compiler_params=pltpu.CompilerParams(vmem_limit_bytes=48 * 2**20),
+        cost_estimate=pl.CostEstimate(flops=30 * rows * depth * n_parts, bytes_accessed=rows * width, transcendentals=0),
         name=cfg["name"],
     )(*operands)
 
@@ -364,11 +364,20 @@
 
     first_row = sorted(steps, key=lambda s: (s < half, s))
     second_row = sorted(steps, key=lambda s: (s != half, s))
+    def add_out(p, step):
+        moves = [hop(z, p, step) for z in range(1, half)]
+        inwards = [hop(z, p, step) for z in range(half + 1, n_col)]
+        if step == 1 and half == 2:
+            moves += inwards
+            joined.add(p)
+        add("out", f"o{p}s{step}", moves)
+
+    joined = set()
     for p, step in pairs[:-1]:
-        add("out", f"o{p}s{step}", [hop(z, p, step) for z in range(1, half)])
+        add_out(p, step)
     add_end(0)
     for p, step in pairs[-1:]:
-        add("out", f"o{p}s{step}", [hop(z, p, step) for z in range(1, half)])
+        add_out(p, step)
     for i in range(1, len(first_row)):
         add_end(i)
     pairs = [(p, step) for p in range(poles) for step in range(1, half + 1)]
@@ -377,7 +386,8 @@
         add("across", f"a{p}s{step}", [hop(half, p, step)])
     for p in range(poles):
         for step in steps:
-            add("in", f"i{p}s{step}", [hop(z, p, step) for z in range(half + 1, n_col)])
+            if step > 1 or p not in joined:
+                add("in", f"i{p}s{step}", [hop(z, p, step) for z in range(half + 1, n_col)])
     return lists, where, at
 
 
@@ -518,7 +528,6 @@
 
         launch("out", 0, [])
         launch("across", 0, [])
-        launch("in", 0, [])
         launch("out", 1, [])
         launch("across", 1, [])
         for t in range(final + 1):
@@ -527,7 +536,7 @@
             deps += [state["sent"][key] for key, at in sent_at.items() if at == t - 2]
             launch("out", t + 2, deps)
             launch("across", t + 2, landed("out", t) + landed("across", t))
-            launch("in", t + 1, landed("out", t) + landed("in", t))
+            launch("in", t, landed("out", t) + landed("in", t - 1))
             for kind in ("send", "keep"):
                 for call in queue[t]:
                     if call[1] == kind:

time: 334 us -> 328 us (0.982); the launches traced: 332 us -> 321 us
  waiting for transfers between devices: 137 us -> 173 us
  Pallas kernels: 114 us -> 81.1 us
  local copies, waits for them, and re-layouts: 19.9 us -> 12.2 us
  starting transfers between devices: 54.3 us -> 48.6 us
    pallas_call x13, Pallas kernels: 114 us -> 81.1 us  [slice_product(): pl.pallas_call(functools.partial(slice_kernel, cfg), out_shape=outs, in_s...]
    ppermute x19 -> x17, waiting for transfers between devices: 133 us -> 159 us  [launch(): moved.append(lax.ppermute(value, 'col', ways))]
    ppermute x6, waiting for transfers between devices: 0.02 us -> 8.81 us  [run(): state['sent'][p, i] = lax.ppermute(part, 'row', [(0, 1), (1, 0)])]
    unnamed x45 -> x29, local copies, waits for them, and re-layouts: 12.4 us -> 4.73 us
    ppermute x19 -> x17, starting transfers between devices: 37.5 us -> 31.3 us  [launch(): moved.append(lax.ppermute(value, 'col', ways))]
  transfers between devices with their start and end apart: 31 -> 29, of which waited for: 12 -> 14; matrix products, arithmetic and copies ran while one was open for 3% -> 3% of each run, Pallas kernels for 34% -> 25%
where the time goes in v3:
time: 328 us; the launch traced here: 321 us
  waiting for transfers between devices  173 us (53%)
  Pallas kernels  81.1 us (25%)
  starting transfers between devices  48.6 us (15%)
  local copies, waits for them, and re-layouts  12.2 us (4%)
  other arithmetic  5.76 us (2%)
    ppermute x17, waiting for transfers between devices, launch(): moved.append(lax.ppermute(value, 'col', ways))  159 us
    pallas_call x13, Pallas kernels, slice_product(): pl.pallas_call(functools.partial(slice_kernel, cfg), out_shape=outs, in_s...  81.1 us
    ppermute x17, starting transfers between devices, launch(): moved.append(lax.ppermute(value, 'col', ways))  31.3 us
    ppermute x6, starting transfers between devices, run(): total = total + lax.ppermute(shares[d], 'pole', ways).astype(jnp.float32)  9.45 us
    ppermute x6, waiting for transfers between devices, run(): state['sent'][p, i] = lax.ppermute(part, 'row', [(0, 1), (1, 0)])  8.81 us
    ppermute x6, starting transfers between devices, run(): state['sent'][p, i] = lax.ppermute(part, 'row', [(0, 1), (1, 0)])  7.79 us
    squeeze x3, local copies, waits for them, and re-layouts, body(): arrays['own', p] = rest[p]  6.82 us
  transfers between devices with their start and end apart: 29, of which 14 were waited for; matrix products, arithmetic and copies ran while one was open for 3% of the time, Pallas kernels for 25%

profile of v3, /device:TPU:1, one launch (start us, length us, event | category | flops | bytes accessed | tf_op | source)
XLA Modules:
  0.0 321.3 jit_solution(6476127469875770150)
XLA Ops:
  11.5 27.0 %collective-permute-done.refs_4_ = bf16[2,3072,128]{2,1,0:T(8,128)(2,1)S(1)} collective-permute-done((bf16[2,3072,128]{2,1,0:T(8,128)(2,1)S(1)}, bf16[2,3072,128]{2,1,0:T(8,128)(2,1)S(1)}, u32[]{:S(2)}, u32[]{:S(2)}) %collective-permute-start) | collective-permute-done | bytes 1572896 | tf_op jit(solution)/shard_map/ppermute | solution.py:523
  45.1 27.2 %collective-permute-done.3.refs_4_ = bf16[2,3072,128]{2,1,0:T(8,128)(2,1)} collective-permute-done((bf16[2,3072,128]{2,1,0:T(8,128)(2,1)}, bf16[2,3072,128]{2,1,0:T(8,128)(2,1)}, u32[]{:S(2)}, u32[]{:S(2)}) %collective-permute-start.3) | collective-permute-done | bytes 1572896 | tf_op jit(solution)/shard_map/ppermute | solution.py:523
  75.5 7.1 %collective-permute-start.1 = (bf16[2,3072,128]{2,1,0:T(8,128)(2,1)}, bf16[2,3072,128]{2,1,0:T(8,128)(2,1)S(1)}, u32[]{:S(2)}, u32[]{:S(2)}) collective-permute-start(bf16[2,3072,128]{2,1,0:T(8,128)(2,1)} %slice_bitcast_fusion), channel_id=1, source_target_pairs={{3,2},{0,1},{7,6},{4,5},{11,10},{8,9},{15,14},{12,13},{19,18},{16,... | collective-permute-start | bytes 4718600 | tf_op jit(solution)/shard_map/ppermute | solution.py:523
  84.3 21.7 %collective-permute-done.9.refs_4_ = bf16[2,3072,128]{2,1,0:T(8,128)(2,1)} collective-permute-done((bf16[2,3072,128]{2,1,0:T(8,128)(2,1)}, bf16[2,3072,128]{2,1,0:T(8,128)(2,1)}, u32[]{:S(2)}, u32[]{:S(2)}) %collective-permute-start.9) | collective-permute-done | bytes 1572896 | tf_op jit(solution)/shard_map/ppermute | solution.py:523
  109.2 6.3 %send_0_0.1 = bf16[2,1536,128]{2,1,0:T(8,128)(2,1)S(1)} custom-call(s32[33]{0:T(128)S(1)} %pad_add_fusion.refs_0_, f32[3,2]{1,0:T(4,128)S(1)} %copy.17.refs_1_, bf16[3,2,1536,3072]{3,2,1,0:T(8,128)(2,1)} %refs_2_.25, bf16[2,3072,128]{2,1,0:T(8,128)(2,1)} %collective-permute-done.7.refs_3_, bf16[2,3072,128]{2,1,0:T(8,128)(2,1)} %collective-permute-done.9.refs_4_, ...), custom_call_target="tpu_custom_call" | custom-call | flops 141557760 | bytes 196608 | tf_op jit(solution)/shard_map/send_0_0/pallas_call | solution.py:318
  117.0 22.7 %collective-permute-done.4.refs_5_ = bf16[2,3072,128]{2,1,0:T(8,128)(2,1)} collective-permute-done((bf16[2,3072,128]{2,1,0:T(8,128)(2,1)S(1)}, bf16[2,3072,128]{2,1,0:T(8,128)(2,1)}, u32[]{:S(2)}, u32[]{:S(2)}) %collective-permute-start.4) | collective-permute-done | bytes 1572896 | tf_op jit(solution)/shard_map/ppermute | solution.py:523
  143.2 6.4 %send_0_1.1 = bf16[2,1536,128]{2,1,0:T(8,128)(2,1)} custom-call(s32[33]{0:T(128)S(1)} %pad_add_fusion.refs_0_, f32[3,2]{1,0:T(4,128)S(1)} %copy.17.refs_1_, bf16[3,2,1536,3072]{3,2,1,0:T(8,128)(2,1)} %refs_2_.25, bf16[2,3072,128]{2,1,0:T(8,128)(2,1)S(1)} %copy-done.8, bf16[2,3072,128]{2,1,0:T(8,128)(2,1)S(1)} %copy-done.5, ...), custom_call_target="tpu_custom_call" | custom-call | flops 141557760 | bytes 196608 | tf_op jit(solution)/shard_map/send_0_1/pallas_call | solution.py:318
  152.8 6.5 %keep_0_0.1.refs_7_ = bf16[3,2,1536,256]{3,2,1,0:T(8,128)(2,1)} custom-call(s32[33]{0:T(128)S(1)} %pad_add_fusion.refs_0_, f32[3,2]{1,0:T(4,128)S(1)} %copy.17.refs_1_, bf16[3,2,1536,3072]{3,2,1,0:T(8,128)(2,1)} %refs_2_.25, bf16[2,3072,128]{2,1,0:T(8,128)(2,1)} %collective-permute-done.7.refs_3_, bf16[2,3072,128]{2,1,0:T(8,128)(2,1)} %collective-permute-done.9.refs_4_, ...), custom_call_target="tpu_custom_call" | custom-call | flops 141557760 | bytes 196608 | tf_op jit(solution)/shard_map/keep_0_0/pallas_call | solution.py:318
  159.3 14.1 %collective-permute-done.10.refs_4_ = bf16[2,3072,128]{2,1,0:T(8,128)(2,1)} collective-permute-done((bf16[2,3072,128]{2,1,0:T(8,128)(2,1)}, bf16[2,3072,128]{2,1,0:T(8,128)(2,1)}, u32[]{:S(2)}, u32[]{:S(2)}) %collective-permute-start.10) | collective-permute-done | bytes 1572896 | tf_op jit(solution)/shard_map/ppermute | solution.py:523
  174.7 6.3 %send_1_0.1 = bf16[2,1536,128]{2,1,0:T(8,128)(2,1)S(1)} custom-call(s32[33]{0:T(128)S(1)} %pad_add_fusion.refs_0_, f32[3,2]{1,0:T(4,128)S(1)} %copy.17.refs_1_, bf16[3,2,1536,3072]{3,2,1,0:T(8,128)(2,1)} %refs_2_.25, bf16[2,3072,128]{2,1,0:T(8,128)(2,1)} %collective-permute-done.8.refs_3_, bf16[2,3072,128]{2,1,0:T(8,128)(2,1)} %collective-permute-done.10.refs_4_, ...), custom_call_target="tpu_custom_call" | custom-call | flops 141557760 | bytes 196608 | tf_op jit(solution)/shard_map/send_1_0/pallas_call | solution.py:318
  181.1 6.3 %keep_0_1.1.refs_7_ = bf16[3,2,1536,256]{3,2,1,0:T(8,128)(2,1)} custom-call(s32[33]{0:T(128)S(1)} %pad_add_fusion.refs_0_, f32[3,2]{1,0:T(4,128)S(1)} %copy.17.refs_1_, bf16[3,2,1536,3072]{3,2,1,0:T(8,128)(2,1)} %refs_2_.25, bf16[2,3072,128]{2,1,0:T(8,128)(2,1)S(1)} %copy-done.9, ...), custom_call_target="tpu_custom_call", output_to_operand_aliasing={{}: (7, {})} | custom-call | flops 141557760 | bytes 196608 | tf_op jit(solution)/shard_map/keep_0_1/pallas_call | solution.py:318
  187.4 19.8 %collective-permute-done.15.refs_4_ = bf16[2,3072,128]{2,1,0:T(8,128)(2,1)} collective-permute-done((bf16[2,3072,128]{2,1,0:T(8,128)(2,1)}, bf16[2,3072,128]{2,1,0:T(8,128)(2,1)}, u32[]{:S(2)}, u32[]{:S(2)}) %collective-permute-start.15) | collective-permute-done | bytes 1572896 | tf_op jit(solution)/shard_map/ppermute | solution.py:523
  211.1 6.3 %send_2_0.1 = bf16[2,1536,128]{2,1,0:T(8,128)(2,1)S(1)} custom-call(s32[33]{0:T(128)S(1)} %pad_add_fusion.refs_0_, f32[3,2]{1,0:T(4,128)S(1)} %copy.17.refs_1_, bf16[3,2,1536,3072]{3,2,1,0:T(8,128)(2,1)} %refs_2_.25, bf16[2,3072,128]{2,1,0:T(8,128)(2,1)} %collective-permute-done.5.refs_3_, bf16[2,3072,128]{2,1,0:T(8,128)(2,1)} %collective-permute-done.15.refs_4_, ...), custom_call_target="tpu_custom_call" | custom-call | flops 141557760 | bytes 196608 | tf_op jit(solution)/shard_map/send_2_0/pallas_call | solution.py:318
  218.2 8.8 %collective-permute-done.11.refs_6_ = bf16[2,1536,128]{2,1,0:T(8,128)(2,1)S(1)} collective-permute-done((bf16[2,1536,128]{2,1,0:T(8,128)(2,1)S(1)}, bf16[2,1536,128]{2,1,0:T(8,128)(2,1)S(1)}, u32[]{:S(2)}, u32[]{:S(2)}) %collective-permute-start.11) | collective-permute-done | bytes 786464 | tf_op jit(solution)/shard_map/ppermute | solution.py:477
  227.0 6.5 %keep_1_0.1.refs_7_ = bf16[3,2,1536,256]{3,2,1,0:T(8,128)(2,1)} custom-call(s32[33]{0:T(128)S(1)} %pad_add_fusion.refs_0_, f32[3,2]{1,0:T(4,128)S(1)} %copy.17.refs_1_, bf16[3,2,1536,3072]{3,2,1,0:T(8,128)(2,1)} %refs_2_.25, bf16[2,3072,128]{2,1,0:T(8,128)(2,1)} %collective-permute-done.8.refs_3_, ...), custom_call_target="tpu_custom_call", output_to_operand_aliasing={{}: (7, {})} | custom-call | flops 141557760 | bytes 196608 | tf_op jit(solution)/shard_map/keep_1_0/pallas_call | solution.py:318
  233.5 7.2 %collective-permute-done.16.refs_5_ = bf16[2,3072,128]{2,1,0:T(8,128)(2,1)S(1)} collective-permute-done((bf16[2,3072,128]{2,1,0:T(8,128)(2,1)}, bf16[2,3072,128]{2,1,0:T(8,128)(2,1)S(1)}, u32[]{:S(2)}, u32[]{:S(2)}) %collective-permute-start.16) | collective-permute-done | bytes 1572896 | tf_op jit(solution)/shard_map/ppermute | solution.py:523
  243.3 6.0 %send_1_1.1 = bf16[2,1536,128]{2,1,0:T(8,128)(2,1)S(1)} custom-call(s32[33]{0:T(128)S(1)} %pad_add_fusion.refs_0_, f32[3,2]{1,0:T(4,128)S(1)} %copy.17.refs_1_, bf16[3,2,1536,3072]{3,2,1,0:T(8,128)(2,1)} %refs_2_.25, bf16[2,3072,128]{2,1,0:T(8,128)(2,1)} %collective-permute-done.13.refs_3_, bf16[2,3072,128]{2,1,0:T(8,128)(2,1)} %collective-permute-done.3.refs_4_, ...), custom_call_target="tpu_custom_call" | custom-call | flops 141557760 | bytes 196608 | tf_op jit(solution)/shard_map/send_1_1/pallas_call | solution.py:318
  251.2 7.0 %keep_2_0.1 = (bf16[3,2,1536,256]{3,2,1,0:T(8,128)(2,1)}, f32[384,128]{1,0:T(8,128)S(1)}, bf16[384,128]{1,0:T(8,128)(2,1)S(1)}, bf16[384,128]{1,0:T(8,128)(2,1)S(1)}, bf16[384,128]{1,0:T(8,128)(2,1)S(1)}) custom-call(s32[33]{0:T(128)S(1)} %pad_add_fusion.refs_0_, f32[3,2]{1,0:T(4,128)S(1)} %copy.17.refs_1_, ...), custom_call_target="tpu_custom_call", output_to_operand_aliasing={{0}: (7, {})} | custom-call | flops 141557760 | bytes 196608 | tf_op jit(solution)/shard_map/keep_2_0/pallas_call | solution.py:318
  258.2 16.3 %collective-permute-done.18.refs_5_ = bf16[2,3072,128]{2,1,0:T(8,128)(2,1)S(1)} collective-permute-done((bf16[2,3072,128]{2,1,0:T(8,128)(2,1)}, bf16[2,3072,128]{2,1,0:T(8,128)(2,1)S(1)}, u32[]{:S(2)}, u32[]{:S(2)}) %collective-permute-start.18) | collective-permute-done | bytes 1572896 | tf_op jit(solution)/shard_map/ppermute | solution.py:523
  274.4 6.0 %send_2_1.1 = bf16[2,1536,128]{2,1,0:T(8,128)(2,1)S(1)} custom-call(s32[33]{0:T(128)S(1)} %pad_add_fusion.refs_0_, f32[3,2]{1,0:T(4,128)S(1)} %copy.17.refs_1_, bf16[3,2,1536,3072]{3,2,1,0:T(8,128)(2,1)} %refs_2_.25, bf16[2,3072,128]{2,1,0:T(8,128)(2,1)S(1)} %collective-permute-done.6.refs_3_, bf16[2,3072,128]{2,1,0:T(8,128)(2,1)S(1)} %collective-permute-done.1.refs_4_, ...), custom_call_target="tpu_custom_call" | custom-call | flops 141557760 | bytes 196608 | tf_op jit(solution)/shard_map/send_2_1/pallas_call | solution.py:318
  284.4 4.1 %collective-permute-start.26 = (bf16[384,128]{1,0:T(8,128)(2,1)S(1)}, bf16[384,128]{1,0:T(8,128)(2,1)S(1)}, u32[]{:S(2)}, u32[]{:S(2)}) collective-permute-start(bf16[384,128]{1,0:T(8,128)(2,1)S(1)} %get-tuple-element.91), channel_id=1, source_target_pairs={{0,8},{8,16},{16,24},{24,0},{1,9},{9,17},{17,25},{25,1},{2,10},{10... | collective-permute-start | bytes 294920 | tf_op jit(solution)/shard_map/ppermute | solution.py:497
  288.7 6.5 %keep_1_1.1.refs_6_.refs_9_ = bf16[3,2,1536,256]{3,2,1,0:T(8,128)(2,1)} custom-call(s32[33]{0:T(128)S(1)} %pad_add_fusion.refs_0_, f32[3,2]{1,0:T(4,128)S(1)} %copy.17.refs_1_, bf16[3,2,1536,3072]{3,2,1,0:T(8,128)(2,1)} %refs_2_.25, bf16[2,3072,128]{2,1,0:T(8,128)(2,1)} %collective-permute-done.13.refs_3_, ...), custom_call_target="tpu_custom_call", output_to_operand_aliasing={{}: (7, {})} | custom-call | flops 141557760 | bytes 196608 | tf_op jit(solution)/shard_map/keep_1_1/pallas_call | solution.py:318
  297.5 6.5 %fold_2_1.1 = (f32[2,1536,128]{2,1,0:T(8,128)S(1)}, f32[1536,128]{1,0:T(8,128)S(1)}) custom-call(s32[33]{0:T(128)S(1)} %pad_add_fusion.refs_0_, f32[3,2]{1,0:T(4,128)S(1)} %copy.17.refs_1_, bf16[3,2,1536,3072]{3,2,1,0:T(8,128)(2,1)} %refs_2_.25, bf16[2,3072,128]{2,1,0:T(8,128)(2,1)S(1)} %collective-permute-done.6.refs_3_, bf16[2,3072,128]{2,1,0:T(8,128)(2,1)} %copy-done.2, ...), custom_call_target="tpu_custom_call" | custom-call | flops 88473600 | bytes 196608 | tf_op jit(solution)/shard_map/fold_2_1/pallas_call | solution.py:318
  308.1 4.5 %keep_2_1.1 = (bf16[3,2,1536,256]{3,2,1,0:T(8,128)(2,1)}, f32[384,128]{1,0:T(8,128)S(1)}, bf16[384,128]{1,0:T(8,128)(2,1)S(1)}, bf16[384,128]{1,0:T(8,128)(2,1)S(1)}, bf16[384,128]{1,0:T(8,128)(2,1)S(1)}) custom-call(s32[33]{0:T(128)S(1)} %pad_add_fusion.refs_0_, f32[3,2]{1,0:T(4,128)S(1)} %copy.17.refs_1_, ...), custom_call_target="tpu_custom_call", output_to_operand_aliasing={{0}: (9, {})} | custom-call | flops 53084160 | bytes 196608 | tf_op jit(solution)/shard_map/keep_2_1/pallas_call | solution.py:318
  (89 shorter events, 63.3 us)
Async XLA Ops:
  2.2 36.3 %collective-permute-start = (bf16[2,3072,128]{2,1,0:T(8,128)(2,1)S(1)}, bf16[2,3072,128]{2,1,0:T(8,128)(2,1)S(1)}, u32[]{:S(2)}, u32[]{:S(2)}) collective-permute-start(bf16[2,3072,128]{2,1,0:T(8,128)(2,1)S(1)} %slice_bitcast_fusion.2), channel_id=1, source_target_pairs={{1,0},{3,2},{2,3},{0,1},{5,4},{7,6},{6,7},{4,5},{9,8},{11,10},{10,... | collective-permute-start | bytes 4718600 | tf_op jit(solution)/shard_map/ppermute | solution.py:523
  4.4 34.9 %collective-permute-start.7 = (bf16[2,3072,128]{2,1,0:T(8,128)(2,1)S(1)}, bf16[2,3072,128]{2,1,0:T(8,128)(2,1)}, u32[]{:S(2)}, u32[]{:S(2)}) collective-permute-start(bf16[2,3072,128]{2,1,0:T(8,128)(2,1)S(1)} %slice_bitcast_fusion.2), channel_id=1, source_target_pairs={{2,1},{1,2},{6,5},{5,6},{10,9},{9,10},{14,13},{13,14},{18,17},{17,... | collective-permute-start | bytes 4718600 | tf_op jit(solution)/shard_map/ppermute | solution.py:523
  8.9 63.4 %collective-permute-start.3 = (bf16[2,3072,128]{2,1,0:T(8,128)(2,1)}, bf16[2,3072,128]{2,1,0:T(8,128)(2,1)}, u32[]{:S(2)}, u32[]{:S(2)}) collective-permute-start(bf16[2,3072,128]{2,1,0:T(8,128)(2,1)} %slice_bitcast_fusion.1), channel_id=1, source_target_pairs={{1,0},{3,2},{2,3},{0,1},{5,4},{7,6},{6,7},{4,5},{9,8},{11,10},{10,... | collective-permute-start | bytes 4718600 | tf_op jit(solution)/shard_map/ppermute | solution.py:523
  38.5 33.8 %collective-permute-start.2 = (bf16[2,3072,128]{2,1,0:T(8,128)(2,1)S(1)}, bf16[2,3072,128]{2,1,0:T(8,128)(2,1)S(1)}, u32[]{:S(2)}, u32[]{:S(2)}) collective-permute-start(bf16[2,3072,128]{2,1,0:T(8,128)(2,1)S(1)} %collective-permute-done.refs_4_), channel_id=1, source_target_pairs={{2,1},{1,2},{6,5},{5,6},{10,9},{9,10},{14,13},{13,14},{18,17},{17,... | collective-permute-start | bytes 4718600 | tf_op jit(solution)/shard_map/ppermute | solution.py:523
  39.2 66.7 %collective-permute-start.9 = (bf16[2,3072,128]{2,1,0:T(8,128)(2,1)}, bf16[2,3072,128]{2,1,0:T(8,128)(2,1)}, u32[]{:S(2)}, u32[]{:S(2)}) collective-permute-start(bf16[2,3072,128]{2,1,0:T(8,128)(2,1)} %collective-permute-done.7.refs_3_), channel_id=1, source_target_pairs={{1,0},{2,3},{5,4},{6,7},{9,8},{10,11},{13,12},{14,15},{17,16},{18,... | collective-permute-start | bytes 4718600 | tf_op jit(solution)/shard_map/ppermute | solution.py:523
  40.5 65.4 %collective-permute-start.8 = (bf16[2,3072,128]{2,1,0:T(8,128)(2,1)}, bf16[2,3072,128]{2,1,0:T(8,128)(2,1)}, u32[]{:S(2)}, u32[]{:S(2)}) collective-permute-start(bf16[2,3072,128]{2,1,0:T(8,128)(2,1)} %slice_bitcast_fusion.1), channel_id=1, source_target_pairs={{2,1},{1,2},{6,5},{5,6},{10,9},{9,10},{14,13},{13,14},{18,17},{17,... | collective-permute-start | bytes 4718600 | tf_op jit(solution)/shard_map/ppermute | solution.py:523
  72.3 43.3 %collective-permute-start.5 = (bf16[2,3072,128]{2,1,0:T(8,128)(2,1)}, bf16[2,3072,128]{2,1,0:T(8,128)(2,1)}, u32[]{:S(2)}, u32[]{:S(2)}) collective-permute-start(bf16[2,3072,128]{2,1,0:T(8,128)(2,1)} %slice_bitcast_fusion), channel_id=1, source_target_pairs={{2,1},{1,2},{6,5},{5,6},{10,9},{9,10},{14,13},{13,14},{18,17},{17,... | collective-permute-start | bytes 4718600 | tf_op jit(solution)/shard_map/ppermute | solution.py:523
  74.2 65.5 %collective-permute-start.4 = (bf16[2,3072,128]{2,1,0:T(8,128)(2,1)S(1)}, bf16[2,3072,128]{2,1,0:T(8,128)(2,1)}, u32[]{:S(2)}, u32[]{:S(2)}) collective-permute-start(bf16[2,3072,128]{2,1,0:T(8,128)(2,1)S(1)} %collective-permute-done.2.refs_3_), channel_id=1, source_target_pairs={{1,0},{2,3},{5,4},{6,7},{9,8},{10,11},{13,12},{14,15},{17,16},{18,... | collective-permute-start | bytes 4718600 | tf_op jit(solution)/shard_map/ppermute | solution.py:523
  75.5 65.5 %collective-permute-start.1 = (bf16[2,3072,128]{2,1,0:T(8,128)(2,1)}, bf16[2,3072,128]{2,1,0:T(8,128)(2,1)S(1)}, u32[]{:S(2)}, u32[]{:S(2)}) collective-permute-start(bf16[2,3072,128]{2,1,0:T(8,128)(2,1)} %slice_bitcast_fusion), channel_id=1, source_target_pairs={{3,2},{0,1},{7,6},{4,5},{11,10},{8,9},{15,14},{12,13},{19,18},{16,... | collective-permute-start | bytes 4718600 | tf_op jit(solution)/shard_map/ppermute | solution.py:523
  106.0 53.3 %collective-permute-start.13 = (bf16[2,3072,128]{2,1,0:T(8,128)(2,1)}, bf16[2,3072,128]{2,1,0:T(8,128)(2,1)}, u32[]{:S(2)}, u32[]{:S(2)}) collective-permute-start(bf16[2,3072,128]{2,1,0:T(8,128)(2,1)} %collective-permute-done.3.refs_4_), channel_id=1, source_target_pairs={{2,1},{1,2},{6,5},{5,6},{10,9},{9,10},{14,13},{13,14},{18,17},{17,... | collective-permute-start | bytes 4718600 | tf_op jit(solution)/shard_map/ppermute | solution.py:523
  107.8 65.6 %collective-permute-start.10 = (bf16[2,3072,128]{2,1,0:T(8,128)(2,1)}, bf16[2,3072,128]{2,1,0:T(8,128)(2,1)}, u32[]{:S(2)}, u32[]{:S(2)}) collective-permute-start(bf16[2,3072,128]{2,1,0:T(8,128)(2,1)} %collective-permute-done.8.refs_3_), channel_id=1, source_target_pairs={{1,0},{2,3},{5,4},{6,7},{9,8},{10,11},{13,12},{14,15},{17,16},{18,... | collective-permute-start | bytes 4718600 | tf_op jit(solution)/shard_map/ppermute | solution.py:523
  115.6 34.0 %collective-permute-start.14 = (bf16[2,1536,128]{2,1,0:T(8,128)(2,1)S(1)}, bf16[2,1536,128]{2,1,0:T(8,128)(2,1)S(1)}, u32[]{:S(2)}, u32[]{:S(2)}) collective-permute-start(bf16[2,1536,128]{2,1,0:T(8,128)(2,1)S(1)} %send_0_0.1), channel_id=1, source_target_pairs={{0,4},{4,0},{1,5},{5,1},{2,6},{6,2},{3,7},{7,3},{8,12},{12,8},{9,1... | collective-permute-start | bytes 2359304 | tf_op jit(solution)/shard_map/ppermute | solution.py:477
  139.7 67.4 %collective-permute-start.15 = (bf16[2,3072,128]{2,1,0:T(8,128)(2,1)}, bf16[2,3072,128]{2,1,0:T(8,128)(2,1)}, u32[]{:S(2)}, u32[]{:S(2)}) collective-permute-start(bf16[2,3072,128]{2,1,0:T(8,128)(2,1)} %collective-permute-done.5.refs_3_), channel_id=1, source_target_pairs={{1,0},{2,3},{5,4},{6,7},{9,8},{10,11},{13,12},{14,15},{17,16},{18,... | collective-permute-start | bytes 4718600 | tf_op jit(solution)/shard_map/ppermute | solution.py:523
  141.0 66.1 %collective-permute-start.6 = (bf16[2,3072,128]{2,1,0:T(8,128)(2,1)S(1)}, bf16[2,3072,128]{2,1,0:T(8,128)(2,1)S(1)}, u32[]{:S(2)}, u32[]{:S(2)}) collective-permute-start(bf16[2,3072,128]{2,1,0:T(8,128)(2,1)S(1)} %collective-permute-done.1.refs_4_), channel_id=1, source_target_pairs={{2,1},{1,2},{6,5},{5,6},{10,9},{9,10},{14,13},{13,14},{18,17},{17,... | collective-permute-start | bytes 4718600 | tf_op jit(solution)/shard_map/ppermute | solution.py:523
  150.5 30.6 %collective-permute-start.12 = (bf16[2,1536,128]{2,1,0:T(8,128)(2,1)}, bf16[2,1536,128]{2,1,0:T(8,128)(2,1)}, u32[]{:S(2)}, u32[]{:S(2)}) collective-permute-start(bf16[2,1536,128]{2,1,0:T(8,128)(2,1)} %send_0_1.1), channel_id=1, source_target_pairs={{0,4},{4,0},{1,5},{5,1},{2,6},{6,2},{3,7},{7,3},{8,12},{12,8},{9,1... | collective-permute-start | bytes 2359304 | tf_op jit(solution)/shard_map/ppermute | solution.py:477
  173.4 67.3 %collective-permute-start.16 = (bf16[2,3072,128]{2,1,0:T(8,128)(2,1)}, bf16[2,3072,128]{2,1,0:T(8,128)(2,1)S(1)}, u32[]{:S(2)}, u32[]{:S(2)}) collective-permute-start(bf16[2,3072,128]{2,1,0:T(8,128)(2,1)} %collective-permute-done.13.refs_3_), channel_id=1, source_target_pairs={{1,0},{2,3},{5,4},{6,7},{9,8},{10,11},{13,12},{14,15},{17,16},{18,... | collective-permute-start | bytes 4718600 | tf_op jit(solution)/shard_map/ppermute | solution.py:523
  208.5 65.9 %collective-permute-start.18 = (bf16[2,3072,128]{2,1,0:T(8,128)(2,1)}, bf16[2,3072,128]{2,1,0:T(8,128)(2,1)S(1)}, u32[]{:S(2)}, u32[]{:S(2)}) collective-permute-start(bf16[2,3072,128]{2,1,0:T(8,128)(2,1)} %broadcast_select_fusion), channel_id=1, source_target_pairs={{1,0},{2,3},{5,4},{6,7},{9,8},{10,11},{13,12},{14,15},{17,16},{18,... | collective-permute-start | bytes 4718600 | tf_op jit(solution)/shard_map/ppermute | solution.py:523
  217.4 33.7 %collective-permute-start.17 = (bf16[2,1536,128]{2,1,0:T(8,128)(2,1)S(1)}, bf16[2,1536,128]{2,1,0:T(8,128)(2,1)S(1)}, u32[]{:S(2)}, u32[]{:S(2)}) collective-permute-start(bf16[2,1536,128]{2,1,0:T(8,128)(2,1)S(1)} %send_2_0.1), channel_id=1, source_target_pairs={{0,4},{4,0},{1,5},{5,1},{2,6},{6,2},{3,7},{7,3},{8,12},{12,8},{9,1... | collective-permute-start | bytes 2359304 | tf_op jit(solution)/shard_map/ppermute | solution.py:477
  242.0 53.4 %collective-permute-start.22 = (bf16[2,1920,128]{2,1,0:T(8,128)(2,1)S(1)}, bf16[2,1920,128]{2,1,0:T(8,128)(2,1)S(1)}, u32[]{:S(2)}, u32[]{:S(2)}) collective-permute-start(bf16[2,1920,128]{2,1,0:T(8,128)(2,1)S(1)} %slice_select_fusion), channel_id=1, source_target_pairs={{1,0},{2,3},{5,4},{6,7},{9,8},{10,11},{13,12},{14,15},{17,16},{18,... | collective-permute-start | bytes 2949128 | tf_op jit(solution)/shard_map/ppermute | solution.py:523
  249.4 39.1 %collective-permute-start.19 = (bf16[2,1536,128]{2,1,0:T(8,128)(2,1)S(1)}, bf16[2,1536,128]{2,1,0:T(8,128)(2,1)S(1)}, u32[]{:S(2)}, u32[]{:S(2)}) collective-permute-start(bf16[2,1536,128]{2,1,0:T(8,128)(2,1)S(1)} %send_1_1.1), channel_id=1, source_target_pairs={{0,4},{4,0},{1,5},{5,1},{2,6},{6,2},{3,7},{7,3},{8,12},{12,8},{9,1... | collective-permute-start | bytes 2359304 | tf_op jit(solution)/shard_map/ppermute | solution.py:477
  280.5 27.7 %collective-permute-start.21 = (bf16[2,1536,128]{2,1,0:T(8,128)(2,1)S(1)}, bf16[2,1536,128]{2,1,0:T(8,128)(2,1)S(1)}, u32[]{:S(2)}, u32[]{:S(2)}) collective-permute-start(bf16[2,1536,128]{2,1,0:T(8,128)(2,1)S(1)} %send_2_1.1), channel_id=1, source_target_pairs={{0,4},{4,0},{1,5},{5,1},{2,6},{6,2},{3,7},{7,3},{8,12},{12,8},{9,1... | collective-permute-start | bytes 2359304 | tf_op jit(solution)/shard_map/ppermute | solution.py:477
  283.1 25.1 %collective-permute-start.20 = (bf16[2,1152,128]{2,1,0:T(8,128)(2,1)S(1)}, bf16[2,1152,128]{2,1,0:T(8,128)(2,1)S(1)}, u32[]{:S(2)}, u32[]{:S(2)}) collective-permute-start(bf16[2,1152,128]{2,1,0:T(8,128)(2,1)S(1)} %slice_select_fusion.1), channel_id=1, source_target_pairs={{1,0},{2,3},{5,4},{6,7},{9,8},{10,11},{13,12},{14,15},{17,16},{18,... | collective-permute-start | bytes 1769480 | tf_op jit(solution)/shard_map/ppermute | solution.py:523
  284.4 30.9 %collective-permute-start.26 = (bf16[384,128]{1,0:T(8,128)(2,1)S(1)}, bf16[384,128]{1,0:T(8,128)(2,1)S(1)}, u32[]{:S(2)}, u32[]{:S(2)}) collective-permute-start(bf16[384,128]{1,0:T(8,128)(2,1)S(1)} %get-tuple-element.91), channel_id=1, source_target_pairs={{0,8},{8,16},{16,24},{24,0},{1,9},{9,17},{17,25},{25,1},{2,10},{10... | collective-permute-start | bytes 294920 | tf_op jit(solution)/shard_map/ppermute | solution.py:497
  288.5 27.1 %collective-permute-start.27 = (bf16[384,128]{1,0:T(8,128)(2,1)S(1)}, bf16[384,128]{1,0:T(8,128)(2,1)S(1)}, u32[]{:S(2)}, u32[]{:S(2)}) collective-permute-start(bf16[384,128]{1,0:T(8,128)(2,1)S(1)} %get-tuple-element.92), channel_id=1, source_target_pairs={{0,16},{8,24},{16,0},{24,8},{1,17},{9,25},{17,1},{25,9},{2,18},{10... | collective-permute-start | bytes 294920 | tf_op jit(solution)/shard_map/ppermute | solution.py:497
  (19 other events, 523.5 us)

commit v4 on v3

--- a/solution.py
+++ b/solution.py
@@ -520,7 +520,8 @@
                 value = values[0][:, piece]
                 for other, (_, spots) in zip(values[1:], held[1:]):
                     value = jnp.where(is_one_of(spots), other[:, piece], value)
-                moved.append(lax.ppermute(value, "col", ways))
+                moved.append(value)
+            moved = [lax.ppermute(value, "col", ways) for value in lax.optimization_barrier(moved)]
             arrays[name] = moved if len(moved) > 1 else moved[0]
 
         def landed(kind, t):

time: 328 us -> 327 us (level)
  waiting for transfers between devices: 173 us -> 151 us
  Pallas kernels: 81.1 us -> 96.9 us
  starting transfers between devices: 48.6 us -> 55.3 us
    pallas_call x13, Pallas kernels: 81.1 us -> 96.9 us  [slice_product(): pl.pallas_call(functools.partial(slice_kernel, cfg), out_shape=outs, in_s...]
    ppermute x17, waiting for transfers between devices: 159 us -> 146 us  [launch(): lax.ppermute(value, 'col', ways)]
    ppermute x6, waiting for transfers between devices: 8.81 us -> 0.02 us  [run(): state['sent'][p, i] = lax.ppermute(part, 'row', [(0, 1), (1, 0)])]
    ppermute x6, starting transfers between devices: 7.79 us -> 14.9 us  [run(): state['sent'][p, i] = lax.ppermute(part, 'row', [(0, 1), (1, 0)])]
  transfers between devices with their start and end apart: 29 -> 29, of which waited for: 14 -> 12; matrix products, arithmetic and copies ran while one was open for 3% -> 3% of each run, Pallas kernels for 25% -> 30%
where the time goes in v4:
time: 327 us; the launch traced here: 322 us
  waiting for transfers between devices  151 us (46%)
  Pallas kernels  96.9 us (30%)
  starting transfers between devices  55.3 us (17%)
  local copies, waits for them, and re-layouts  12.8 us (4%)
  other arithmetic  5.7 us (2%)
    ppermute x17, waiting for transfers between devices, launch(): lax.ppermute(value, 'col', ways)  146 us
    pallas_call x13, Pallas kernels, slice_product(): pl.pallas_call(functools.partial(slice_kernel, cfg), out_shape=outs, in_s...  96.9 us
    ppermute x17, starting transfers between devices, launch(): lax.ppermute(value, 'col', ways)  31.4 us
    ppermute x6, starting transfers between devices, run(): state['sent'][p, i] = lax.ppermute(part, 'row', [(0, 1), (1, 0)])  14.9 us
    ppermute x6, starting transfers between devices, run(): total = total + lax.ppermute(shares[d], 'pole', ways).astype(jnp.float32)  8.92 us
    squeeze x3, local copies, waits for them, and re-layouts, body(): arrays['own', p] = rest[p]  6.83 us
  transfers between devices with their start and end apart: 29, of which 12 were waited for; matrix products, arithmetic and copies ran while one was open for 3% of the time, Pallas kernels for 30%

profile of v4, /device:TPU:1, one launch (start us, length us, event | category | flops | bytes accessed | tf_op | source)
XLA Modules:
  0.0 322.2 jit_solution(18086209577719321281)
XLA Ops:
  11.5 27.0 %collective-permute-done.refs_4_ = bf16[2,3072,128]{2,1,0:T(8,128)(2,1)S(1)} collective-permute-done((bf16[2,3072,128]{2,1,0:T(8,128)(2,1)S(1)}, bf16[2,3072,128]{2,1,0:T(8,128)(2,1)S(1)}, u32[]{:S(2)}, u32[]{:S(2)}) %collective-permute-start) | collective-permute-done | bytes 1572896 | tf_op jit(solution)/shard_map/ppermute | solution.py:524
  45.1 27.2 %collective-permute-done.3.refs_4_ = bf16[2,3072,128]{2,1,0:T(8,128)(2,1)} collective-permute-done((bf16[2,3072,128]{2,1,0:T(8,128)(2,1)}, bf16[2,3072,128]{2,1,0:T(8,128)(2,1)}, u32[]{:S(2)}, u32[]{:S(2)}) %collective-permute-start.3) | collective-permute-done | bytes 1572896 | tf_op jit(solution)/shard_map/ppermute | solution.py:524
  75.5 7.1 %collective-permute-start.1 = (bf16[2,3072,128]{2,1,0:T(8,128)(2,1)}, bf16[2,3072,128]{2,1,0:T(8,128)(2,1)S(1)}, u32[]{:S(2)}, u32[]{:S(2)}) collective-permute-start(bf16[2,3072,128]{2,1,0:T(8,128)(2,1)} %slice_bitcast_fusion), channel_id=1, source_target_pairs={{3,2},{0,1},{7,6},{4,5},{11,10},{8,9},{15,14},{12,13},{19,18},{16,... | collective-permute-start | bytes 4718600 | tf_op jit(solution)/shard_map/ppermute | solution.py:524
  83.6 22.4 %collective-permute-done.9.refs_4_ = bf16[2,3072,128]{2,1,0:T(8,128)(2,1)} collective-permute-done((bf16[2,3072,128]{2,1,0:T(8,128)(2,1)}, bf16[2,3072,128]{2,1,0:T(8,128)(2,1)}, u32[]{:S(2)}, u32[]{:S(2)}) %collective-permute-start.9) | collective-permute-done | bytes 1572896 | tf_op jit(solution)/shard_map/ppermute | solution.py:524
  109.9 7.1 %send_0_0.1 = bf16[2,1536,128]{2,1,0:T(8,128)(2,1)S(1)} custom-call(s32[33]{0:T(128)S(1)} %pad_add_fusion.refs_0_, f32[3,2]{1,0:T(4,128)S(1)} %copy.17.refs_1_, bf16[3,2,1536,3072]{3,2,1,0:T(8,128)(2,1)} %refs_2_.25, bf16[2,3072,128]{2,1,0:T(8,128)(2,1)} %collective-permute-done.7.refs_3_, bf16[2,3072,128]{2,1,0:T(8,128)(2,1)} %collective-permute-done.9.refs_4_, ...), custom_call_target="tpu_custom_call" | custom-call | flops 141557760 | bytes 196608 | tf_op jit(solution)/shard_map/send_0_0/pallas_call | solution.py:318
  119.9 19.8 %collective-permute-done.4.refs_5_ = bf16[2,3072,128]{2,1,0:T(8,128)(2,1)} collective-permute-done((bf16[2,3072,128]{2,1,0:T(8,128)(2,1)S(1)}, bf16[2,3072,128]{2,1,0:T(8,128)(2,1)}, u32[]{:S(2)}, u32[]{:S(2)}) %collective-permute-start.4) | collective-permute-done | bytes 1572896 | tf_op jit(solution)/shard_map/ppermute | solution.py:524
  143.2 7.3 %send_0_1.1 = bf16[2,1536,128]{2,1,0:T(8,128)(2,1)} custom-call(s32[33]{0:T(128)S(1)} %pad_add_fusion.refs_0_, f32[3,2]{1,0:T(4,128)S(1)} %copy.17.refs_1_, bf16[3,2,1536,3072]{3,2,1,0:T(8,128)(2,1)} %refs_2_.25, bf16[2,3072,128]{2,1,0:T(8,128)(2,1)S(1)} %copy-done.8, bf16[2,3072,128]{2,1,0:T(8,128)(2,1)S(1)} %copy-done.5, ...), custom_call_target="tpu_custom_call" | custom-call | flops 141557760 | bytes 196608 | tf_op jit(solution)/shard_map/send_0_1/pallas_call | solution.py:318
  152.0 7.4 %keep_0_0.1.refs_7_ = bf16[3,2,1536,256]{3,2,1,0:T(8,128)(2,1)} custom-call(s32[33]{0:T(128)S(1)} %pad_add_fusion.refs_0_, f32[3,2]{1,0:T(4,128)S(1)} %copy.17.refs_1_, bf16[3,2,1536,3072]{3,2,1,0:T(8,128)(2,1)} %refs_2_.25, bf16[2,3072,128]{2,1,0:T(8,128)(2,1)} %collective-permute-done.7.refs_3_, bf16[2,3072,128]{2,1,0:T(8,128)(2,1)} %collective-permute-done.9.refs_4_, ...), custom_call_target="tpu_custom_call" | custom-call | flops 141557760 | bytes 196608 | tf_op jit(solution)/shard_map/keep_0_0/pallas_call | solution.py:318
  159.5 13.8 %collective-permute-done.10.refs_4_ = bf16[2,3072,128]{2,1,0:T(8,128)(2,1)S(1)} collective-permute-done((bf16[2,3072,128]{2,1,0:T(8,128)(2,1)}, bf16[2,3072,128]{2,1,0:T(8,128)(2,1)S(1)}, u32[]{:S(2)}, u32[]{:S(2)}) %collective-permute-start.10) | collective-permute-done | bytes 1572896 | tf_op jit(solution)/shard_map/ppermute | solution.py:524
  177.2 6.9 %send_1_0.1 = bf16[2,1536,128]{2,1,0:T(8,128)(2,1)S(1)} custom-call(s32[33]{0:T(128)S(1)} %pad_add_fusion.refs_0_, f32[3,2]{1,0:T(4,128)S(1)} %copy.17.refs_1_, bf16[3,2,1536,3072]{3,2,1,0:T(8,128)(2,1)} %refs_2_.25, bf16[2,3072,128]{2,1,0:T(8,128)(2,1)} %collective-permute-done.8.refs_3_, bf16[2,3072,128]{2,1,0:T(8,128)(2,1)S(1)} %copy-done.11, ...), custom_call_target="tpu_custom_call" | custom-call | flops 141557760 | bytes 196608 | tf_op jit(solution)/shard_map/send_1_0/pallas_call | solution.py:318
  184.1 3.4 %collective-permute-start.11 = (bf16[2,1536,128]{2,1,0:T(8,128)(2,1)S(1)}, bf16[2,1536,128]{2,1,0:T(8,128)(2,1)S(1)}, u32[]{:S(2)}, u32[]{:S(2)}) collective-permute-start(bf16[2,1536,128]{2,1,0:T(8,128)(2,1)S(1)} %send_1_0.1), channel_id=1, source_target_pairs={{0,4},{4,0},{1,5},{5,1},{2,6},{6,2},{3,7},{7,3},{8,12},{12,8},{9,1... | collective-permute-start | bytes 2359304 | tf_op jit(solution)/shard_map/ppermute | solution.py:477
  187.5 8.7 %keep_0_1.1.refs_7_ = bf16[3,2,1536,256]{3,2,1,0:T(8,128)(2,1)} custom-call(s32[33]{0:T(128)S(1)} %pad_add_fusion.refs_0_, f32[3,2]{1,0:T(4,128)S(1)} %copy.17.refs_1_, bf16[3,2,1536,3072]{3,2,1,0:T(8,128)(2,1)} %refs_2_.25, bf16[2,3072,128]{2,1,0:T(8,128)(2,1)S(1)} %copy-done.9, ...), custom_call_target="tpu_custom_call", output_to_operand_aliasing={{}: (7, {})} | custom-call | flops 141557760 | bytes 196608 | tf_op jit(solution)/shard_map/keep_0_1/pallas_call | solution.py:318
  196.2 10.9 %collective-permute-done.15.refs_4_ = bf16[2,3072,128]{2,1,0:T(8,128)(2,1)} collective-permute-done((bf16[2,3072,128]{2,1,0:T(8,128)(2,1)}, bf16[2,3072,128]{2,1,0:T(8,128)(2,1)}, u32[]{:S(2)}, u32[]{:S(2)}) %collective-permute-start.15) | collective-permute-done | bytes 1572896 | tf_op jit(solution)/shard_map/ppermute | solution.py:524
  210.1 7.1 %send_2_0.1 = bf16[2,1536,128]{2,1,0:T(8,128)(2,1)S(1)} custom-call(s32[33]{0:T(128)S(1)} %pad_add_fusion.refs_0_, f32[3,2]{1,0:T(4,128)S(1)} %copy.17.refs_1_, bf16[3,2,1536,3072]{3,2,1,0:T(8,128)(2,1)} %refs_2_.25, bf16[2,3072,128]{2,1,0:T(8,128)(2,1)} %collective-permute-done.5.refs_3_, bf16[2,3072,128]{2,1,0:T(8,128)(2,1)} %collective-permute-done.15.refs_4_, ...), custom_call_target="tpu_custom_call" | custom-call | flops 141557760 | bytes 196608 | tf_op jit(solution)/shard_map/send_2_0/pallas_call | solution.py:318
  220.1 7.4 %keep_1_0.1.refs_7_ = bf16[3,2,1536,256]{3,2,1,0:T(8,128)(2,1)} custom-call(s32[33]{0:T(128)S(1)} %pad_add_fusion.refs_0_, f32[3,2]{1,0:T(4,128)S(1)} %copy.17.refs_1_, bf16[3,2,1536,3072]{3,2,1,0:T(8,128)(2,1)} %refs_2_.25, bf16[2,3072,128]{2,1,0:T(8,128)(2,1)} %collective-permute-done.8.refs_3_, ...), custom_call_target="tpu_custom_call", output_to_operand_aliasing={{}: (7, {})} | custom-call | flops 141557760 | bytes 196608 | tf_op jit(solution)/shard_map/keep_1_0/pallas_call | solution.py:318
  227.5 13.3 %collective-permute-done.16.refs_5_ = bf16[2,3072,128]{2,1,0:T(8,128)(2,1)} collective-permute-done((bf16[2,3072,128]{2,1,0:T(8,128)(2,1)}, bf16[2,3072,128]{2,1,0:T(8,128)(2,1)}, u32[]{:S(2)}, u32[]{:S(2)}) %collective-permute-start.16) | collective-permute-done | bytes 1572896 | tf_op jit(solution)/shard_map/ppermute | solution.py:524
  244.6 7.2 %send_1_1.1 = bf16[2,1536,128]{2,1,0:T(8,128)(2,1)S(1)} custom-call(s32[33]{0:T(128)S(1)} %pad_add_fusion.refs_0_, f32[3,2]{1,0:T(4,128)S(1)} %copy.17.refs_1_, bf16[3,2,1536,3072]{3,2,1,0:T(8,128)(2,1)} %refs_2_.25, bf16[2,3072,128]{2,1,0:T(8,128)(2,1)} %collective-permute-done.13.refs_3_, bf16[2,3072,128]{2,1,0:T(8,128)(2,1)} %collective-permute-done.3.refs_4_, ...), custom_call_target="tpu_custom_call" | custom-call | flops 141557760 | bytes 196608 | tf_op jit(solution)/shard_map/send_1_1/pallas_call | solution.py:318
  254.6 9.6 %keep_2_0.1 = (bf16[3,2,1536,256]{3,2,1,0:T(8,128)(2,1)}, f32[384,128]{1,0:T(8,128)S(1)}, bf16[384,128]{1,0:T(8,128)(2,1)S(1)}, bf16[384,128]{1,0:T(8,128)(2,1)S(1)}, bf16[384,128]{1,0:T(8,128)(2,1)S(1)}) custom-call(s32[33]{0:T(128)S(1)} %pad_add_fusion.refs_0_, f32[3,2]{1,0:T(4,128)S(1)} %copy.17.refs_1_, ...), custom_call_target="tpu_custom_call", output_to_operand_aliasing={{0}: (7, {})} | custom-call | flops 141557760 | bytes 196608 | tf_op jit(solution)/shard_map/keep_2_0/pallas_call | solution.py:318
  264.2 10.2 %collective-permute-done.18.refs_5_ = bf16[2,3072,128]{2,1,0:T(8,128)(2,1)S(1)} collective-permute-done((bf16[2,3072,128]{2,1,0:T(8,128)(2,1)}, bf16[2,3072,128]{2,1,0:T(8,128)(2,1)S(1)}, u32[]{:S(2)}, u32[]{:S(2)}) %collective-permute-start.18) | collective-permute-done | bytes 1572896 | tf_op jit(solution)/shard_map/ppermute | solution.py:524
  274.4 6.8 %send_2_1.1 = bf16[2,1536,128]{2,1,0:T(8,128)(2,1)S(1)} custom-call(s32[33]{0:T(128)S(1)} %pad_add_fusion.refs_0_, f32[3,2]{1,0:T(4,128)S(1)} %copy.17.refs_1_, bf16[3,2,1536,3072]{3,2,1,0:T(8,128)(2,1)} %refs_2_.25, bf16[2,3072,128]{2,1,0:T(8,128)(2,1)S(1)} %collective-permute-done.6.refs_3_, bf16[2,3072,128]{2,1,0:T(8,128)(2,1)S(1)} %collective-permute-done.1.refs_4_, ...), custom_call_target="tpu_custom_call" | custom-call | flops 141557760 | bytes 196608 | tf_op jit(solution)/shard_map/send_2_1/pallas_call | solution.py:318
  284.2 4.1 %collective-permute-start.26 = (bf16[384,128]{1,0:T(8,128)(2,1)S(1)}, bf16[384,128]{1,0:T(8,128)(2,1)S(1)}, u32[]{:S(2)}, u32[]{:S(2)}) collective-permute-start(bf16[384,128]{1,0:T(8,128)(2,1)S(1)} %get-tuple-element.95), channel_id=1, source_target_pairs={{0,8},{8,16},{16,24},{24,0},{1,9},{9,17},{17,25},{25,1},{2,10},{10... | collective-permute-start | bytes 294920 | tf_op jit(solution)/shard_map/ppermute | solution.py:497
  288.6 7.4 %keep_1_1.1.refs_6_.refs_9_ = bf16[3,2,1536,256]{3,2,1,0:T(8,128)(2,1)} custom-call(s32[33]{0:T(128)S(1)} %pad_add_fusion.refs_0_, f32[3,2]{1,0:T(4,128)S(1)} %copy.17.refs_1_, bf16[3,2,1536,3072]{3,2,1,0:T(8,128)(2,1)} %refs_2_.25, bf16[2,3072,128]{2,1,0:T(8,128)(2,1)} %collective-permute-done.13.refs_3_, ...), custom_call_target="tpu_custom_call", output_to_operand_aliasing={{}: (7, {})} | custom-call | flops 141557760 | bytes 196608 | tf_op jit(solution)/shard_map/keep_1_1/pallas_call | solution.py:318
  297.5 8.3 %fold_2_1.1 = (f32[2,1536,128]{2,1,0:T(8,128)S(1)}, f32[1536,128]{1,0:T(8,128)S(1)}) custom-call(s32[33]{0:T(128)S(1)} %pad_add_fusion.refs_0_, f32[3,2]{1,0:T(4,128)S(1)} %copy.17.refs_1_, bf16[3,2,1536,3072]{3,2,1,0:T(8,128)(2,1)} %refs_2_.25, bf16[2,3072,128]{2,1,0:T(8,128)(2,1)S(1)} %collective-permute-done.6.refs_3_, bf16[2,3072,128]{2,1,0:T(8,128)(2,1)} %copy-done.2, ...), custom_call_target="tpu_custom_call" | custom-call | flops 88473600 | bytes 196608 | tf_op jit(solution)/shard_map/fold_2_1/pallas_call | solution.py:318
  308.1 5.4 %keep_2_1.1 = (bf16[3,2,1536,256]{3,2,1,0:T(8,128)(2,1)}, f32[384,128]{1,0:T(8,128)S(1)}, bf16[384,128]{1,0:T(8,128)(2,1)S(1)}, bf16[384,128]{1,0:T(8,128)(2,1)S(1)}, bf16[384,128]{1,0:T(8,128)(2,1)S(1)}) custom-call(s32[33]{0:T(128)S(1)} %pad_add_fusion.refs_0_, f32[3,2]{1,0:T(4,128)S(1)} %copy.17.refs_1_, ...), custom_call_target="tpu_custom_call", output_to_operand_aliasing={{0}: (9, {})} | custom-call | flops 53084160 | bytes 196608 | tf_op jit(solution)/shard_map/keep_2_1/pallas_call | solution.py:318
  (91 shorter events, 65.1 us)
Async XLA Ops:
  2.2 36.3 %collective-permute-start = (bf16[2,3072,128]{2,1,0:T(8,128)(2,1)S(1)}, bf16[2,3072,128]{2,1,0:T(8,128)(2,1)S(1)}, u32[]{:S(2)}, u32[]{:S(2)}) collective-permute-start(bf16[2,3072,128]{2,1,0:T(8,128)(2,1)S(1)} %slice_bitcast_fusion.2), channel_id=1, source_target_pairs={{1,0},{3,2},{2,3},{0,1},{5,4},{7,6},{6,7},{4,5},{9,8},{11,10},{10,... | collective-permute-start | bytes 4718600 | tf_op jit(solution)/shard_map/ppermute | solution.py:524
  4.4 34.9 %collective-permute-start.7 = (bf16[2,3072,128]{2,1,0:T(8,128)(2,1)S(1)}, bf16[2,3072,128]{2,1,0:T(8,128)(2,1)}, u32[]{:S(2)}, u32[]{:S(2)}) collective-permute-start(bf16[2,3072,128]{2,1,0:T(8,128)(2,1)S(1)} %slice_bitcast_fusion.2), channel_id=1, source_target_pairs={{2,1},{1,2},{6,5},{5,6},{10,9},{9,10},{14,13},{13,14},{18,17},{17,... | collective-permute-start | bytes 4718600 | tf_op jit(solution)/shard_map/ppermute | solution.py:524
  8.8 63.5 %collective-permute-start.3 = (bf16[2,3072,128]{2,1,0:T(8,128)(2,1)}, bf16[2,3072,128]{2,1,0:T(8,128)(2,1)}, u32[]{:S(2)}, u32[]{:S(2)}) collective-permute-start(bf16[2,3072,128]{2,1,0:T(8,128)(2,1)} %slice_bitcast_fusion.1), channel_id=1, source_target_pairs={{1,0},{3,2},{2,3},{0,1},{5,4},{7,6},{6,7},{4,5},{9,8},{11,10},{10,... | collective-permute-start | bytes 4718600 | tf_op jit(solution)/shard_map/ppermute | solution.py:524
  38.5 33.8 %collective-permute-start.2 = (bf16[2,3072,128]{2,1,0:T(8,128)(2,1)S(1)}, bf16[2,3072,128]{2,1,0:T(8,128)(2,1)S(1)}, u32[]{:S(2)}, u32[]{:S(2)}) collective-permute-start(bf16[2,3072,128]{2,1,0:T(8,128)(2,1)S(1)} %collective-permute-done.refs_4_), channel_id=1, source_target_pairs={{2,1},{1,2},{6,5},{5,6},{10,9},{9,10},{14,13},{13,14},{18,17},{17,... | collective-permute-start | bytes 4718600 | tf_op jit(solution)/shard_map/ppermute | solution.py:524
  39.2 66.7 %collective-permute-start.9 = (bf16[2,3072,128]{2,1,0:T(8,128)(2,1)}, bf16[2,3072,128]{2,1,0:T(8,128)(2,1)}, u32[]{:S(2)}, u32[]{:S(2)}) collective-permute-start(bf16[2,3072,128]{2,1,0:T(8,128)(2,1)} %collective-permute-done.7.refs_3_), channel_id=1, source_target_pairs={{1,0},{2,3},{5,4},{6,7},{9,8},{10,11},{13,12},{14,15},{17,16},{18,... | collective-permute-start | bytes 4718600 | tf_op jit(solution)/shard_map/ppermute | solution.py:524
  40.5 65.4 %collective-permute-start.8 = (bf16[2,3072,128]{2,1,0:T(8,128)(2,1)}, bf16[2,3072,128]{2,1,0:T(8,128)(2,1)}, u32[]{:S(2)}, u32[]{:S(2)}) collective-permute-start(bf16[2,3072,128]{2,1,0:T(8,128)(2,1)} %slice_bitcast_fusion.1), channel_id=1, source_target_pairs={{2,1},{1,2},{6,5},{5,6},{10,9},{9,10},{14,13},{13,14},{18,17},{17,... | collective-permute-start | bytes 4718600 | tf_op jit(solution)/shard_map/ppermute | solution.py:524
  72.3 44.7 %collective-permute-start.5 = (bf16[2,3072,128]{2,1,0:T(8,128)(2,1)}, bf16[2,3072,128]{2,1,0:T(8,128)(2,1)}, u32[]{:S(2)}, u32[]{:S(2)}) collective-permute-start(bf16[2,3072,128]{2,1,0:T(8,128)(2,1)} %slice_bitcast_fusion), channel_id=1, source_target_pairs={{2,1},{1,2},{6,5},{5,6},{10,9},{9,10},{14,13},{13,14},{18,17},{17,... | collective-permute-start | bytes 4718600 | tf_op jit(solution)/shard_map/ppermute | solution.py:524
  74.2 65.5 %collective-permute-start.4 = (bf16[2,3072,128]{2,1,0:T(8,128)(2,1)S(1)}, bf16[2,3072,128]{2,1,0:T(8,128)(2,1)}, u32[]{:S(2)}, u32[]{:S(2)}) collective-permute-start(bf16[2,3072,128]{2,1,0:T(8,128)(2,1)S(1)} %collective-permute-done.2.refs_3_), channel_id=1, source_target_pairs={{1,0},{2,3},{5,4},{6,7},{9,8},{10,11},{13,12},{14,15},{17,16},{18,... | collective-permute-start | bytes 4718600 | tf_op jit(solution)/shard_map/ppermute | solution.py:524
  75.5 65.5 %collective-permute-start.1 = (bf16[2,3072,128]{2,1,0:T(8,128)(2,1)}, bf16[2,3072,128]{2,1,0:T(8,128)(2,1)S(1)}, u32[]{:S(2)}, u32[]{:S(2)}) collective-permute-start(bf16[2,3072,128]{2,1,0:T(8,128)(2,1)} %slice_bitcast_fusion), channel_id=1, source_target_pairs={{3,2},{0,1},{7,6},{4,5},{11,10},{8,9},{15,14},{12,13},{19,18},{16,... | collective-permute-start | bytes 4718600 | tf_op jit(solution)/shard_map/ppermute | solution.py:524
  106.0 53.5 %collective-permute-start.13 = (bf16[2,3072,128]{2,1,0:T(8,128)(2,1)}, bf16[2,3072,128]{2,1,0:T(8,128)(2,1)}, u32[]{:S(2)}, u32[]{:S(2)}) collective-permute-start(bf16[2,3072,128]{2,1,0:T(8,128)(2,1)} %collective-permute-done.3.refs_4_), channel_id=1, source_target_pairs={{2,1},{1,2},{6,5},{5,6},{10,9},{9,10},{14,13},{13,14},{18,17},{17,... | collective-permute-start | bytes 4718600 | tf_op jit(solution)/shard_map/ppermute | solution.py:524
  107.8 65.5 %collective-permute-start.10 = (bf16[2,3072,128]{2,1,0:T(8,128)(2,1)}, bf16[2,3072,128]{2,1,0:T(8,128)(2,1)S(1)}, u32[]{:S(2)}, u32[]{:S(2)}) collective-permute-start(bf16[2,3072,128]{2,1,0:T(8,128)(2,1)} %collective-permute-done.8.refs_3_), channel_id=1, source_target_pairs={{1,0},{2,3},{5,4},{6,7},{9,8},{10,11},{13,12},{14,15},{17,16},{18,... | collective-permute-start | bytes 4718600 | tf_op jit(solution)/shard_map/ppermute | solution.py:524
  117.0 33.5 %collective-permute-start.14 = (bf16[2,1536,128]{2,1,0:T(8,128)(2,1)S(1)}, bf16[2,1536,128]{2,1,0:T(8,128)(2,1)S(1)}, u32[]{:S(2)}, u32[]{:S(2)}) collective-permute-start(bf16[2,1536,128]{2,1,0:T(8,128)(2,1)S(1)} %send_0_0.1), channel_id=1, source_target_pairs={{0,4},{4,0},{1,5},{5,1},{2,6},{6,2},{3,7},{7,3},{8,12},{12,8},{9,1... | collective-permute-start | bytes 2359304 | tf_op jit(solution)/shard_map/ppermute | solution.py:477
  139.7 67.4 %collective-permute-start.15 = (bf16[2,3072,128]{2,1,0:T(8,128)(2,1)}, bf16[2,3072,128]{2,1,0:T(8,128)(2,1)}, u32[]{:S(2)}, u32[]{:S(2)}) collective-permute-start(bf16[2,3072,128]{2,1,0:T(8,128)(2,1)} %collective-permute-done.5.refs_3_), channel_id=1, source_target_pairs={{1,0},{2,3},{5,4},{6,7},{9,8},{10,11},{13,12},{14,15},{17,16},{18,... | collective-permute-start | bytes 4718600 | tf_op jit(solution)/shard_map/ppermute | solution.py:524
  141.0 66.1 %collective-permute-start.6 = (bf16[2,3072,128]{2,1,0:T(8,128)(2,1)S(1)}, bf16[2,3072,128]{2,1,0:T(8,128)(2,1)S(1)}, u32[]{:S(2)}, u32[]{:S(2)}) collective-permute-start(bf16[2,3072,128]{2,1,0:T(8,128)(2,1)S(1)} %collective-permute-done.1.refs_4_), channel_id=1, source_target_pairs={{2,1},{1,2},{6,5},{5,6},{10,9},{9,10},{14,13},{13,14},{18,17},{17,... | collective-permute-start | bytes 4718600 | tf_op jit(solution)/shard_map/ppermute | solution.py:524
  150.6 36.9 %collective-permute-start.12 = (bf16[2,1536,128]{2,1,0:T(8,128)(2,1)}, bf16[2,1536,128]{2,1,0:T(8,128)(2,1)}, u32[]{:S(2)}, u32[]{:S(2)}) collective-permute-start(bf16[2,1536,128]{2,1,0:T(8,128)(2,1)} %send_0_1.1), channel_id=1, source_target_pairs={{0,4},{4,0},{1,5},{5,1},{2,6},{6,2},{3,7},{7,3},{8,12},{12,8},{9,1... | collective-permute-start | bytes 2359304 | tf_op jit(solution)/shard_map/ppermute | solution.py:477
  174.5 66.3 %collective-permute-start.16 = (bf16[2,3072,128]{2,1,0:T(8,128)(2,1)}, bf16[2,3072,128]{2,1,0:T(8,128)(2,1)}, u32[]{:S(2)}, u32[]{:S(2)}) collective-permute-start(bf16[2,3072,128]{2,1,0:T(8,128)(2,1)} %collective-permute-done.13.refs_3_), channel_id=1, source_target_pairs={{1,0},{2,3},{5,4},{6,7},{9,8},{10,11},{13,12},{14,15},{17,16},{18,... | collective-permute-start | bytes 4718600 | tf_op jit(solution)/shard_map/ppermute | solution.py:524
  184.1 36.0 %collective-permute-start.11 = (bf16[2,1536,128]{2,1,0:T(8,128)(2,1)S(1)}, bf16[2,1536,128]{2,1,0:T(8,128)(2,1)S(1)}, u32[]{:S(2)}, u32[]{:S(2)}) collective-permute-start(bf16[2,1536,128]{2,1,0:T(8,128)(2,1)S(1)} %send_1_0.1), channel_id=1, source_target_pairs={{0,4},{4,0},{1,5},{5,1},{2,6},{6,2},{3,7},{7,3},{8,12},{12,8},{9,1... | collective-permute-start | bytes 2359304 | tf_op jit(solution)/shard_map/ppermute | solution.py:477
  208.5 65.9 %collective-permute-start.18 = (bf16[2,3072,128]{2,1,0:T(8,128)(2,1)}, bf16[2,3072,128]{2,1,0:T(8,128)(2,1)S(1)}, u32[]{:S(2)}, u32[]{:S(2)}) collective-permute-start(bf16[2,3072,128]{2,1,0:T(8,128)(2,1)} %broadcast_select_fusion), channel_id=1, source_target_pairs={{1,0},{2,3},{5,4},{6,7},{9,8},{10,11},{13,12},{14,15},{17,16},{18,... | collective-permute-start | bytes 4718600 | tf_op jit(solution)/shard_map/ppermute | solution.py:524
  217.2 37.3 %collective-permute-start.17 = (bf16[2,1536,128]{2,1,0:T(8,128)(2,1)S(1)}, bf16[2,1536,128]{2,1,0:T(8,128)(2,1)S(1)}, u32[]{:S(2)}, u32[]{:S(2)}) collective-permute-start(bf16[2,1536,128]{2,1,0:T(8,128)(2,1)S(1)} %send_2_0.1), channel_id=1, source_target_pairs={{0,4},{4,0},{1,5},{5,1},{2,6},{6,2},{3,7},{7,3},{8,12},{12,8},{9,1... | collective-permute-start | bytes 2359304 | tf_op jit(solution)/shard_map/ppermute | solution.py:477
  243.3 52.7 %collective-permute-start.22 = (bf16[2,1920,128]{2,1,0:T(8,128)(2,1)S(1)}, bf16[2,1920,128]{2,1,0:T(8,128)(2,1)S(1)}, u32[]{:S(2)}, u32[]{:S(2)}) collective-permute-start(bf16[2,1920,128]{2,1,0:T(8,128)(2,1)S(1)} %slice_select_fusion), channel_id=1, source_target_pairs={{1,0},{2,3},{5,4},{6,7},{9,8},{10,11},{13,12},{14,15},{17,16},{18,... | collective-permute-start | bytes 2949128 | tf_op jit(solution)/shard_map/ppermute | solution.py:524
  251.8 36.5 %collective-permute-start.19 = (bf16[2,1536,128]{2,1,0:T(8,128)(2,1)S(1)}, bf16[2,1536,128]{2,1,0:T(8,128)(2,1)S(1)}, u32[]{:S(2)}, u32[]{:S(2)}) collective-permute-start(bf16[2,1536,128]{2,1,0:T(8,128)(2,1)S(1)} %send_1_1.1), channel_id=1, source_target_pairs={{0,4},{4,0},{1,5},{5,1},{2,6},{6,2},{3,7},{7,3},{8,12},{12,8},{9,1... | collective-permute-start | bytes 2359304 | tf_op jit(solution)/shard_map/ppermute | solution.py:477
  281.2 26.9 %collective-permute-start.21 = (bf16[2,1536,128]{2,1,0:T(8,128)(2,1)S(1)}, bf16[2,1536,128]{2,1,0:T(8,128)(2,1)S(1)}, u32[]{:S(2)}, u32[]{:S(2)}) collective-permute-start(bf16[2,1536,128]{2,1,0:T(8,128)(2,1)S(1)} %send_2_1.1), channel_id=1, source_target_pairs={{0,4},{4,0},{1,5},{5,1},{2,6},{6,2},{3,7},{7,3},{8,12},{12,8},{9,1... | collective-permute-start | bytes 2359304 | tf_op jit(solution)/shard_map/ppermute | solution.py:477
  284.2 32.0 %collective-permute-start.26 = (bf16[384,128]{1,0:T(8,128)(2,1)S(1)}, bf16[384,128]{1,0:T(8,128)(2,1)S(1)}, u32[]{:S(2)}, u32[]{:S(2)}) collective-permute-start(bf16[384,128]{1,0:T(8,128)(2,1)S(1)} %get-tuple-element.95), channel_id=1, source_target_pairs={{0,8},{8,16},{16,24},{24,0},{1,9},{9,17},{17,25},{25,1},{2,10},{10... | collective-permute-start | bytes 294920 | tf_op jit(solution)/shard_map/ppermute | solution.py:497
  288.3 28.3 %collective-permute-start.27 = (bf16[384,128]{1,0:T(8,128)(2,1)S(1)}, bf16[384,128]{1,0:T(8,128)(2,1)S(1)}, u32[]{:S(2)}, u32[]{:S(2)}) collective-permute-start(bf16[384,128]{1,0:T(8,128)(2,1)S(1)} %get-tuple-element.96), channel_id=1, source_target_pairs={{0,16},{8,24},{16,0},{24,8},{1,17},{9,25},{17,1},{25,9},{2,18},{10... | collective-permute-start | bytes 294920 | tf_op jit(solution)/shard_map/ppermute | solution.py:497
  (20 other events, 496.0 us)
